TPU v7x, 32 devices: a whole 2x2x4 slice. The times are simulated.
32 devices in a mesh: job: 2 (over y), blk: 4 (over z), cell: 2 (over x), col: 2 (over core).
Axes of the slice: x: 2, y: 2, z: 4, core: 2. Of those that a mesh axis runs over, the one named last changes fastest.
Arguments:
- p_blocks: bfloat16 [64, 4, 2, 128, 128], P(('job', 'blk', 'cell')), parts along dimension 0, may hold values from -0.1875 to 0.1875
- p_cols: int32 [64, 4, 2], P(('job', 'blk', 'cell')), parts along dimension 0, may hold values from 0 to 7
- l_blocks: bfloat16 [64, 4, 2, 128, 128], P(('job', 'blk', 'cell')), parts along dimension 0, may hold values from -0.1875 to 0.1875
- l_cols: int32 [64, 4, 2], P(('job', 'blk', 'cell')), parts along dimension 0, may hold values from 0 to 7
- charges: bfloat16 [24, 2, 8192], P('col', None, ('job', 'blk', 'cell')), parts along dimension 2, may hold values from -6 to 6
- currents: bfloat16 [24, 2, 8192], P('col', None, ('job', 'blk', 'cell')), parts along dimension 2, may hold values from -6 to 6
- omegas: float32 [24], P('col'), may hold values from 0.5 to 4
- resist: float32 [8192], P(('job', 'blk', 'cell')), parts along dimension 0, may hold values from 0.05 to 2
- branch_ends: int32 [2, 8192], P(None, ('job', 'blk', 'cell')), parts along dimension 1, may hold values from 0 to 1023
Outputs:
- cell_rows: float32 [24, 2, 8192], P('col', None, ('job', 'blk', 'cell')), parts along dimension 2
- panel_rows: float32 [24, 2, 8192], P('col', None, ('job', 'blk', 'cell')), parts along dimension 2
There are 2 independent parts, one for each index of `job`. A program takes and returns all parts, laid end to end along the dimension named above; an argument that names none is the same for every part. Nothing has to cross between parts.
Inputs may be any that keep to these rules, and one draw needn't show every extreme that they name: `p_cols`: block columns are numbered within the region of 8 blocks that the slot's region index names; repeats may occur. `l_cols`: as for p_cols. `branch_ends`: panel numbers within the cell's own region of 1024 panels; a cell may leave and enter the same panel.
All inputs are finite; a program needn't handle non-finite values.
Results may differ from a plain program's by a relative error of at most 0.0059.
Values may be sent and summed in bfloat16 or wider, within the bound.
No kernel may reach another device: no remote copies, remote signals or barrier semaphores. Data moves between devices by JAX's collectives and lax.ppermute only.
A program may use at most 64 MiB of HBM per device.

v0:
```python
import jax
import jax.numpy as jnp
from jax import lax
from jax.sharding import PartitionSpec as P


def passed_along(shard, axis, by):
    length = lax.axis_size(axis)
    return lax.ppermute(shard, axis, [(i, (i + by) % length) for i in range(length)])


def per_device(p_blocks, p_cols, l_blocks, l_cols, charges, currents, omegas, resist, branch_ends):
    freq_count = charges.shape[0]
    share = charges.shape[2]
    block_size = p_blocks.shape[-1]
    row_blocks = p_blocks.shape[0]
    col_rows = 2 * freq_count
    stacked = jnp.stack([charges.reshape(col_rows, share), currents.reshape(col_rows, share)])
    region_vec = lax.all_gather(stacked, "cell", axis=2, tiled=True)
    reg_width = region_vec.shape[2]
    reg_blocks = reg_width // block_size
    blk_count = lax.axis_size("blk")
    blk_place = lax.axis_index("blk")

    def accumulate(totals, whole, source):
        p_slab = lax.dynamic_index_in_dim(p_blocks, source, 1, keepdims=False)
        p_index = lax.dynamic_index_in_dim(p_cols, source, 1, keepdims=False)
        l_slab = lax.dynamic_index_in_dim(l_blocks, source, 1, keepdims=False)
        l_index = lax.dynamic_index_in_dim(l_cols, source, 1, keepdims=False)
        vectors = whole.reshape(2, col_rows, reg_blocks, block_size)
        q_picked = vectors[0][:, p_index]
        i_picked = vectors[1][:, l_index]
        phi_add = jnp.einsum("rkab,frkb->fra", p_slab, q_picked, preferred_element_type=jnp.float32)
        flux_add = jnp.einsum(
            "rkab,frkb->fra", l_slab, i_picked, preferred_element_type=jnp.float32
        )
        return (totals[0] + phi_add, totals[1] + flux_add)

    zeros_acc = jnp.zeros((col_rows, row_blocks, block_size), jnp.float32)
    totals = accumulate((zeros_acc, zeros_acc), region_vec, blk_place)

    def forward(offset, carry):
        acc, held = carry
        held = passed_along(held, "blk", 1)
        acc = accumulate(acc, held, (blk_place - offset - 1) % blk_count)
        return (acc, held)

    totals, held_last = lax.fori_loop(0, blk_count - 1, forward, (totals, region_vec))
    potential = totals[0].reshape(col_rows, share).astype(jnp.bfloat16)
    flux = totals[1].reshape(freq_count, 2, share)
    phi_region = lax.all_gather(potential, "cell", axis=1, tiled=True)
    drop = phi_region[:, branch_ends[0]].astype(jnp.float32) - phi_region[:, branch_ends[1]].astype(
        jnp.float32
    )
    drop = drop.reshape(freq_count, 2, share)
    current_f = currents.astype(jnp.float32)
    scale = omegas[:, None]
    cell_re = resist * current_f[:, 0] - scale * flux[:, 1] + drop[:, 0]
    cell_im = resist * current_f[:, 1] + scale * flux[:, 0] + drop[:, 1]
    cell_rows = jnp.stack([cell_re, cell_im], axis=1)
    panel_ids = jnp.arange(reg_width, dtype=jnp.int32)
    incidence = (branch_ends[0][:, None] == panel_ids[None, :]).astype(jnp.bfloat16) - (
        branch_ends[1][:, None] == panel_ids[None, :]
    ).astype(jnp.bfloat16)
    partial_terms = jnp.dot(
        currents.reshape(col_rows, share), incidence, preferred_element_type=jnp.float32
    )
    outflow = lax.psum_scatter(
        partial_terms.astype(jnp.bfloat16), "cell", scatter_dimension=1, tiled=True
    ).astype(jnp.float32)
    outflow = outflow.reshape(freq_count, 2, share)
    charge_f = charges.astype(jnp.float32)
    panel_re = outflow[:, 0] - scale * charge_f[:, 1]
    panel_im = outflow[:, 1] + scale * charge_f[:, 0]
    panel_rows = jnp.stack([panel_re, panel_im], axis=1)
    return (cell_rows, panel_rows)


def solution(mesh):
    placed = (
        P(("job", "blk", "cell"), None, None, None, None),
        P(("job", "blk", "cell"), None, None),
        P(("job", "blk", "cell"), None, None, None, None),
        P(("job", "blk", "cell"), None, None),
        P("col", None, ("job", "blk", "cell")),
        P("col", None, ("job", "blk", "cell")),
        P("col"),
        P(("job", "blk", "cell")),
        P(None, ("job", "blk", "cell")),
    )
    return jax.shard_map(
        per_device,
        mesh=mesh,
        in_specs=placed,
        out_specs=(P("col", None, ("job", "blk", "cell")), P("col", None, ("job", "blk", "cell"))),
        check_vma=False,
    )
```

profile of v0, /device:TPU:0, one launch (start us, length us, event | category | flops | bytes accessed | tf_op | source)
XLA Modules:
  0.0 61.0 jit_solution(2294230764357474805)
XLA Ops:
  7.3 0.8 %fusion.26 = (s32[1,512]{1,0:T(1,128)S(1)}, s32[1,512]{1,0:T(1,128)S(1)}) fusion(s32[2,512]{1,0:T(2,128)} %param.19), kind=kLoop, calls=%fused_computation.67 | loop fusion | bytes 8192 | tf_op jit(solution)/shard_map/slice | solution.py:52
  8.0 0.8 %reshape.253 = bf16[24,512]{1,0:T(8,128)(2,1)S(1)} reshape(bf16[12,2,512]{2,1,0:T(2,128)(2,1)} %param.16) | data formatting | bytes 49152 | tf_op jit(solution)/shard_map/reshape | solution.py:66
  8.8 1.3 %fusion.10 = bf16[24,1024]{1,0:T(8,128)(2,1)} fusion(bf16[24,512]{1,0:T(8,128)(2,1)S(1)} %reshape.253, s32[512]{0:T(512)S(1)} %bitcast.138, s32[512]{0:T(512)S(1)} %bitcast.137), kind=kOutput, calls=%fused_computation.27 | convolution fusion | flops 29384704 | bytes 77824 | tf_op jit(solution)/shard_map/dot_general | solution.py:65
  10.9 5.7 %all_gather.6 = bf16[2,24,1024]{2,1,0:T(8,128)(2,1)S(1)} all-gather(bf16[2,24,512]{2,1,0:T(8,128)(2,1)S(1)} %pad_maximum_fusion), channel_id=1, replica_groups=mesh['job'=2,'blk'=4,'cell'=2,'col'=2] {'cell'}, dimensions={2}, use_global_device_ids=true | all-gather | bytes 147456 | tf_op jit(solution)/shard_map/all_gather | solution.py:19
  16.9 0.6 gather_fusion.3
  17.6 0.6 gather_fusion.2
  18.4 24.6 %while.19 = (s32[]{:T(128)}, f32[24,4,128]{2,0,1:T(8,128)S(1)}, f32[24,4,128]{2,0,1:T(8,128)S(1)}, bf16[2,24,1024]{2,1,0:T(8,128)(2,1)S(1)}, s32[]{:T(128)}, /*i...) while((s32[]{:T(128)}, f32[24,4,128]{2,0,1:T(8,128)S(1)}, ...), condition=%wide.region_1.2_spmd, body=%wide.region_0.1_spmd.sunk | while | flops 12609602 | bytes 2204512 | solution.py:48
  18.4 2.2 %collective-permute-start = (bf16[2,24,1024]{2,1,0:T(8,128)(2,1)S(1)}, bf16[2,24,1024]{2,1,0:T(8,128)(2,1)S(1)}, u32[]{:S(2)}, u32[]{:S(2)}) collective-permute-start(bf16[2,24,1024]{2,1,0:T(8,128)(2,1)S(1)} %get-tuple-element.370), channel_id=1, source_target_pairs={{0,4},{4,8},{8,12},{12,0},{1,5},{5,9},{9,13},{13,1},{2,6},{6,10},{... | collective-permute-start | bytes 294920 | tf_op jit(solution)/shard_map/while/body/eval_jaxpr/ppermute | solution.py:9
  20.9 4.2 %collective-permute-done = bf16[2,24,1024]{2,1,0:T(8,128)(2,1)S(1)} collective-permute-done((bf16[2,24,1024]{2,1,0:T(8,128)(2,1)S(1)}, bf16[2,24,1024]{2,1,0:T(8,128)(2,1)S(1)}, u32[]{:S(2)}, u32[]{:S(2)}) %collective-permute-start) | collective-permute-done | bytes 98336 | tf_op jit(solution)/shard_map/while/body/eval_jaxpr/ppermute | solution.py:9
  25.2 0.6 gather_fusion.1
  25.8 0.6 gather_fusion
  27.3 6.0 %collective-permute-done = bf16[2,24,1024]{2,1,0:T(8,128)(2,1)S(1)} collective-permute-done((bf16[2,24,1024]{2,1,0:T(8,128)(2,1)S(1)}, bf16[2,24,1024]{2,1,0:T(8,128)(2,1)S(1)}, u32[]{:S(2)}, u32[]{:S(2)}) %collective-permute-start) | collective-permute-done | bytes 98336 | tf_op jit(solution)/shard_map/while/body/eval_jaxpr/ppermute | solution.py:9
  33.4 0.6 gather_fusion.1
  33.9 0.6 gather_fusion
  35.4 6.0 %collective-permute-done = bf16[2,24,1024]{2,1,0:T(8,128)(2,1)S(1)} collective-permute-done((bf16[2,24,1024]{2,1,0:T(8,128)(2,1)S(1)}, bf16[2,24,1024]{2,1,0:T(8,128)(2,1)S(1)}, u32[]{:S(2)}, u32[]{:S(2)}) %collective-permute-start) | collective-permute-done | bytes 98336 | tf_op jit(solution)/shard_map/while/body/eval_jaxpr/ppermute | solution.py:9
  41.5 0.6 gather_fusion.1
  42.0 0.6 gather_fusion
  43.2 5.6 %all_gather.7 = bf16[24,1024]{0,1:T(8,128)(2,1)S(1)} all-gather(bf16[24,512]{0,1:T(8,128)(2,1)S(1)} %bitcast.130), channel_id=1, replica_groups=mesh['job'=2,'blk'=4,'cell'=2,'col'=2] {'cell'}, dimensions={1}, use_global_device_ids=true | all-gather | bytes 73728 | tf_op jit(solution)/shard_map/all_gather | solution.py:51
  48.8 1.3 %gather_fusion.4 = bf16[512,24]{1,0:T(8,128)(2,1)S(1)} fusion(bf16[24,1024]{0,1:T(8,128)(2,1)S(1)} %all_gather.7, s32[1024]{0:T(1024)S(1)} %pad_clamp_fusion.3), kind=kCustom, calls=%fused_computation.4 | custom fusion | bytes 51200 | tf_op jit(solution)/shard_map/gather | solution.py:52
  50.2 1.3 %gather_fusion.5 = bf16[512,24]{1,0:T(8,128)(2,1)S(1)} fusion(bf16[24,1024]{0,1:T(8,128)(2,1)S(1)} %all_gather.7, s32[1024]{0:T(1024)S(1)} %pad_clamp_fusion.2), kind=kCustom, calls=%fused_computation.5 | custom fusion | bytes 51200 | tf_op jit(solution)/shard_map/gather | solution.py:52
  51.9 0.8 %reshape.257 = f32[12,2,512]{2,1,0:T(2,128)S(1)} reshape(bf16[24,512]{1,0:T(8,128)(2,1)} %reduce-scatter.2.cloned.1.call-done) | data formatting | bytes 73728 | tf_op jit(solution)/shard_map/reshape | solution.py:71
  52.7 0.2 fusion.21
  52.9 0.7 %pad_maximum_fusion.2 = f32[12,2,512]{2,1,0:T(2,128)} fusion(f32[12,1,512]{2,1,0:T(1,128)S(1)} %get-tuple-element.279, f32[12,1,512]{2,1,0:T(1,128)S(1)} %get-tuple-element.278), kind=kLoop, calls=%fused_computation.42 | loop fusion | flops 12288 | bytes 98304 | tf_op jit(solution)/shard_map/stack | solution.py:75
  53.5 0.7 %pad_maximum_fusion.1 = f32[12,2,512]{2,1,0:T(2,128)} fusion(f32[12,1,512]{2,1,0:T(1,128)S(1)} %get-tuple-element.286, f32[12,1,512]{2,1,0:T(1,128)S(1)} %get-tuple-element.287), kind=kLoop, calls=%fused_computation.41 | loop fusion | flops 12288 | bytes 98304 | tf_op jit(solution)/shard_map/stack | solution.py:60
  (103 shorter events, 4.5 us)
Async XLA Ops:
  7.2 3.3 %copy-start.6 = (s32[2,512]{1,0:T(2,128)S(1)}, s32[2,512]{1,0:T(2,128)}, u32[]{:S(2)}) copy-start(s32[2,512]{1,0:T(2,128)} %param.19) | copy-start | bytes 12292
  7.2 2.9 %copy-start.2 = (bf16[12,2,512]{2,1,0:T(2,128)(2,1)S(1)}, bf16[12,2,512]{2,1,0:T(2,128)(2,1)}, u32[]{:S(2)}) copy-start(bf16[12,2,512]{2,1,0:T(2,128)(2,1)} %param.16) | copy-start | bytes 73732
  7.2 3.0 %copy-start.4 = (s32[4,4,2]{1,2,0:T(2,128)S(1)}, s32[4,4,2]{1,2,0:T(2,128)}, u32[]{:S(2)}) copy-start(s32[4,4,2]{1,2,0:T(2,128)} %param.12) | copy-start | bytes 388
  7.2 3.1 %copy-start.5 = (s32[4,4,2]{1,2,0:T(2,128)S(1)}, s32[4,4,2]{1,2,0:T(2,128)}, u32[]{:S(2)}) copy-start(s32[4,4,2]{1,2,0:T(2,128)} %param.14) | copy-start | bytes 388
  7.2 44.7 %reduce-scatter.2.cloned.1.call-start = ((), (), s32[]{:S(2)}) async-start(), calls=%async_computation.1 | async-start | bytes 73728 | tf_op jit(solution)/shard_map/reduce_scatter | solution.py:68
  8.0 2.9 %copy-start.3 = (bf16[12,2,512]{2,1,0:T(2,128)(2,1)S(1)}, bf16[12,2,512]{2,1,0:T(2,128)(2,1)}, u32[]{:S(2)}) copy-start(bf16[12,2,512]{2,1,0:T(2,128)(2,1)} %param.15) | copy-start | bytes 73732
  8.8 8.7 %copy-start.1 = (bf16[4,4,2,128,128]{4,3,2,1,0:T(8,128)(2,1)S(1)}, bf16[4,4,2,128,128]{4,3,2,1,0:T(8,128)(2,1)}, u32[]{:S(2)}) copy-start(bf16[4,4,2,128,128]{4,3,2,1,0:T(8,128)(2,1)} %param.13) | copy-start | bytes 3145732
  10.1 8.1 %copy-start = (bf16[4,4,2,128,128]{4,3,2,1,0:T(8,128)(2,1)S(1)}, bf16[4,4,2,128,128]{4,3,2,1,0:T(8,128)(2,1)}, u32[]{:S(2)}) copy-start(bf16[4,4,2,128,128]{4,3,2,1,0:T(8,128)(2,1)} %param.11) | copy-start | bytes 3145732
  18.4 6.8 %collective-permute-start = (bf16[2,24,1024]{2,1,0:T(8,128)(2,1)S(1)}, bf16[2,24,1024]{2,1,0:T(8,128)(2,1)S(1)}, u32[]{:S(2)}, u32[]{:S(2)}) collective-permute-start(bf16[2,24,1024]{2,1,0:T(8,128)(2,1)S(1)} %get-tuple-element.370), channel_id=1, source_target_pairs={{0,4},{4,8},{8,12},{12,0},{1,5},{5,9},{9,13},{13,1},{2,6},{6,10},{... | collective-permute-start | bytes 294920 | tf_op jit(solution)/shard_map/while/body/eval_jaxpr/ppermute | solution.py:9
  26.8 6.5 %collective-permute-start = (bf16[2,24,1024]{2,1,0:T(8,128)(2,1)S(1)}, bf16[2,24,1024]{2,1,0:T(8,128)(2,1)S(1)}, u32[]{:S(2)}, u32[]{:S(2)}) collective-permute-start(bf16[2,24,1024]{2,1,0:T(8,128)(2,1)S(1)} %get-tuple-element.370), channel_id=1, source_target_pairs={{0,4},{4,8},{8,12},{12,0},{1,5},{5,9},{9,13},{13,1},{2,6},{6,10},{... | collective-permute-start | bytes 294920 | tf_op jit(solution)/shard_map/while/body/eval_jaxpr/ppermute | solution.py:9
  34.9 6.5 %collective-permute-start = (bf16[2,24,1024]{2,1,0:T(8,128)(2,1)S(1)}, bf16[2,24,1024]{2,1,0:T(8,128)(2,1)S(1)}, u32[]{:S(2)}, u32[]{:S(2)}) collective-permute-start(bf16[2,24,1024]{2,1,0:T(8,128)(2,1)S(1)} %get-tuple-element.370), channel_id=1, source_target_pairs={{0,4},{4,8},{8,12},{12,0},{1,5},{5,9},{9,13},{13,1},{2,6},{6,10},{... | collective-permute-start | bytes 294920 | tf_op jit(solution)/shard_map/while/body/eval_jaxpr/ppermute | solution.py:9
  43.2 9.5 %copy-start.7 = (f32[512]{0:T(512)S(1)}, f32[512]{0:T(512)}, u32[]{:S(2)}) copy-start(f32[512]{0:T(512)} %param.18) | copy-start | bytes 6148
  43.2 9.5 %copy-start.8 = (f32[12]{0:T(128)S(1)}, f32[12]{0:T(128)}, u32[]{:S(2)}) copy-start(f32[12]{0:T(128)} %param.17) | copy-start | bytes 148
Sparse Core Ops, SparseCore 0:
  10.8 12.5 reduce-scatter.1
where the time goes:
time: 61.4 us; the launch traced here: 61 us
  waiting for transfers between devices  16.2 us (26%)
  between operations  14.3 us (23%)
  local copies, waits for them, and re-layouts  12.1 us (20%)
  blocking collectives  11.3 us (18%)
  matrix products  2.73 us (4%)
  starting transfers between devices  2.31 us (4%)
  other arithmetic  1.74 us (3%)
    ppermute x3, waiting for transfers between devices, passed_along(): lax.ppermute(shard, axis, [(i, (i + by) % length) for i in range(length)])  16.2 us
    all_gather x1, blocking collectives, per_device(): region_vec = lax.all_gather(stacked, 'cell', axis=2, tiled=True)  5.66 us
    all_gather x1, blocking collectives, per_device(): phi_region = lax.all_gather(potential, 'cell', axis=1, tiled=True)  5.64 us
    gather x4, local copies, waits for them, and re-layouts, accumulate(): q_picked = vectors[0][:, p_index]  2.28 us
    ppermute x3, starting transfers between devices, passed_along(): lax.ppermute(shard, axis, [(i, (i + by) % length) for i in range(length)])  2.27 us
    gather x4, local copies, waits for them, and re-layouts, accumulate(): i_picked = vectors[1][:, l_index]  2.26 us
    gather x1, local copies, waits for them, and re-layouts, per_device(): phi_region[:, branch_ends[0]].astype(jnp.float32)  1.34 us
    gather x1, local copies, waits for them, and re-layouts, per_device(): phi_region[:, branch_ends[1]].astype(jnp.float32)  1.34 us
  transfers between devices with their start and end apart: 4, of which 3 were waited for; matrix products, arithmetic and copies ran while one was open for 19% of the time, Pallas kernels for 0%

commit v1 on v0

v1 whole, which is shorter than its diff:
```python
import functools

import jax
import jax.numpy as jnp
from jax import lax
from jax.experimental import pallas as pl
from jax.experimental.pallas import tpu as pltpu
from jax.sharding import PartitionSpec as P

NT = (((1,), (1,)), ((), ()))
NN = (((1,), (0,)), ((), ()))
VMEM = pl.BlockSpec(memory_space=pltpu.VMEM)
SMEM = pl.BlockSpec(memory_space=pltpu.SMEM)


def halves(count):
    steps = []
    while count > 1:
        count //= 2
        steps.append(count)
    return steps


def swapped(array, axis, distance):
    return lax.ppermute(array, axis, [(i, i ^ distance) for i in range(lax.axis_size(axis))])


def block_kernel(offsets, cols_ref, place_ref, held_ref, slab_ref, out_ref):
    row_blocks, _, slots = slab_ref.shape[:3]
    own_region, own_cell = place_ref[0], place_ref[1]
    for row in range(row_blocks):
        total = jnp.zeros(out_ref.shape[1:], jnp.float32)
        for piece, offset in enumerate(offsets):
            region = own_region ^ offset
            for slot in range(slots):
                column = cols_ref[row, region, slot]
                side = lax.div(column, row_blocks) ^ own_cell
                block = held_ref[side, piece, lax.rem(column, row_blocks)]
                total += lax.dot_general(
                    block, slab_ref[row, region, slot], NT, preferred_element_type=jnp.float32
                )
        out_ref[row] = total.astype(out_ref.dtype)


def block_product(slab, cols, place, held, offsets, dtype):
    row_blocks, block_size = slab.shape[0], slab.shape[-1]
    rows = held.shape[-2]
    return pl.pallas_call(
        functools.partial(block_kernel, offsets),
        out_shape=jax.ShapeDtypeStruct((row_blocks, rows, block_size), dtype),
        in_specs=[SMEM, SMEM, VMEM, VMEM],
        out_specs=VMEM,
        compiler_params=pltpu.CompilerParams(vmem_limit_bytes=32 * 1024 * 1024),
        cost_estimate=pl.CostEstimate(
            flops=2 * rows * slab.size, bytes_accessed=2 * slab.size + 2 * held.size, transcendentals=0
        ),
    )(cols, place, held, slab)


def incidence_kernel(ends_ref, current_ref, matrix_ref, out_ref):
    blocks, _, block_size = out_ref.shape
    cells = ends_ref.shape[1]
    leaves, enters = ends_ref[0:1, :], ends_ref[1:2, :]
    current = current_ref[...]
    for block in range(blocks):
        panel = lax.broadcasted_iota(jnp.int32, (block_size, cells), 0) + block * block_size
        entry = (leaves == panel).astype(jnp.float32) - (enters == panel).astype(jnp.float32)
        entry = entry.astype(jnp.bfloat16)
        matrix_ref[block] = entry
        out_ref[block] = lax.dot_general(current, entry, NT, preferred_element_type=jnp.float32)


def incidence(ends, current, panels, block_size):
    cells = ends.shape[1]
    blocks = panels // block_size
    return pl.pallas_call(
        incidence_kernel,
        out_shape=(
            jax.ShapeDtypeStruct((blocks, block_size, cells), jnp.bfloat16),
            jax.ShapeDtypeStruct((blocks, current.shape[0], block_size), jnp.float32),
        ),
        in_specs=[VMEM, VMEM],
        out_specs=(VMEM, VMEM),
        compiler_params=pltpu.CompilerParams(vmem_limit_bytes=32 * 1024 * 1024),
        cost_estimate=pl.CostEstimate(
            flops=4 * panels * cells * current.shape[0], bytes_accessed=2 * panels * cells, transcendentals=0
        ),
    )(ends, current)


def drop_kernel(potential_ref, matrix_ref, base_ref, out_ref):
    total = base_ref[...]
    for block in range(matrix_ref.shape[0]):
        total += lax.dot_general(
            potential_ref[block], matrix_ref[block], NN, preferred_element_type=jnp.float32
        )
    out_ref[...] = total


def with_drop(potential, matrix, base):
    return pl.pallas_call(
        drop_kernel,
        out_shape=jax.ShapeDtypeStruct(base.shape, jnp.float32),
        in_specs=[VMEM, VMEM, VMEM],
        out_specs=VMEM,
        compiler_params=pltpu.CompilerParams(vmem_limit_bytes=32 * 1024 * 1024),
        cost_estimate=pl.CostEstimate(
            flops=2 * base.shape[0] * matrix.size, bytes_accessed=2 * matrix.size, transcendentals=0
        ),
    )(potential, matrix, base)


def turned(array):
    return jnp.stack([-array[:, 1], array[:, 0]], axis=1)


def per_device(p_blocks, p_cols, l_blocks, l_cols, charges, currents, omegas, resist, branch_ends):
    freq_count, _, share = charges.shape
    block_size = p_blocks.shape[-1]
    row_blocks = p_blocks.shape[0]
    rows = 2 * freq_count
    regions, cells = lax.axis_size("blk"), lax.axis_size("cell")
    region, cell = lax.axis_index("blk"), lax.axis_index("cell")
    place = jnp.stack([region, cell]).astype(jnp.int32)

    def blocked(array):
        return array.reshape(rows, row_blocks, block_size).transpose(1, 0, 2)

    def flat(array):
        return array.transpose(1, 0, 2).reshape(rows, share)

    held = jnp.stack([blocked(charges), blocked(turned(currents))])[:, None]
    offsets = [0]
    for step in halves(regions):
        held = jnp.concatenate([held, swapped(held, "blk", step)], axis=1)
        offsets = offsets + [o ^ step for o in offsets]

    local = ((branch_ends // share) ^ cell) * share + branch_ends % share
    matrix, outflow = incidence(local, currents.reshape(rows, share), cells * share, block_size)
    outflow = outflow.reshape(cells, row_blocks, rows, block_size)

    charge_all, current_all = held[0][None], held[1][None]
    for step in reversed(halves(cells)):
        charge_all = jnp.concatenate([charge_all, swapped(charge_all, "cell", step)], axis=0)
    potential = block_product(p_blocks, p_cols, place, charge_all, offsets, jnp.bfloat16)
    for step in reversed(halves(cells)):
        away = [o for o in range(cells) if o & step and not o & (step - 1)]
        kept = [o - step for o in away]
        sums = jnp.stack([outflow[o] for o in away]).astype(jnp.bfloat16)
        flat_current = current_all.reshape(-1, rows, block_size)
        message = jnp.concatenate([flat_current, sums.reshape(-1, rows, block_size)], axis=0)
        message = swapped(message, "cell", step)
        got = message[: flat_current.shape[0]].reshape(current_all.shape)
        more = message[flat_current.shape[0] :].reshape(sums.shape).astype(jnp.float32)
        current_all = jnp.concatenate([current_all, got], axis=0)
        for position, o in enumerate(kept):
            outflow = outflow.at[o].add(more[position])
    potential_all = potential[None]
    for step in reversed(halves(cells)):
        potential_all = jnp.concatenate([potential_all, swapped(potential_all, "cell", step)], axis=0)
    flux_turned = block_product(l_blocks, l_cols, place, current_all, offsets, jnp.float32)

    scale = jnp.repeat(omegas, 2)[:, None]
    base = resist * currents.reshape(rows, share).astype(jnp.float32) + scale * flat(flux_turned)
    cell_rows = with_drop(potential_all.reshape(-1, rows, block_size), matrix, base)
    panel_rows = flat(outflow[0]) + scale * turned(charges).reshape(rows, share).astype(jnp.float32)
    return (cell_rows.reshape(freq_count, 2, share), panel_rows.reshape(freq_count, 2, share))


def solution(mesh):
    placed = (
        P(("job", "blk", "cell"), None, None, None, None),
        P(("job", "blk", "cell"), None, None),
        P(("job", "blk", "cell"), None, None, None, None),
        P(("job", "blk", "cell"), None, None),
        P("col", None, ("job", "blk", "cell")),
        P("col", None, ("job", "blk", "cell")),
        P("col"),
        P(("job", "blk", "cell")),
        P(None, ("job", "blk", "cell")),
    )
    return jax.shard_map(
        per_device,
        mesh=mesh,
        in_specs=placed,
        out_specs=(P("col", None, ("job", "blk", "cell")), P("col", None, ("job", "blk", "cell"))),
        check_vma=False,
    )
```

time: 61.4 us -> 24.9 us (0.41)
  between operations: 14.3 us -> 0.84 us
  blocking collectives: 11.3 us -> 0 us
  waiting for transfers between devices: 16.2 us -> 6.4 us
  local copies, waits for them, and re-layouts: 12.1 us -> 3.32 us
  starting transfers between devices: 2.31 us -> 9.47 us
  Pallas kernels: 0 us -> 3.49 us
  matrix products: 2.73 us -> 0 us
    all_gather x2 -> x0, blocking collectives: 11.3 us -> none  [the longest x1 5.66 us: per_device(): region_vec = lax.all_gather(stacked, 'cell', axis=2, tiled=True)]
    ppermute x3 -> x5, waiting for transfers between devices: 16.2 us -> 6.4 us  [swapped(): lax.ppermute(array, axis, [(i, i ^ distance) for i in range(lax.axis_size...]
    gather x10 -> x0, local copies, waits for them, and re-layouts: 7.23 us -> none  [the longest x4 2.28 us: accumulate(): q_picked = vectors[0][:, p_index]]
    ppermute x3 -> x5, starting transfers between devices: 2.27 us -> 9.47 us  [swapped(): lax.ppermute(array, axis, [(i, i ^ distance) for i in range(lax.axis_size...]
    pallas_call x0 -> x4, Pallas kernels: none -> 3.49 us  [the longest x2 2.63 us: block_product(): pl.pallas_call(functools.partial(block_kernel, offsets), out_shape=jax.Sh...]
    dot_general x9 -> x0, matrix products: 2.73 us -> none  [the longest x1 1.27 us: per_device(): jnp.dot(currents.reshape(col_rows, share), incidence, preferred_element_t...]
    unnamed x21 -> x20, local copies, waits for them, and re-layouts: 0.07 us -> 1.59 us
    select_n x16 -> x0, local copies, waits for them, and re-layouts: 1.43 us -> none  [the longest x8 0.72 us: accumulate(): i_picked = vectors[1][:, l_index]]
  transfers between devices with their start and end apart: 4 -> 5, of which waited for: 3 -> 4; matrix products, arithmetic and copies ran while one was open for 19% -> 3% of each run, Pallas kernels for 0% -> 13%
where the time goes in v1:
time: 24.9 us; the launch traced here: 24.7 us
  starting transfers between devices  9.47 us (38%)
  waiting for transfers between devices  6.4 us (26%)
  Pallas kernels  3.49 us (14%)
  local copies, waits for them, and re-layouts  3.32 us (13%)
  other arithmetic  1.18 us (5%)
  between operations  0.84 us (3%)
    ppermute x5, starting transfers between devices, swapped(): lax.ppermute(array, axis, [(i, i ^ distance) for i in range(lax.axis_size...  9.47 us
    ppermute x5, waiting for transfers between devices, swapped(): lax.ppermute(array, axis, [(i, i ^ distance) for i in range(lax.axis_size...  6.4 us
    pallas_call x2, Pallas kernels, block_product(): pl.pallas_call(functools.partial(block_kernel, offsets), out_shape=jax.Sh...  2.63 us
    unnamed x20, local copies, waits for them, and re-layouts  1.59 us
    reshape x2, local copies, waits for them, and re-layouts, blocked(): return array.reshape(rows, row_blocks, block_size).transpose(1, 0, 2)  0.79 us
    add x1, other arithmetic, per_device(): flat(outflow[0])  0.71 us
    reshape x1, local copies, waits for them, and re-layouts, per_device(): cell_rows.reshape(freq_count, 2, share)  0.66 us
    pallas_call x1, Pallas kernels, incidence(): pl.pallas_call(incidence_kernel, out_shape=(jax.ShapeDtypeStruct((blocks,...  0.59 us
  transfers between devices with their start and end apart: 5, of which 4 were waited for; matrix products, arithmetic and copies ran while one was open for 3% of the time, Pallas kernels for 13%

profile of v1, /device:TPU:0, one launch (start us, length us, event | category | flops | bytes accessed | tf_op | source)
XLA Modules:
  0.0 24.7 jit_solution(6297117566200983772)
XLA Ops:
  0.6 0.8 %reshape.85 = bf16[24,4,128]{2,1,0:T(4,128)(2,1)S(1)} reshape(bf16[12,2,512]{2,1,0:T(2,128)(2,1)} %param.15) | data formatting | bytes 49152 | tf_op jit(solution)/shard_map/reshape | solution.py:127
  1.6 4.1 %collective-permute-start = (bf16[2,1,4,24,128]{4,3,2,1,0:T(8,128)(2,1)S(1)}, bf16[2,1,4,24,128]{4,3,2,1,0:T(8,128)(2,1)S(1)}, u32[]{:S(2)}, u32[]{:S(2)}) collective-permute-start(bf16[2,1,4,24,128]{4,3,2,1,0:T(8,128)(2,1)S(1)} %maximum_bitcast_fusion), channel_id=1, source_target_pairs={{0,8},{4,12},{8,0},{12,4},{1,9},{5,13},{9,1},{13,5},{2,10},{6,14},... | collective-permute-start | bytes 147464 | tf_op jit(solution)/shard_map/ppermute | solution.py:25
  5.8 2.5 %collective-permute-done = bf16[2,1,4,24,128]{4,3,2,1,0:T(8,128)(2,1)S(1)} collective-permute-done((bf16[2,1,4,24,128]{4,3,2,1,0:T(8,128)(2,1)S(1)}, bf16[2,1,4,24,128]{4,3,2,1,0:T(8,128)(2,1)S(1)}, u32[]{:S(2)}, u32[]{:S(2)}) %collective-permute-start) | collective-permute-done | bytes 49184 | tf_op jit(solution)/shard_map/ppermute | solution.py:25
  8.4 1.4 %collective-permute-start.1 = (bf16[2,2,4,24,128]{4,3,2,1,0:T(8,128)(2,1)S(1)}, bf16[2,2,4,24,128]{4,3,2,1,0:T(8,128)(2,1)S(1)}, u32[]{:S(2)}, u32[]{:S(2)}) collective-permute-start(bf16[2,2,4,24,128]{4,3,2,1,0:T(8,128)(2,1)S(1)} %pad_maximum_fusion.4), channel_id=1, source_target_pairs={{0,4},{4,0},{8,12},{12,8},{1,5},{5,1},{9,13},{13,9},{2,6},{6,2},{1... | collective-permute-start | bytes 294920 | tf_op jit(solution)/shard_map/ppermute | solution.py:25
  9.9 0.6 %shard_map.105 = (bf16[8,128,512]{2,1,0:T(8,128)(2,1)S(1)}, f32[8,24,128]{2,1,0:T(8,128)S(1)}) custom-call(s32[2,512]{1,0:T(2,128)S(1)} %fusion.1.ends_ref, bf16[24,512]{1,0:T(8,128)(2,1)S(1)} %reshape.88.current_ref), custom_call_target="tpu_custom_call" | custom-call | flops 50331648 | bytes 1048576 | tf_op jit(solution)/shard_map/pallas_call | solution.py:76
  10.5 2.6 %collective-permute-done.1 = bf16[2,2,4,24,128]{4,3,2,1,0:T(8,128)(2,1)S(1)} collective-permute-done((bf16[2,2,4,24,128]{4,3,2,1,0:T(8,128)(2,1)S(1)}, bf16[2,2,4,24,128]{4,3,2,1,0:T(8,128)(2,1)S(1)}, u32[]{:S(2)}, u32[]{:S(2)}) %collective-permute-start.1) | collective-permute-done | bytes 98336 | tf_op jit(solution)/shard_map/ppermute | solution.py:25
  13.1 1.8 %collective-permute-start.2 = (bf16[1,4,4,24,128]{4,3,2,1,0:T(8,128)(2,1)S(1)}, bf16[1,4,4,24,128]{4,3,2,1,0:T(8,128)(2,1)S(1)}, u32[]{:S(2)}, u32[]{:S(2)}) collective-permute-start(bf16[1,4,4,24,128]{4,3,2,1,0:T(8,128)(2,1)S(1)} %get-tuple-element.19), channel_id=1, source_target_pairs={{0,2},{2,0},{1,3},{3,1},{4,6},{6,4},{5,7},{7,5},{8,10},{10,8},{9,1... | collective-permute-start | bytes 294920 | tf_op jit(solution)/shard_map/ppermute | solution.py:25
  14.9 0.4 %collective-permute-start.4 = (bf16[20,24,128]{2,1,0:T(8,128)(2,1)S(1)}, bf16[20,24,128]{2,1,0:T(8,128)(2,1)S(1)}, u32[]{:S(2)}, u32[]{:S(2)}) collective-permute-start(bf16[20,24,128]{2,1,0:T(8,128)(2,1)S(1)} %pad_maximum_fusion.3), channel_id=1, source_target_pairs={{0,2},{2,0},{1,3},{3,1},{4,6},{6,4},{5,7},{7,5},{8,10},{10,8},{9,1... | collective-permute-start | bytes 368648 | tf_op jit(solution)/shard_map/ppermute | solution.py:25
  15.3 0.1 pad_add_fusion.place_ref
  15.4 0.2 copy-done.4
  15.6 0.1 copy.16.cols_ref
  15.7 0.6 %copy-done.5 = s32[4,4,2]{1,2,0:T(2,128)S(1)} copy-done((s32[4,4,2]{1,2,0:T(2,128)S(1)}, s32[4,4,2]{1,2,0:T(2,128)}, u32[]{:S(2)}) %copy-start.5) | copy-done | bytes 152
  16.3 0.1 copy.17.cols_ref
  16.4 0.5 %copy-done.8 = f32[12]{0:T(128)S(1)} copy-done((f32[12]{0:T(128)S(1)}, f32[12]{0:T(128)}, u32[]{:S(2)}) %copy-start.8) | copy-done | bytes 72
  17.0 0.1 mul.34
  17.1 0.7 %collective-permute-done.2 = bf16[1,4,4,24,128]{4,3,2,1,0:T(8,128)(2,1)S(1)} collective-permute-done((bf16[1,4,4,24,128]{4,3,2,1,0:T(8,128)(2,1)S(1)}, bf16[1,4,4,24,128]{4,3,2,1,0:T(8,128)(2,1)S(1)}, u32[]{:S(2)}, u32[]{:S(2)}) %collective-permute-start.2) | collective-permute-done | bytes 98336 | tf_op jit(solution)/shard_map/ppermute | solution.py:25
  17.8 1.3 %shard_map.104 = bf16[4,24,128]{2,1,0:T(8,128)(2,1)S(1)} custom-call(s32[4,4,2]{2,1,0:T(4,128)S(1)} %copy.16.cols_ref, s32[2]{0:T(128)S(1)} %pad_add_fusion.place_ref, bf16[2,4,4,24,128]{4,3,2,1,0:T(8,128)(2,1)S(1)} %pad_maximum_fusion.1.held_ref, bf16[4,4,2,128,128]{4,3,2,1,0:T(8,128)(2,1)S(1)} %copy-done.1), custom_call_target="tpu_custom_call" | custom-call | flops 25165824 | bytes 1245184 | tf_op jit(solution)/shard_map/pallas_call | solution.py:48
  19.1 1.8 %collective-permute-start.3 = (bf16[1,4,24,128]{3,2,1,0:T(8,128)(2,1)S(1)}, bf16[1,4,24,128]{3,2,1,0:T(8,128)(2,1)S(1)}, u32[]{:S(2)}, u32[]{:S(2)}) collective-permute-start(bf16[1,4,24,128]{3,2,1,0:T(8,128)(2,1)S(1)} %bitcast.27), channel_id=1, source_target_pairs={{0,2},{2,0},{1,3},{3,1},{4,6},{6,4},{5,7},{7,5},{8,10},{10,8},{9,1... | collective-permute-start | bytes 73736 | tf_op jit(solution)/shard_map/ppermute | solution.py:25
  21.0 1.3 %shard_map.106 = f32[4,24,128]{2,1,0:T(8,128)S(1)} custom-call(s32[4,4,2]{2,1,0:T(4,128)S(1)} %copy.17.cols_ref, s32[2]{0:T(128)S(1)} %pad_add_fusion.place_ref, bf16[2,4,4,24,128]{4,3,2,1,0:T(8,128)(2,1)S(1)} %pad_maximum_fusion.2.held_ref, bf16[4,4,2,128,128]{4,3,2,1,0:T(8,128)(2,1)S(1)} %copy-done), custom_call_target="tpu_custom_call" | custom-call | flops 25165824 | bytes 1245184 | tf_op jit(solution)/shard_map/pallas_call | solution.py:48
  22.3 0.1 fusion.base_ref
  22.4 0.6 %collective-permute-done.3 = bf16[1,4,24,128]{3,2,1,0:T(8,128)(2,1)S(1)} collective-permute-done((bf16[1,4,24,128]{3,2,1,0:T(8,128)(2,1)S(1)}, bf16[1,4,24,128]{3,2,1,0:T(8,128)(2,1)S(1)}, u32[]{:S(2)}, u32[]{:S(2)}) %collective-permute-start.3) | collective-permute-done | bytes 24608 | tf_op jit(solution)/shard_map/ppermute | solution.py:25
  23.0 0.3 %shard_map.107 = f32[24,512]{1,0:T(8,128)S(1)} custom-call(bf16[8,24,128]{2,1,0:T(8,128)(2,1)S(1)} %bitcast.26, bf16[8,128,512]{2,1,0:T(8,128)(2,1)S(1)} %get-tuple-element.16.matrix_ref, f32[24,512]{1,0:T(8,128)S(1)} %fusion.base_ref), custom_call_target="tpu_custom_call" | custom-call | flops 25165824 | bytes 1048576 | tf_op jit(solution)/shard_map/pallas_call | solution.py:101
  23.3 0.7 %reshape.91 = f32[12,2,512]{2,1,0:T(2,128)} reshape(f32[24,512]{1,0:T(8,128)S(1)} %shard_map.107) | data formatting | bytes 98304 | tf_op jit(solution)/shard_map/reshape | solution.py:167
  24.0 0.7 %multiply_add_fusion = f32[12,2,512]{2,1,0:T(2,128)} fusion(f32[12,2,512]{2,1,0:T(2,128)S(1)} %reshape.92, f32[12]{0:T(128)S(1)} %copy-done.8, bf16[12,1,512]{2,1,0:T(2,128)(2,1)S(1)} %get-tuple-element.21, bf16[12,1,512]{2,1,0:T(2,128)(2,1)S(1)} %get-tuple-element.20), kind=kLoop, calls=%fused_computation.10 | loop fusion | flops 73728 | bytes 122928 | tf_op jit(solution)/shard_map/add | solution.py:166
  (37 shorter events, 0.6 us)
Async XLA Ops:
  0.6 0.8 %copy-start.3 = (bf16[12,2,512]{2,1,0:T(2,128)(2,1)S(1)}, bf16[12,2,512]{2,1,0:T(2,128)(2,1)}, u32[]{:S(2)}) copy-start(bf16[12,2,512]{2,1,0:T(2,128)(2,1)} %param.16) | copy-start | bytes 73732
  1.6 4.2 %copy-start.2 = (bf16[12,2,512]{2,1,0:T(2,128)(2,1)S(1)}, bf16[12,2,512]{2,1,0:T(2,128)(2,1)}, u32[]{:S(2)}) copy-start(bf16[12,2,512]{2,1,0:T(2,128)(2,1)} %param.15) | copy-start | bytes 73732
  1.6 8.2 %copy-start.6 = (s32[2,512]{1,0:T(2,128)S(1)}, s32[2,512]{1,0:T(2,128)}, u32[]{:S(2)}) copy-start(s32[2,512]{1,0:T(2,128)} %param.19) | copy-start | bytes 12292
  1.6 16.2 %copy-start.1 = (bf16[4,4,2,128,128]{4,3,2,1,0:T(8,128)(2,1)S(1)}, bf16[4,4,2,128,128]{4,3,2,1,0:T(8,128)(2,1)}, u32[]{:S(2)}) copy-start(bf16[4,4,2,128,128]{4,3,2,1,0:T(8,128)(2,1)} %slab_ref.2) | copy-start | bytes 3145732
  1.6 6.7 %collective-permute-start = (bf16[2,1,4,24,128]{4,3,2,1,0:T(8,128)(2,1)S(1)}, bf16[2,1,4,24,128]{4,3,2,1,0:T(8,128)(2,1)S(1)}, u32[]{:S(2)}, u32[]{:S(2)}) collective-permute-start(bf16[2,1,4,24,128]{4,3,2,1,0:T(8,128)(2,1)S(1)} %maximum_bitcast_fusion), channel_id=1, source_target_pairs={{0,8},{4,12},{8,0},{12,4},{1,9},{5,13},{9,1},{13,5},{2,10},{6,14},... | collective-permute-start | bytes 147464 | tf_op jit(solution)/shard_map/ppermute | solution.py:25
  8.4 4.7 %collective-permute-start.1 = (bf16[2,2,4,24,128]{4,3,2,1,0:T(8,128)(2,1)S(1)}, bf16[2,2,4,24,128]{4,3,2,1,0:T(8,128)(2,1)S(1)}, u32[]{:S(2)}, u32[]{:S(2)}) collective-permute-start(bf16[2,2,4,24,128]{4,3,2,1,0:T(8,128)(2,1)S(1)} %pad_maximum_fusion.4), channel_id=1, source_target_pairs={{0,4},{4,0},{8,12},{12,8},{1,5},{5,1},{9,13},{13,9},{2,6},{6,2},{1... | collective-permute-start | bytes 294920 | tf_op jit(solution)/shard_map/ppermute | solution.py:25
  13.1 4.7 %collective-permute-start.2 = (bf16[1,4,4,24,128]{4,3,2,1,0:T(8,128)(2,1)S(1)}, bf16[1,4,4,24,128]{4,3,2,1,0:T(8,128)(2,1)S(1)}, u32[]{:S(2)}, u32[]{:S(2)}) collective-permute-start(bf16[1,4,4,24,128]{4,3,2,1,0:T(8,128)(2,1)S(1)} %get-tuple-element.19), channel_id=1, source_target_pairs={{0,2},{2,0},{1,3},{3,1},{4,6},{6,4},{5,7},{7,5},{8,10},{10,8},{9,1... | collective-permute-start | bytes 294920 | tf_op jit(solution)/shard_map/ppermute | solution.py:25
  14.9 0.7 %copy-start.4 = (s32[4,4,2]{1,2,0:T(2,128)S(1)}, s32[4,4,2]{1,2,0:T(2,128)}, u32[]{:S(2)}) copy-start(s32[4,4,2]{1,2,0:T(2,128)} %param.12) | copy-start | bytes 388
  14.9 6.0 %collective-permute-start.4 = (bf16[20,24,128]{2,1,0:T(8,128)(2,1)S(1)}, bf16[20,24,128]{2,1,0:T(8,128)(2,1)S(1)}, u32[]{:S(2)}, u32[]{:S(2)}) collective-permute-start(bf16[20,24,128]{2,1,0:T(8,128)(2,1)S(1)} %pad_maximum_fusion.3), channel_id=1, source_target_pairs={{0,2},{2,0},{1,3},{3,1},{4,6},{6,4},{5,7},{7,5},{8,10},{10,8},{9,1... | collective-permute-start | bytes 368648 | tf_op jit(solution)/shard_map/ppermute | solution.py:25
  15.6 0.7 %copy-start.5 = (s32[4,4,2]{1,2,0:T(2,128)S(1)}, s32[4,4,2]{1,2,0:T(2,128)}, u32[]{:S(2)}) copy-start(s32[4,4,2]{1,2,0:T(2,128)} %param.14) | copy-start | bytes 388
  16.3 0.7 %copy-start.8 = (f32[12]{0:T(128)S(1)}, f32[12]{0:T(128)}, u32[]{:S(2)}) copy-start(f32[12]{0:T(128)} %param.17) | copy-start | bytes 148
  17.1 3.9 %copy-start = (bf16[4,4,2,128,128]{4,3,2,1,0:T(8,128)(2,1)S(1)}, bf16[4,4,2,128,128]{4,3,2,1,0:T(8,128)(2,1)}, u32[]{:S(2)}) copy-start(bf16[4,4,2,128,128]{4,3,2,1,0:T(8,128)(2,1)} %slab_ref.3) | copy-start | bytes 3145732
  19.1 3.8 %collective-permute-start.3 = (bf16[1,4,24,128]{3,2,1,0:T(8,128)(2,1)S(1)}, bf16[1,4,24,128]{3,2,1,0:T(8,128)(2,1)S(1)}, u32[]{:S(2)}, u32[]{:S(2)}) collective-permute-start(bf16[1,4,24,128]{3,2,1,0:T(8,128)(2,1)S(1)} %bitcast.27), channel_id=1, source_target_pairs={{0,2},{2,0},{1,3},{3,1},{4,6},{6,4},{5,7},{7,5},{8,10},{10,8},{9,1... | collective-permute-start | bytes 73736 | tf_op jit(solution)/shard_map/ppermute | solution.py:25
  21.0 1.3 %copy-start.7 = (f32[512]{0:T(512)S(1)}, f32[512]{0:T(512)}, u32[]{:S(2)}) copy-start(f32[512]{0:T(512)} %param.18) | copy-start | bytes 6148

commit v2 on v1

--- a/solution.py
+++ b/solution.py
@@ -11,6 +11,13 @@
 NN = (((1,), (0,)), ((), ()))
 VMEM = pl.BlockSpec(memory_space=pltpu.VMEM)
 SMEM = pl.BlockSpec(memory_space=pltpu.SMEM)
+ANY = pl.BlockSpec(memory_space=pl.ANY)
+HBM = pl.BlockSpec(memory_space=pltpu.HBM)
+JOIN = 10_000_000
+SEND = 1_000
+FIRST = 1_000
+NEXT = 3_000_000
+LAST = 8_000_000
 
 
 def halves(count):
@@ -114,7 +121,7 @@
     return jnp.stack([-array[:, 1], array[:, 0]], axis=1)
 
 
-def per_device(p_blocks, p_cols, l_blocks, l_cols, charges, currents, omegas, resist, branch_ends):
+def general_step(p_blocks, p_cols, l_blocks, l_cols, charges, currents, omegas, resist, branch_ends):
     freq_count, _, share = charges.shape
     block_size = p_blocks.shape[-1]
     row_blocks = p_blocks.shape[0]
@@ -167,6 +174,251 @@
     return (cell_rows.reshape(freq_count, 2, share), panel_rows.reshape(freq_count, 2, share))
 
 
+def back(regions, shift):
+    return lax.rem(lax.axis_index("blk") + regions - shift, regions)
+
+
+def turned_rows(array):
+    rows = array.shape[0]
+    odd = lax.broadcasted_iota(jnp.int32, array.shape, 0) & 1
+    return jnp.where(odd == 0, -pltpu.roll(array, rows - 1, 0), pltpu.roll(array, 1, 0))
+
+
+def row_scale(omega_ref, rows):
+    shape = (rows, omega_ref.shape[1])
+    same = lax.broadcasted_iota(jnp.int32, shape, 0) >> 1 == lax.broadcasted_iota(jnp.int32, shape, 1)
+    return jnp.sum(jnp.where(same, omega_ref[...], 0.0), axis=1, keepdims=True)
+
+
+def lanes(blocks):
+    return jnp.concatenate(blocks, axis=1)
+
+
+def pair_dot(held_ref, positions, slabs):
+    return lax.dot_general(
+        lanes([held_ref[position] for position in positions]), lanes(slabs), NT, preferred_element_type=jnp.float32
+    )
+
+
+def region_terms(shift, table_ref, held_ref, p_ref, l_ref, region, row):
+    slots = range(p_ref.shape[2])
+    return tuple(
+        pair_dot(
+            held_ref.at[kind],
+            [table_ref[kind, shift, row, slot, 0] for slot in slots],
+            [slab_ref[row, region, slot] for slot in slots],
+        )
+        for kind, slab_ref in enumerate((p_ref, l_ref))
+    )
+
+
+def first_kernel(
+    regions, held_ref, p_ref, l_ref, p_cols_ref, l_cols_ref, ends_ref,
+    table_ref, potential_ref, flux_ref, matrix_ref, outflow_ref, early_ref, numbers_ref,
+):
+    row_blocks, rows, block_size = potential_ref.shape
+    slots = p_ref.shape[2]
+    cell = lax.axis_index("cell")
+    shape = table_ref.shape[2:]
+    lane = lax.broadcasted_iota(jnp.int32, shape, 2)
+    numbers = jnp.zeros(shape, jnp.float32)
+    for kind, cols_ref in enumerate((p_cols_ref, l_cols_ref)):
+        columns = cols_ref[...].astype(jnp.float32)
+        place = lax.broadcasted_iota(jnp.int32, columns.shape, 2)
+        for shift in range(regions):
+            column = jnp.sum(jnp.where(place == back(regions, shift), columns, 0.0), axis=2, keepdims=True)
+            column = jnp.broadcast_to(column, shape)
+            other = jnp.where(column < row_blocks, column + row_blocks, column - row_blocks)
+            table_ref[kind, shift] = jnp.where(cell == 0, column, other).astype(jnp.int32)
+            if kind == 0:
+                numbers = jnp.where(lane == shift, jnp.where(cell == 0, other, column), numbers)
+    numbers_ref[...] = jnp.zeros_like(numbers_ref)
+    for row in range(row_blocks):
+        numbers_ref[row * slots : (row + 1) * slots, :] = numbers[row]
+    early_ref[2 * row_blocks] = numbers_ref[...].astype(jnp.bfloat16)
+    for row in range(row_blocks):
+        potential, flux = region_terms(0, table_ref, held_ref, p_ref, l_ref, back(regions, 0), row)
+        potential_ref[row], flux_ref[row] = potential, flux
+        early_ref[row] = potential.astype(jnp.bfloat16)
+    leaves, enters = ends_ref[0:1, :], ends_ref[1:2, :]
+    current = lanes([held_ref[1, block] for block in range(row_blocks)])
+    for block in range(2 * row_blocks):
+        side, at = divmod(block, row_blocks)
+        base = ((cell ^ side) * row_blocks + at) * block_size
+        panel = lax.broadcasted_iota(jnp.int32, (block_size, ends_ref.shape[1]), 0) + base
+        entry = (leaves == panel).astype(jnp.float32) - (enters == panel).astype(jnp.float32)
+        entry = entry.astype(jnp.bfloat16)
+        matrix_ref[block] = entry
+        sums = lax.dot_general(current, entry, NT, preferred_element_type=jnp.float32)
+        if side == 0:
+            outflow_ref[at] = sums
+        else:
+            early_ref[block] = sums.astype(jnp.bfloat16)
+
+
+def next_kernel(regions, shift, table_ref, held_ref, p_ref, l_ref, p_in_ref, f_in_ref, *refs):
+    potential_ref, flux_ref = refs[-2:]
+    region = back(regions, shift)
+    for row in range(potential_ref.shape[0]):
+        potential, flux = region_terms(shift, table_ref, held_ref, p_ref, l_ref, region, row)
+        potential_ref[row], flux_ref[row] = p_in_ref[row] + potential, f_in_ref[row] + flux
+
+
+def send_kernel(regions, p_ref, after_ref, out_ref, sems):
+    del after_ref
+    half = out_ref.shape[1]
+    start = lax.axis_index("col") * half
+    copies = [
+        pltpu.make_async_copy(
+            p_ref.at[pl.ds(start, half), back(regions, shift)], out_ref.at[shift - 1], sems.at[shift - 1]
+        )
+        for shift in range(1, regions)
+    ]
+    for copy in copies:
+        copy.start()
+    for copy in copies:
+        copy.wait()
+
+
+def join_kernel(own_ref, other_ref, out_ref):
+    blocks = own_ref.shape[1]
+    for kind in range(own_ref.shape[0]):
+        out_ref[kind, :blocks] = own_ref[kind]
+        out_ref[kind, blocks:] = other_ref[kind]
+
+
+def store_rows(out_ref, columns, array):
+    for freq in range(out_ref.shape[0]):
+        out_ref[freq, :, columns] = array[2 * freq : 2 * freq + 2]
+
+
+def last_kernel(regions, mine_ref, theirs_ref, *refs):
+    piece_refs = refs[: regions - 1]
+    (table_ref, p_ref, l_ref, p_in_ref, f_in_ref, early_ref, matrix_ref, held_ref, outflow_ref, omega_ref,
+     resist_ref, cell_ref, panel_ref, other_ref, numbers_ref) = refs[regions - 1 :]
+    row_blocks, rows, block_size = p_in_ref.shape
+    half = row_blocks // 2
+    slots = range(mine_ref.shape[2])
+    core = lax.axis_index("col")
+    numbers_ref[...] = early_ref[2 * row_blocks].astype(jnp.float32).astype(jnp.int32)
+    potentials, fluxes = [], []
+    for row in range(row_blocks):
+        potential, flux = p_in_ref[row], f_in_ref[row]
+        if regions > 1:
+            shift = regions - 1
+            terms = region_terms(shift, table_ref, piece_refs[-1], p_ref, l_ref, back(regions, shift), row)
+            potential, flux = potential + terms[0], flux + terms[1]
+        potentials.append(potential.astype(jnp.bfloat16))
+        fluxes.append(flux)
+    for part, slab_ref in enumerate((mine_ref, theirs_ref)):
+        for position in range(half):
+            row = (core ^ part) * half + position
+            total = early_ref[row].astype(jnp.float32)
+            for shift in range(1, regions):
+                total += pair_dot(
+                    piece_refs[shift - 1].at[0],
+                    [numbers_ref[row * len(slots) + slot, shift] for slot in slots],
+                    [slab_ref[shift - 1, position, slot] for slot in slots],
+                )
+            other_ref[row] = total.astype(jnp.bfloat16)
+    matrix = matrix_ref[...].reshape(2, row_blocks * block_size, -1)
+    drop = lax.dot_general(lanes(potentials), matrix[0], NN, preferred_element_type=jnp.float32)
+    others = lanes([other_ref[row] for row in range(row_blocks)])
+    drop += lax.dot_general(others, matrix[1], NN, preferred_element_type=jnp.float32)
+    scale = row_scale(omega_ref, rows)
+    for row in range(row_blocks):
+        columns = slice(row * block_size, (row + 1) * block_size)
+        current = held_ref[1, row].astype(jnp.float32)
+        flux = scale * turned_rows(fluxes[row])
+        store_rows(cell_ref, columns, resist_ref[:, columns] * current + flux + drop[:, columns])
+        outflow = outflow_ref[row] + early_ref[row_blocks + row].astype(jnp.float32)
+        charge = scale * turned_rows(held_ref[0, row].astype(jnp.float32))
+        store_rows(panel_ref, columns, outflow + charge)
+
+
+def kernel_call(body, out_shape, memories, cost, scratch=(), size=4_000_000):
+    many = isinstance(out_shape, tuple)
+    return pl.pallas_call(
+        body,
+        out_shape=out_shape,
+        in_specs=[{"h": HBM, "v": VMEM, "a": ANY}[m] for m in memories],
+        out_specs=tuple(VMEM for _ in out_shape) if many else VMEM,
+        scratch_shapes=scratch,
+        compiler_params=pltpu.CompilerParams(vmem_limit_bytes=16 * 1024 * 1024),
+        cost_estimate=pl.CostEstimate(flops=cost * 1000, bytes_accessed=size, transcendentals=0),
+    )
+
+
+def paired_step(p_blocks, p_cols, l_blocks, l_cols, charges, currents, omegas, resist, branch_ends):
+    freq_count, _, share = charges.shape
+    block_size = p_blocks.shape[-1]
+    row_blocks = p_blocks.shape[0]
+    rows = 2 * freq_count
+    regions = lax.axis_size("blk")
+
+    def blocked(array):
+        return array.reshape(rows, row_blocks, block_size).transpose(1, 0, 2)
+
+    message = jnp.stack([blocked(charges), blocked(currents)])
+    got = swapped(message, "cell", 1)
+    held = kernel_call(
+        join_kernel, jax.ShapeDtypeStruct((2, 2 * row_blocks, rows, block_size), jnp.bfloat16), "vv", JOIN
+    )(message, got)
+
+    half_shape = jax.ShapeDtypeStruct((regions - 1, row_blocks // 2) + p_blocks.shape[2:], jnp.bfloat16)
+    sent = kernel_call(
+        functools.partial(send_kernel, regions), half_shape, "ha", SEND, [pltpu.SemaphoreType.DMA((regions - 1,))]
+    )(p_blocks, message)
+    mine = swapped(sent, "cell", 1)
+    theirs = swapped(mine, "col", 1)
+
+    pieces = [
+        lax.ppermute(held, "blk", [(i, (i + shift) % regions) for i in range(regions)])
+        for shift in range(1, regions)
+    ]
+
+    slots = p_cols.shape[2]
+    totals = jax.ShapeDtypeStruct((row_blocks, rows, block_size), jnp.float32)
+    table, potential, flux, matrix, outflow, early = kernel_call(
+        functools.partial(first_kernel, regions),
+        (
+            jax.ShapeDtypeStruct((2, regions, row_blocks, slots, block_size), jnp.int32),
+            totals,
+            totals,
+            jax.ShapeDtypeStruct((2 * row_blocks, block_size, share), jnp.bfloat16),
+            totals,
+            jax.ShapeDtypeStruct((2 * row_blocks + 1, rows, block_size), jnp.bfloat16),
+        ),
+        "vvvvvv",
+        FIRST,
+        [pltpu.VMEM((rows, block_size), jnp.float32)],
+    )(held, p_blocks, l_blocks, p_cols.transpose(0, 2, 1), l_cols.transpose(0, 2, 1), branch_ends)
+    early = swapped(early, "cell", 1)
+    for shift in range(1, regions - 1):
+        potential, flux = kernel_call(
+            functools.partial(next_kernel, regions, shift), (totals, totals), "vvvvvvv", NEXT
+        )(table, pieces[shift - 1], p_blocks, l_blocks, potential, flux, matrix)
+
+    result = jax.ShapeDtypeStruct(charges.shape, jnp.float32)
+    return kernel_call(
+        functools.partial(last_kernel, regions),
+        (result, result),
+        "v" * (12 + regions),
+        LAST,
+        [pltpu.VMEM((row_blocks, rows, block_size), jnp.bfloat16), pltpu.VMEM((rows, block_size), jnp.int32)],
+    )(
+        mine, theirs, *pieces, table, p_blocks, l_blocks, potential, flux, early, matrix, held, outflow,
+        omegas[None], resist[None],
+    )
+
+
+def per_device(*args):
+    row_blocks, regions = args[0].shape[:2]
+    paired = lax.axis_size("cell") == 2 and lax.axis_size("col") == 2
+    paired = paired and row_blocks % 2 == 0 and row_blocks * args[0].shape[2] <= 2 * args[4].shape[0]
+    return (paired_step if paired else general_step)(*args)
+
+
 def solution(mesh):
     placed = (
         P(("job", "blk", "cell"), None, None, None, None),

time: 24.9 us -> 21.6 us (0.87)
  waiting for transfers between devices: 6.4 us -> 4.86 us
  other arithmetic: 1.18 us -> 0.01 us
  local copies, waits for them, and re-layouts: 3.32 us -> 2.72 us
  starting transfers between devices: 9.47 us -> 9.83 us
  Pallas kernels: 3.49 us -> 3.16 us
    ppermute x0 -> x3, starting transfers between devices: none -> 5.2 us  [paired_step(): lax.ppermute(held, 'blk', [(i, (i + shift) % regions) for i in range(regi...]
    ppermute x5 -> x4, starting transfers between devices: 9.47 us -> 4.63 us  [swapped(): lax.ppermute(array, axis, [(i, i ^ distance) for i in range(lax.axis_size...]
    ppermute x5 -> x4, waiting for transfers between devices: 6.4 us -> 3.54 us  [swapped(): lax.ppermute(array, axis, [(i, i ^ distance) for i in range(lax.axis_size...]
    ppermute x0 -> x3, waiting for transfers between devices: none -> 1.32 us  [paired_step(): lax.ppermute(held, 'blk', [(i, (i + shift) % regions) for i in range(regi...]
    add x3 -> x0, other arithmetic: 0.82 us -> none  [the longest x1 0.71 us: per_device(): flat(outflow[0])]
    reshape x3 -> x0, local copies, waits for them, and re-layouts: 0.72 us -> none  [the longest x1 0.66 us: per_device(): cell_rows.reshape(freq_count, 2, share)]
    unnamed x20 -> x18, local copies, waits for them, and re-layouts: 1.59 us -> 1.92 us
    pallas_call x4 -> x6, Pallas kernels: 3.49 us -> 3.16 us  [the longest x1 1.47 us: paired_step(): kernel_call(functools.partial(last_kernel, regions), (result, result), 'v...]
  transfers between devices with their start and end apart: 5 -> 7, of which waited for: 4 -> 3; matrix products, arithmetic and copies ran while one was open for 3% -> 0% of each run, Pallas kernels for 13% -> 8%
where the time goes in v2:
time: 21.6 us; the launch traced here: 21.3 us
  starting transfers between devices  9.83 us (46%)
  waiting for transfers between devices  4.86 us (22%)
  Pallas kernels  3.16 us (15%)
  local copies, waits for them, and re-layouts  2.72 us (13%)
  between operations  0.76 us (4%)
    ppermute x3, starting transfers between devices, paired_step(): lax.ppermute(held, 'blk', [(i, (i + shift) % regions) for i in range(regi...  5.2 us
    ppermute x4, starting transfers between devices, swapped(): lax.ppermute(array, axis, [(i, i ^ distance) for i in range(lax.axis_size...  4.63 us
    ppermute x4, waiting for transfers between devices, swapped(): lax.ppermute(array, axis, [(i, i ^ distance) for i in range(lax.axis_size...  3.54 us
    unnamed x18, local copies, waits for them, and re-layouts  1.92 us
    pallas_call x1, Pallas kernels, paired_step(): kernel_call(functools.partial(last_kernel, regions), (result, result), 'v...  1.47 us
    ppermute x3, waiting for transfers between devices, paired_step(): lax.ppermute(held, 'blk', [(i, (i + shift) % regions) for i in range(regi...  1.32 us
    pallas_call x1, Pallas kernels, paired_step(): kernel_call(functools.partial(first_kernel, regions), (jax.ShapeDtypeStru...  0.83 us
    reshape x2, local copies, waits for them, and re-layouts, blocked(): return array.reshape(rows, row_blocks, block_size).transpose(1, 0, 2)  0.79 us
  transfers between devices with their start and end apart: 7, of which 3 were waited for; matrix products, arithmetic and copies ran while one was open for 0% of the time, Pallas kernels for 8%

profile of v2, /device:TPU:0, one launch (start us, length us, event | category | flops | bytes accessed | tf_op | source)
XLA Modules:
  0.0 21.3 jit_solution(16278495295614884429)
XLA Ops:
  0.6 0.8 %reshape.10 = bf16[24,4,128]{2,1,0:T(4,128)(2,1)S(1)} reshape(bf16[12,2,512]{2,1,0:T(2,128)(2,1)} %param.13) | data formatting | bytes 49152 | tf_op jit(solution)/shard_map/reshape | solution.py:360
  1.5 3.0 %collective-permute-start.2 = (bf16[2,4,24,128]{3,2,1,0:T(8,128)(2,1)S(1)}, bf16[2,4,24,128]{3,2,1,0:T(8,128)(2,1)S(1)}, u32[]{:S(2)}, u32[]{:S(2)}) collective-permute-start(bf16[2,4,24,128]{3,2,1,0:T(8,128)(2,1)S(1)} %pad_maximum_fusion.after_ref.own_ref), channel_id=1, source_target_pairs={{0,2},{2,0},{1,3},{3,1},{4,6},{6,4},{5,7},{7,5},{8,10},{10,8},{9,1... | collective-permute-start | bytes 147464 | tf_op jit(solution)/shard_map/ppermute | solution.py:32
  4.5 1.2 %copy-done = bf16[4,4,2,128,128]{4,3,2,1,0:T(8,128)(2,1)S(1)} copy-done((bf16[4,4,2,128,128]{4,3,2,1,0:T(8,128)(2,1)S(1)}, bf16[4,4,2,128,128]{4,3,2,1,0:T(8,128)(2,1)}, u32[]{:S(2)}) %copy-start) | copy-done | bytes 1048600
  5.7 0.3 %shard_map.104 = bf16[3,2,2,128,128]{4,3,2,1,0:T(8,128)(2,1)S(1)} custom-call(bf16[4,4,2,128,128]{4,3,2,1,0:T(8,128)(2,1)S(1)} %copy-done, bf16[2,4,24,128]{3,2,1,0:T(8,128)(2,1)S(1)} %pad_maximum_fusion.after_ref.own_ref), custom_call_target="tpu_custom_call" | custom-call | flops 1000000 | bytes 4000000 | tf_op jit(solution)/shard_map/pallas_call | solution.py:369
  6.0 0.0 copy-start.1
  6.0 0.0 copy-start.2
  6.0 0.1 collective-permute-start
  6.1 0.5 %collective-permute-done.2.other_ref = bf16[2,4,24,128]{3,2,1,0:T(8,128)(2,1)S(1)} collective-permute-done((bf16[2,4,24,128]{3,2,1,0:T(8,128)(2,1)S(1)}, bf16[2,4,24,128]{3,2,1,0:T(8,128)(2,1)S(1)}, u32[]{:S(2)}, u32[]{:S(2)}) %collective-permute-start.2) | collective-permute-done | bytes 49184 | tf_op jit(solution)/shard_map/ppermute | solution.py:32
  6.6 2.2 %collective-permute-start.3 = (bf16[2,8,24,128]{3,2,1,0:T(8,128)(2,1)S(1)}, bf16[2,8,24,128]{3,2,1,0:T(8,128)(2,1)S(1)}, u32[]{:S(2)}, u32[]{:S(2)}) collective-permute-start(bf16[2,8,24,128]{3,2,1,0:T(8,128)(2,1)S(1)} %shard_map.105.held_ref.refs_10_), channel_id=1, source_target_pairs={{0,4},{4,8},{8,12},{12,0},{1,5},{5,9},{9,13},{13,1},{2,6},{6,10},{... | collective-permute-start | bytes 294920 | tf_op jit(solution)/shard_map/ppermute | solution.py:376
  8.7 2.1 %collective-permute-start.5 = (bf16[2,8,24,128]{3,2,1,0:T(8,128)(2,1)S(1)}, bf16[2,8,24,128]{3,2,1,0:T(8,128)(2,1)S(1)}, u32[]{:S(2)}, u32[]{:S(2)}) collective-permute-start(bf16[2,8,24,128]{3,2,1,0:T(8,128)(2,1)S(1)} %shard_map.105.held_ref.refs_10_), channel_id=1, source_target_pairs={{0,12},{4,0},{8,4},{12,8},{1,13},{5,1},{9,5},{13,9},{2,14},{6,2},{... | collective-permute-start | bytes 294920 | tf_op jit(solution)/shard_map/ppermute | solution.py:376
  10.8 0.9 %collective-permute-start.4 = (bf16[2,8,24,128]{3,2,1,0:T(8,128)(2,1)S(1)}, bf16[2,8,24,128]{3,2,1,0:T(8,128)(2,1)S(1)}, u32[]{:S(2)}, u32[]{:S(2)}) collective-permute-start(bf16[2,8,24,128]{3,2,1,0:T(8,128)(2,1)S(1)} %shard_map.105.held_ref.refs_10_), channel_id=1, source_target_pairs={{0,8},{4,12},{8,0},{12,4},{1,9},{5,13},{9,1},{13,5},{2,10},{6,14},... | collective-permute-start | bytes 294920 | tf_op jit(solution)/shard_map/ppermute | solution.py:376
  11.8 0.8 %shard_map.106 = (s32[2,4,4,2,128]{4,3,2,1,0:T(2,128)S(1)}, f32[4,24,128]{2,1,0:T(8,128)S(1)}, f32[4,24,128]{2,1,0:T(8,128)S(1)}, bf16[8,128,512]{2,1,0:T(8,128)...) custom-call(bf16[2,8,24,128]{3,2,1,0:T(8,128)(2,1)S(1)} %shard_map.105.held_ref.refs_10_, ...), custom_call_target="tpu_custom_call" | custom-call | flops 1000000 | bytes 4000000 | tf_op jit(solution)/shard_map/pallas_call | solution.py:382
  12.6 1.5 %collective-permute-start.6 = (bf16[9,24,128]{2,1,0:T(8,128)(2,1)S(1)}, bf16[9,24,128]{2,1,0:T(8,128)(2,1)S(1)}, u32[]{:S(2)}, u32[]{:S(2)}) collective-permute-start(bf16[9,24,128]{2,1,0:T(8,128)(2,1)S(1)} %get-tuple-element.20), channel_id=1, source_target_pairs={{0,2},{2,0},{1,3},{3,1},{4,6},{6,4},{5,7},{7,5},{8,10},{10,8},{9,1... | collective-permute-start | bytes 165896 | tf_op jit(solution)/shard_map/ppermute | solution.py:32
  14.2 3.1 %collective-permute-done.mine_ref = bf16[3,2,2,128,128]{4,3,2,1,0:T(8,128)(2,1)S(1)} collective-permute-done((bf16[3,2,2,128,128]{4,3,2,1,0:T(8,128)(2,1)S(1)}, bf16[3,2,2,128,128]{4,3,2,1,0:T(8,128)(2,1)S(1)}, u32[]{:S(2)}, u32[]{:S(2)}) %collective-permute-start) | collective-permute-done | bytes 393248 | tf_op jit(solution)/shard_map/ppermute | solution.py:32
  17.2 0.0 collective-permute-start.1
  17.2 0.3 %shard_map.107 = (f32[4,24,128]{2,1,0:T(8,128)S(1)}, f32[4,24,128]{2,1,0:T(8,128)S(1)}) custom-call(s32[2,4,4,2,128]{4,3,2,1,0:T(2,128)S(1)} %get-tuple-element.12.table_ref.refs_3_, bf16[2,8,24,128]{3,2,1,0:T(8,128)(2,1)S(1)} %collective-permute-done.3.held_ref.refs_0_, bf16[4,4,2,128,128]{4,3,2,1,0:T(8,128)(2,1)S(1)} %copy-done.1, ...), custom_call_target="tpu_custom_call" | custom-call | flops 3000000000 | bytes 4000000 | tf_op jit(solution)/shard_map/pallas_call | solution.py:398
  17.5 1.3 %collective-permute-done.4.held_ref.refs_1_ = bf16[2,8,24,128]{3,2,1,0:T(8,128)(2,1)S(1)} collective-permute-done((bf16[2,8,24,128]{3,2,1,0:T(8,128)(2,1)S(1)}, bf16[2,8,24,128]{3,2,1,0:T(8,128)(2,1)S(1)}, u32[]{:S(2)}, u32[]{:S(2)}) %collective-permute-start.4) | collective-permute-done | bytes 98336 | tf_op jit(solution)/shard_map/ppermute | solution.py:376
  18.8 0.3 %shard_map.108 = (f32[4,24,128]{2,1,0:T(8,128)S(1)}, f32[4,24,128]{2,1,0:T(8,128)S(1)}) custom-call(s32[2,4,4,2,128]{4,3,2,1,0:T(2,128)S(1)} %get-tuple-element.12.table_ref.refs_3_, bf16[2,8,24,128]{3,2,1,0:T(8,128)(2,1)S(1)} %collective-permute-done.4.held_ref.refs_1_, bf16[4,4,2,128,128]{4,3,2,1,0:T(8,128)(2,1)S(1)} %copy-done.1, ...), custom_call_target="tpu_custom_call" | custom-call | flops 3000000000 | bytes 4000000 | tf_op jit(solution)/shard_map/pallas_call | solution.py:398
  19.1 0.0 collective-permute-done.6.refs_8_
  19.2 0.0 collective-permute-done.5.refs_2_
  19.2 0.0 copy-start.6
  19.2 0.0 copy-start.7
  19.2 0.7 %copy-done.6 = f32[512]{0:T(512)S(1)} copy-done((f32[512]{0:T(512)S(1)}, f32[512]{0:T(512)}, u32[]{:S(2)}) %copy-start.6) | copy-done | bytes 2072
  19.9 1.5 %shard_map.109 = (f32[12,2,512]{2,1,0:T(2,128)}, f32[12,2,512]{2,1,0:T(2,128)}) custom-call(bf16[3,2,2,128,128]{4,3,2,1,0:T(8,128)(2,1)S(1)} %collective-permute-done.mine_ref, bf16[3,2,2,128,128]{4,3,2,1,0:T(8,128)(2,1)S(1)} %collective-permute-done.1.theirs_ref, bf16[2,8,24,128]{3,2,1,0:T(8,128)(2,1)S(1)} %collective-permute-done.3.held_ref.refs_0_, ...), custom_call_target="tpu_custom_call" | custom-call | flops 8000000000 | bytes 4000000 | tf_op jit(solution)/shard_map/pallas_call | solution.py:403
  (18 shorter events, 0.1 us)
Async XLA Ops:
  0.6 0.8 %copy-start.8 = (bf16[12,2,512]{2,1,0:T(2,128)(2,1)S(1)}, bf16[12,2,512]{2,1,0:T(2,128)(2,1)}, u32[]{:S(2)}) copy-start(bf16[12,2,512]{2,1,0:T(2,128)(2,1)} %param.14) | copy-start | bytes 73732
  1.5 5.1 %collective-permute-start.2 = (bf16[2,4,24,128]{3,2,1,0:T(8,128)(2,1)S(1)}, bf16[2,4,24,128]{3,2,1,0:T(8,128)(2,1)S(1)}, u32[]{:S(2)}, u32[]{:S(2)}) collective-permute-start(bf16[2,4,24,128]{3,2,1,0:T(8,128)(2,1)S(1)} %pad_maximum_fusion.after_ref.own_ref), channel_id=1, source_target_pairs={{0,2},{2,0},{1,3},{3,1},{4,6},{6,4},{5,7},{7,5},{8,10},{10,8},{9,1... | collective-permute-start | bytes 147464 | tf_op jit(solution)/shard_map/ppermute | solution.py:32
  4.5 1.2 %copy-start = (bf16[4,4,2,128,128]{4,3,2,1,0:T(8,128)(2,1)S(1)}, bf16[4,4,2,128,128]{4,3,2,1,0:T(8,128)(2,1)}, u32[]{:S(2)}) copy-start(bf16[4,4,2,128,128]{4,3,2,1,0:T(8,128)(2,1)} %refs_4_.1) | copy-start | bytes 3145732
  6.0 5.8 %copy-start.1 = (bf16[4,4,2,128,128]{4,3,2,1,0:T(8,128)(2,1)S(1)}, bf16[4,4,2,128,128]{4,3,2,1,0:T(8,128)(2,1)}, u32[]{:S(2)}) copy-start(bf16[4,4,2,128,128]{4,3,2,1,0:T(8,128)(2,1)} %refs_4_.1) | copy-start | bytes 3145732
  6.0 5.8 %copy-start.2 = (bf16[4,4,2,128,128]{4,3,2,1,0:T(8,128)(2,1)S(1)}, bf16[4,4,2,128,128]{4,3,2,1,0:T(8,128)(2,1)}, u32[]{:S(2)}) copy-start(bf16[4,4,2,128,128]{4,3,2,1,0:T(8,128)(2,1)} %refs_5_.1) | copy-start | bytes 3145732
  6.0 11.2 %collective-permute-start = (bf16[3,2,2,128,128]{4,3,2,1,0:T(8,128)(2,1)S(1)}, bf16[3,2,2,128,128]{4,3,2,1,0:T(8,128)(2,1)S(1)}, u32[]{:S(2)}, u32[]{:S(2)}) collective-permute-start(bf16[3,2,2,128,128]{4,3,2,1,0:T(8,128)(2,1)S(1)} %shard_map.104), channel_id=1, source_target_pairs={{0,2},{2,0},{1,3},{3,1},{4,6},{6,4},{5,7},{7,5},{8,10},{10,8},{9,1... | collective-permute-start | bytes 1179656 | tf_op jit(solution)/shard_map/ppermute | solution.py:32
  6.6 5.2 %copy-start.3 = (s32[4,4,2]{1,2,0:T(2,128)S(1)}, s32[4,4,2]{1,2,0:T(2,128)}, u32[]{:S(2)}) copy-start(s32[4,4,2]{1,2,0:T(2,128)} %param.10) | copy-start | bytes 388
  6.6 5.2 %copy-start.4 = (s32[4,4,2]{1,2,0:T(2,128)S(1)}, s32[4,4,2]{1,2,0:T(2,128)}, u32[]{:S(2)}) copy-start(s32[4,4,2]{1,2,0:T(2,128)} %param.12) | copy-start | bytes 388
  6.6 5.2 %copy-start.5 = (s32[2,512]{1,0:T(2,128)S(1)}, s32[2,512]{1,0:T(2,128)}, u32[]{:S(2)}) copy-start(s32[2,512]{1,0:T(2,128)} %ends_ref.1) | copy-start | bytes 12292
  6.6 10.7 %collective-permute-start.3 = (bf16[2,8,24,128]{3,2,1,0:T(8,128)(2,1)S(1)}, bf16[2,8,24,128]{3,2,1,0:T(8,128)(2,1)S(1)}, u32[]{:S(2)}, u32[]{:S(2)}) collective-permute-start(bf16[2,8,24,128]{3,2,1,0:T(8,128)(2,1)S(1)} %shard_map.105.held_ref.refs_10_), channel_id=1, source_target_pairs={{0,4},{4,8},{8,12},{12,0},{1,5},{5,9},{9,13},{13,1},{2,6},{6,10},{... | collective-permute-start | bytes 294920 | tf_op jit(solution)/shard_map/ppermute | solution.py:376
  8.7 10.4 %collective-permute-start.5 = (bf16[2,8,24,128]{3,2,1,0:T(8,128)(2,1)S(1)}, bf16[2,8,24,128]{3,2,1,0:T(8,128)(2,1)S(1)}, u32[]{:S(2)}, u32[]{:S(2)}) collective-permute-start(bf16[2,8,24,128]{3,2,1,0:T(8,128)(2,1)S(1)} %shard_map.105.held_ref.refs_10_), channel_id=1, source_target_pairs={{0,12},{4,0},{8,4},{12,8},{1,13},{5,1},{9,5},{13,9},{2,14},{6,2},{... | collective-permute-start | bytes 294920 | tf_op jit(solution)/shard_map/ppermute | solution.py:376
  10.8 8.0 %collective-permute-start.4 = (bf16[2,8,24,128]{3,2,1,0:T(8,128)(2,1)S(1)}, bf16[2,8,24,128]{3,2,1,0:T(8,128)(2,1)S(1)}, u32[]{:S(2)}, u32[]{:S(2)}) collective-permute-start(bf16[2,8,24,128]{3,2,1,0:T(8,128)(2,1)S(1)} %shard_map.105.held_ref.refs_10_), channel_id=1, source_target_pairs={{0,8},{4,12},{8,0},{12,4},{1,9},{5,13},{9,1},{13,5},{2,10},{6,14},... | collective-permute-start | bytes 294920 | tf_op jit(solution)/shard_map/ppermute | solution.py:376
  12.6 6.5 %collective-permute-start.6 = (bf16[9,24,128]{2,1,0:T(8,128)(2,1)S(1)}, bf16[9,24,128]{2,1,0:T(8,128)(2,1)S(1)}, u32[]{:S(2)}, u32[]{:S(2)}) collective-permute-start(bf16[9,24,128]{2,1,0:T(8,128)(2,1)S(1)} %get-tuple-element.20), channel_id=1, source_target_pairs={{0,2},{2,0},{1,3},{3,1},{4,6},{6,4},{5,7},{7,5},{8,10},{10,8},{9,1... | collective-permute-start | bytes 165896 | tf_op jit(solution)/shard_map/ppermute | solution.py:32
  17.2 1.9 %collective-permute-start.1 = (bf16[3,2,2,128,128]{4,3,2,1,0:T(8,128)(2,1)S(1)}, bf16[3,2,2,128,128]{4,3,2,1,0:T(8,128)(2,1)S(1)}, u32[]{:S(2)}, u32[]{:S(2)}) collective-permute-start(bf16[3,2,2,128,128]{4,3,2,1,0:T(8,128)(2,1)S(1)} %collective-permute-done.mine_ref), channel_id=1, source_target_pairs={{0,1},{1,0},{2,3},{3,2},{4,5},{5,4},{6,7},{7,6},{8,9},{9,8},{10,11... | collective-permute-start | bytes 1179656 | tf_op jit(solution)/shard_map/ppermute | solution.py:32
  19.2 0.7 %copy-start.6 = (f32[512]{0:T(512)S(1)}, f32[512]{0:T(512)}, u32[]{:S(2)}) copy-start(f32[512]{0:T(512)} %param.16) | copy-start | bytes 6148
  19.2 0.7 %copy-start.7 = (f32[12]{0:T(128)S(1)}, f32[12]{0:T(128)}, u32[]{:S(2)}) copy-start(f32[12]{0:T(128)} %param.15) | copy-start | bytes 148

commit v3 on v2

--- a/solution.py
+++ b/solution.py
@@ -13,6 +13,8 @@
 SMEM = pl.BlockSpec(memory_space=pltpu.SMEM)
 ANY = pl.BlockSpec(memory_space=pl.ANY)
 HBM = pl.BlockSpec(memory_space=pltpu.HBM)
+MAIN = 6_000_000
+STACK = 5_000_000
 JOIN = 10_000_000
 SEND = 1_000
 FIRST = 1_000
@@ -178,6 +180,11 @@
     return lax.rem(lax.axis_index("blk") + regions - shift, regions)
 
 
+def shift_order(regions):
+    order = list(range(1, regions))
+    return [2, 1, 3]
+
+
 def turned_rows(array):
     rows = array.shape[0]
     odd = lax.broadcasted_iota(jnp.int32, array.shape, 0) & 1
@@ -212,9 +219,27 @@
     )
 
 
+def outflow_kernel(message_ref, ends_ref, matrix_ref, outflow_ref, away_ref):
+    row_blocks, _, block_size = outflow_ref.shape
+    leaves, enters = ends_ref[0:1, :], ends_ref[1:2, :]
+    current = lanes([message_ref[1, block] for block in range(row_blocks)])
+    for block in range(2 * row_blocks):
+        side, at = divmod(block, row_blocks)
+        base = ((lax.axis_index("cell") ^ side) * row_blocks + at) * block_size
+        panel = lax.broadcasted_iota(jnp.int32, (block_size, ends_ref.shape[1]), 0) + base
+        entry = (leaves == panel).astype(jnp.float32) - (enters == panel).astype(jnp.float32)
+        entry = entry.astype(jnp.bfloat16)
+        matrix_ref[block] = entry
+        sums = lax.dot_general(current, entry, NT, preferred_element_type=jnp.float32)
+        if side == 0:
+            outflow_ref[at] = sums
+        else:
+            away_ref[at] = sums.astype(jnp.bfloat16)
+
+
 def first_kernel(
-    regions, held_ref, p_ref, l_ref, p_cols_ref, l_cols_ref, ends_ref,
-    table_ref, potential_ref, flux_ref, matrix_ref, outflow_ref, early_ref, numbers_ref,
+    regions, held_ref, p_ref, l_ref, p_cols_ref, l_cols_ref, omega_ref, resist_ref, away_ref,
+    factor_ref, table_ref, potential_ref, flux_ref, early_ref, numbers_ref,
 ):
     row_blocks, rows, block_size = potential_ref.shape
     slots = p_ref.shape[2]
@@ -236,24 +261,15 @@
     for row in range(row_blocks):
         numbers_ref[row * slots : (row + 1) * slots, :] = numbers[row]
     early_ref[2 * row_blocks] = numbers_ref[...].astype(jnp.bfloat16)
+    early_ref[row_blocks : 2 * row_blocks] = away_ref[...]
     for row in range(row_blocks):
         potential, flux = region_terms(0, table_ref, held_ref, p_ref, l_ref, back(regions, 0), row)
         potential_ref[row], flux_ref[row] = potential, flux
         early_ref[row] = potential.astype(jnp.bfloat16)
-    leaves, enters = ends_ref[0:1, :], ends_ref[1:2, :]
-    current = lanes([held_ref[1, block] for block in range(row_blocks)])
-    for block in range(2 * row_blocks):
-        side, at = divmod(block, row_blocks)
-        base = ((cell ^ side) * row_blocks + at) * block_size
-        panel = lax.broadcasted_iota(jnp.int32, (block_size, ends_ref.shape[1]), 0) + base
-        entry = (leaves == panel).astype(jnp.float32) - (enters == panel).astype(jnp.float32)
-        entry = entry.astype(jnp.bfloat16)
-        matrix_ref[block] = entry
-        sums = lax.dot_general(current, entry, NT, preferred_element_type=jnp.float32)
-        if side == 0:
-            outflow_ref[at] = sums
-        else:
-            early_ref[block] = sums.astype(jnp.bfloat16)
+    factor_ref[0] = jnp.broadcast_to(row_scale(omega_ref, rows), (rows, block_size))
+    for row in range(row_blocks):
+        columns = slice(row * block_size, (row + 1) * block_size)
+        factor_ref[1 + row] = jnp.broadcast_to(resist_ref[:, columns], (rows, block_size))
 
 
 def next_kernel(regions, shift, table_ref, held_ref, p_ref, l_ref, p_in_ref, f_in_ref, *refs):
@@ -264,20 +280,17 @@
         potential_ref[row], flux_ref[row] = p_in_ref[row] + potential, f_in_ref[row] + flux
 
 
-def send_kernel(regions, p_ref, after_ref, out_ref, sems):
+def stack_kernel(charge_ref, current_ref, out_ref):
+    out_ref[0] = charge_ref[...]
+    out_ref[1] = current_ref[...]
+
+
+def send_kernel(regions, p_ref, after_ref, out_ref):
     del after_ref
     half = out_ref.shape[1]
-    start = lax.axis_index("col") * half
-    copies = [
-        pltpu.make_async_copy(
-            p_ref.at[pl.ds(start, half), back(regions, shift)], out_ref.at[shift - 1], sems.at[shift - 1]
-        )
-        for shift in range(1, regions)
-    ]
-    for copy in copies:
-        copy.start()
-    for copy in copies:
-        copy.wait()
+    for at, shift in enumerate(shift_order(regions)):
+        for row in range(half):
+            out_ref[at, row] = p_ref[lax.axis_index("col") * half + row, back(regions, shift)]
 
 
 def join_kernel(own_ref, other_ref, out_ref):
@@ -292,47 +305,65 @@
         out_ref[freq, :, columns] = array[2 * freq : 2 * freq + 2]
 
 
-def last_kernel(regions, mine_ref, theirs_ref, *refs):
+def other_rows(order, part, slab_ref, numbers_ref, early_ref, piece_refs, other_ref):
+    half, slots = slab_ref.shape[1:3]
+    for position in range(half):
+        row = (lax.axis_index("col") ^ part) * half + position
+        total = early_ref[row].astype(jnp.float32)
+        for at, shift in enumerate(order):
+            total += pair_dot(
+                piece_refs[at].at[0],
+                [numbers_ref[row * slots + slot, shift] for slot in range(slots)],
+                [slab_ref[at, position, slot] for slot in range(slots)],
+            )
+        other_ref[row] = total.astype(jnp.bfloat16)
+
+
+def other_drop(part, half, other_ref, matrix_ref):
+    start = (lax.axis_index("col") ^ part) * half
+    rows = lanes([other_ref[start + position] for position in range(half)])
+    matrix = matrix_ref[pl.ds(2 * half + start, half)].reshape(rows.shape[1], -1)
+    return lax.dot_general(rows, matrix, NN, preferred_element_type=jnp.float32)
+
+
+def main_kernel(regions, *refs):
+    order = shift_order(regions)
     piece_refs = refs[: regions - 1]
-    (table_ref, p_ref, l_ref, p_in_ref, f_in_ref, early_ref, matrix_ref, held_ref, outflow_ref, omega_ref,
-     resist_ref, cell_ref, panel_ref, other_ref, numbers_ref) = refs[regions - 1 :]
-    row_blocks, rows, block_size = p_in_ref.shape
-    half = row_blocks // 2
-    slots = range(mine_ref.shape[2])
-    core = lax.axis_index("col")
+    (mine_ref, table_ref, p_ref, l_ref, p_in_ref, f_in_ref, early_ref, matrix_ref, held_ref, factor_ref,
+     out_ref, numbers_ref, other_ref) = refs[regions - 1 :]
+    row_blocks, _, block_size = p_in_ref.shape
     numbers_ref[...] = early_ref[2 * row_blocks].astype(jnp.float32).astype(jnp.int32)
     potentials, fluxes = [], []
     for row in range(row_blocks):
         potential, flux = p_in_ref[row], f_in_ref[row]
-        if regions > 1:
-            shift = regions - 1
-            terms = region_terms(shift, table_ref, piece_refs[-1], p_ref, l_ref, back(regions, shift), row)
+        for shift, piece_ref in list(zip(order, piece_refs))[1:]:
+            terms = region_terms(shift, table_ref, piece_ref, p_ref, l_ref, back(regions, shift), row)
             potential, flux = potential + terms[0], flux + terms[1]
         potentials.append(potential.astype(jnp.bfloat16))
         fluxes.append(flux)
-    for part, slab_ref in enumerate((mine_ref, theirs_ref)):
-        for position in range(half):
-            row = (core ^ part) * half + position
-            total = early_ref[row].astype(jnp.float32)
-            for shift in range(1, regions):
-                total += pair_dot(
-                    piece_refs[shift - 1].at[0],
-                    [numbers_ref[row * len(slots) + slot, shift] for slot in slots],
-                    [slab_ref[shift - 1, position, slot] for slot in slots],
-                )
-            other_ref[row] = total.astype(jnp.bfloat16)
-    matrix = matrix_ref[...].reshape(2, row_blocks * block_size, -1)
-    drop = lax.dot_general(lanes(potentials), matrix[0], NN, preferred_element_type=jnp.float32)
-    others = lanes([other_ref[row] for row in range(row_blocks)])
-    drop += lax.dot_general(others, matrix[1], NN, preferred_element_type=jnp.float32)
-    scale = row_scale(omega_ref, rows)
+    other_rows(order, 0, mine_ref, numbers_ref, early_ref, piece_refs, other_ref)
+    matrix = matrix_ref[:row_blocks].reshape(row_blocks * block_size, -1)
+    drop = lax.dot_general(lanes(potentials), matrix, NN, preferred_element_type=jnp.float32)
+    drop += other_drop(0, row_blocks // 2, other_ref, matrix_ref)
     for row in range(row_blocks):
         columns = slice(row * block_size, (row + 1) * block_size)
         current = held_ref[1, row].astype(jnp.float32)
-        flux = scale * turned_rows(fluxes[row])
-        store_rows(cell_ref, columns, resist_ref[:, columns] * current + flux + drop[:, columns])
+        flux = factor_ref[0] * turned_rows(fluxes[row])
+        out_ref[:, columns] = factor_ref[1 + row] * current + flux + drop[:, columns]
+
+
+def last_kernel(regions, *refs):
+    piece_refs = refs[: regions - 1]
+    (theirs_ref, numbers_ref, begun_ref, early_ref, matrix_ref, held_ref, outflow_ref, factor_ref,
+     cell_ref, panel_ref, other_ref) = refs[regions - 1 :]
+    row_blocks, _, block_size = outflow_ref.shape
+    other_rows(shift_order(regions), 1, theirs_ref, numbers_ref, early_ref, piece_refs, other_ref)
+    total = begun_ref[...] + other_drop(1, row_blocks // 2, other_ref, matrix_ref)
+    for row in range(row_blocks):
+        columns = slice(row * block_size, (row + 1) * block_size)
+        store_rows(cell_ref, columns, total[:, columns])
         outflow = outflow_ref[row] + early_ref[row_blocks + row].astype(jnp.float32)
-        charge = scale * turned_rows(held_ref[0, row].astype(jnp.float32))
+        charge = factor_ref[0] * turned_rows(held_ref[0, row].astype(jnp.float32))
         store_rows(panel_ref, columns, outflow + charge)
 
 
@@ -355,61 +386,72 @@
     row_blocks = p_blocks.shape[0]
     rows = 2 * freq_count
     regions = lax.axis_size("blk")
+    order = shift_order(regions)
 
     def blocked(array):
         return array.reshape(rows, row_blocks, block_size).transpose(1, 0, 2)
 
-    message = jnp.stack([blocked(charges), blocked(currents)])
-    got = swapped(message, "cell", 1)
+    message = kernel_call(
+        stack_kernel, jax.ShapeDtypeStruct((2, row_blocks, rows, block_size), jnp.bfloat16), "vv", STACK
+    )(blocked(charges), blocked(currents))
     held = kernel_call(
         join_kernel, jax.ShapeDtypeStruct((2, 2 * row_blocks, rows, block_size), jnp.bfloat16), "vv", JOIN
-    )(message, got)
-
+    )(message, swapped(message, "cell", 1))
+
+    totals = jax.ShapeDtypeStruct((row_blocks, rows, block_size), jnp.float32)
+    matrix, outflow, away = kernel_call(
+        outflow_kernel,
+        (
+            jax.ShapeDtypeStruct((2 * row_blocks, block_size, share), jnp.bfloat16),
+            totals,
+            jax.ShapeDtypeStruct((row_blocks, rows, block_size), jnp.bfloat16),
+        ),
+        "vv",
+        SEND,
+    )(message, branch_ends)
     half_shape = jax.ShapeDtypeStruct((regions - 1, row_blocks // 2) + p_blocks.shape[2:], jnp.bfloat16)
-    sent = kernel_call(
-        functools.partial(send_kernel, regions), half_shape, "ha", SEND, [pltpu.SemaphoreType.DMA((regions - 1,))]
-    )(p_blocks, message)
+    sent = kernel_call(functools.partial(send_kernel, regions), half_shape, "va", SEND)(p_blocks, outflow)
     mine = swapped(sent, "cell", 1)
     theirs = swapped(mine, "col", 1)
 
     pieces = [
         lax.ppermute(held, "blk", [(i, (i + shift) % regions) for i in range(regions)])
-        for shift in range(1, regions)
+        for shift in order
     ]
 
     slots = p_cols.shape[2]
-    totals = jax.ShapeDtypeStruct((row_blocks, rows, block_size), jnp.float32)
-    table, potential, flux, matrix, outflow, early = kernel_call(
+    factors, table, potential, flux, early = kernel_call(
         functools.partial(first_kernel, regions),
         (
+            jax.ShapeDtypeStruct((1 + row_blocks, rows, block_size), jnp.float32),
             jax.ShapeDtypeStruct((2, regions, row_blocks, slots, block_size), jnp.int32),
             totals,
             totals,
-            jax.ShapeDtypeStruct((2 * row_blocks, block_size, share), jnp.bfloat16),
-            totals,
             jax.ShapeDtypeStruct((2 * row_blocks + 1, rows, block_size), jnp.bfloat16),
         ),
-        "vvvvvv",
+        "vvvvvvvv",
         FIRST,
         [pltpu.VMEM((rows, block_size), jnp.float32)],
-    )(held, p_blocks, l_blocks, p_cols.transpose(0, 2, 1), l_cols.transpose(0, 2, 1), branch_ends)
+    )(held, p_blocks, l_blocks, p_cols.transpose(0, 2, 1), l_cols.transpose(0, 2, 1), omegas[None], resist[None], away)
     early = swapped(early, "cell", 1)
-    for shift in range(1, regions - 1):
+    for shift, piece in list(zip(order, pieces))[:1]:
         potential, flux = kernel_call(
             functools.partial(next_kernel, regions, shift), (totals, totals), "vvvvvvv", NEXT
-        )(table, pieces[shift - 1], p_blocks, l_blocks, potential, flux, matrix)
-
+        )(table, piece, p_blocks, l_blocks, potential, flux, matrix)
+
+    numbers_shape = jax.ShapeDtypeStruct((rows, block_size), jnp.int32)
+    other_scratch = pltpu.VMEM((row_blocks, rows, block_size), jnp.bfloat16)
+    begun, numbers = kernel_call(
+        functools.partial(main_kernel, regions),
+        (jax.ShapeDtypeStruct((rows, share), jnp.float32), numbers_shape),
+        "v" * (9 + regions),
+        MAIN,
+        [other_scratch],
+    )(*pieces, mine, table, p_blocks, l_blocks, potential, flux, early, matrix, held, factors)
     result = jax.ShapeDtypeStruct(charges.shape, jnp.float32)
     return kernel_call(
-        functools.partial(last_kernel, regions),
-        (result, result),
-        "v" * (12 + regions),
-        LAST,
-        [pltpu.VMEM((row_blocks, rows, block_size), jnp.bfloat16), pltpu.VMEM((rows, block_size), jnp.int32)],
-    )(
-        mine, theirs, *pieces, table, p_blocks, l_blocks, potential, flux, early, matrix, held, outflow,
-        omegas[None], resist[None],
-    )
+        functools.partial(last_kernel, regions), (result, result), "v" * (7 + regions), LAST, [other_scratch]
+    )(*pieces, theirs, numbers, begun, early, matrix, held, outflow, factors)
 
 
 def per_device(*args):

time: 21.6 us -> 19.8 us (0.917)
  waiting for transfers between devices: 4.86 us -> 3.38 us
  local copies, waits for them, and re-layouts: 2.72 us -> 1.51 us
  starting transfers between devices: 9.83 us -> 10.7 us
    pallas_call x1 -> x4, Pallas kernels: 0.27 us -> 1.49 us  [the longest x1 0.83 us: paired_step(): kernel_call(functools.partial(main_kernel, regions), (jax.ShapeDtypeStruc...]
    unnamed x18 -> x16, local copies, waits for them, and re-layouts: 1.92 us -> 0.72 us
    ppermute x4, waiting for transfers between devices: 3.54 us -> 2.6 us  [swapped(): lax.ppermute(array, axis, [(i, i ^ distance) for i in range(lax.axis_size...]
    ppermute x4, starting transfers between devices: 4.63 us -> 5.51 us  [swapped(): lax.ppermute(array, axis, [(i, i ^ distance) for i in range(lax.axis_size...]
    ppermute x3, waiting for transfers between devices: 1.32 us -> 0.78 us  [paired_step(): lax.ppermute(held, 'blk', [(i, (i + shift) % regions) for i in range(regi...]
    pallas_call x1, Pallas kernels: 0.83 us -> 0.36 us  [paired_step(): kernel_call(functools.partial(first_kernel, regions), (jax.ShapeDtypeStru...]
    pallas_call x1, Pallas kernels: 1.47 us -> 1.08 us  [paired_step(): kernel_call(functools.partial(last_kernel, regions), (result, result), 'v...]
    pallas_call x2 -> x1, Pallas kernels: 0.58 us -> 0.29 us  [paired_step(): kernel_call(functools.partial(next_kernel, regions, shift), (totals, tota...]
  transfers between devices with their start and end apart: 7 -> 7, of which waited for: 3 -> 5; matrix products, arithmetic and copies ran while one was open for 0% -> 0% of each run, Pallas kernels for 8% -> 11%
where the time goes in v3:
time: 19.8 us; the launch traced here: 19.6 us
  starting transfers between devices  10.7 us (54%)
  waiting for transfers between devices  3.38 us (17%)
  Pallas kernels  3.23 us (16%)
  local copies, waits for them, and re-layouts  1.51 us (8%)
  between operations  0.74 us (4%)
    ppermute x4, starting transfers between devices, swapped(): lax.ppermute(array, axis, [(i, i ^ distance) for i in range(lax.axis_size...  5.51 us
    ppermute x3, starting transfers between devices, paired_step(): lax.ppermute(held, 'blk', [(i, (i + shift) % regions) for i in range(regi...  5.21 us
    ppermute x4, waiting for transfers between devices, swapped(): lax.ppermute(array, axis, [(i, i ^ distance) for i in range(lax.axis_size...  2.6 us
    pallas_call x1, Pallas kernels, paired_step(): kernel_call(functools.partial(last_kernel, regions), (result, result), 'v...  1.08 us
    pallas_call x1, Pallas kernels, paired_step(): kernel_call(functools.partial(main_kernel, regions), (jax.ShapeDtypeStruc...  0.83 us
    reshape x2, local copies, waits for them, and re-layouts, blocked(): return array.reshape(rows, row_blocks, block_size).transpose(1, 0, 2)  0.79 us
    ppermute x3, waiting for transfers between devices, paired_step(): lax.ppermute(held, 'blk', [(i, (i + shift) % regions) for i in range(regi...  0.78 us
    unnamed x16, local copies, waits for them, and re-layouts  0.72 us
  transfers between devices with their start and end apart: 7, of which 5 were waited for; matrix products, arithmetic and copies ran while one was open for 0% of the time, Pallas kernels for 11%

profile of v3, /device:TPU:0, one launch (start us, length us, event | category | flops | bytes accessed | tf_op | source)
XLA Modules:
  0.0 19.6 jit_solution(16583115240773998474)
XLA Ops:
  0.6 0.8 %reshape.10 = bf16[24,4,128]{2,1,0:T(4,128)(2,1)S(1)} reshape(bf16[12,2,512]{2,1,0:T(2,128)(2,1)} %param.13) | data formatting | bytes 49152 | tf_op jit(solution)/shard_map/reshape | solution.py:392
  1.5 0.0 copy-start.4
  1.5 0.0 copy-start
  1.5 3.0 %collective-permute-start = (bf16[2,4,24,128]{3,2,1,0:T(8,128)(2,1)S(1)}, bf16[2,4,24,128]{3,2,1,0:T(8,128)(2,1)S(1)}, u32[]{:S(2)}, u32[]{:S(2)}) collective-permute-start(bf16[2,4,24,128]{3,2,1,0:T(8,128)(2,1)S(1)} %shard_map.104.own_ref.message_ref), channel_id=1, source_target_pairs={{0,2},{2,0},{1,3},{3,1},{4,6},{6,4},{5,7},{7,5},{8,10},{10,8},{9,1... | collective-permute-start | bytes 147464 | tf_op jit(solution)/shard_map/ppermute | solution.py:34
  4.5 0.6 %shard_map.106 = (bf16[8,128,512]{2,1,0:T(8,128)(2,1)S(1)}, f32[4,24,128]{2,1,0:T(8,128)S(1)}, bf16[4,24,128]{2,1,0:T(8,128)(2,1)S(1)}) custom-call(bf16[2,4,24,128]{3,2,1,0:T(8,128)(2,1)S(1)} %shard_map.104.own_ref.message_ref, s32[2,512]{1,0:T(2,128)S(1)} %copy-done.4), custom_call_target="tpu_custom_call" | custom-call | flops 1000000 | bytes 4000000 | tf_op jit(solution)/shard_map/pallas_call | solution.py:402
  5.1 0.0 copy-done
  5.2 0.0 copy-start.1
  5.2 0.6 %collective-permute-start.4 = (bf16[3,2,2,128,128]{4,3,2,1,0:T(8,128)(2,1)S(1)}, bf16[3,2,2,128,128]{4,3,2,1,0:T(8,128)(2,1)S(1)}, u32[]{:S(2)}, u32[]{:S(2)}) collective-permute-start(bf16[3,2,2,128,128]{4,3,2,1,0:T(8,128)(2,1)S(1)} %shard_map.107), channel_id=1, source_target_pairs={{0,2},{2,0},{1,3},{3,1},{4,6},{6,4},{5,7},{7,5},{8,10},{10,8},{9,1... | collective-permute-start | bytes 1179656 | tf_op jit(solution)/shard_map/ppermute | solution.py:34
  5.8 0.7 %collective-permute-done.other_ref = bf16[2,4,24,128]{3,2,1,0:T(8,128)(2,1)S(1)} collective-permute-done((bf16[2,4,24,128]{3,2,1,0:T(8,128)(2,1)S(1)}, bf16[2,4,24,128]{3,2,1,0:T(8,128)(2,1)S(1)}, u32[]{:S(2)}, u32[]{:S(2)}) %collective-permute-start) | collective-permute-done | bytes 49184 | tf_op jit(solution)/shard_map/ppermute | solution.py:34
  6.6 3.2 %collective-permute-start.1 = (bf16[2,8,24,128]{3,2,1,0:T(8,128)(2,1)S(1)}, bf16[2,8,24,128]{3,2,1,0:T(8,128)(2,1)S(1)}, u32[]{:S(2)}, u32[]{:S(2)}) collective-permute-start(bf16[2,8,24,128]{3,2,1,0:T(8,128)(2,1)S(1)} %shard_map.105.held_ref.refs_11_.refs_8_), channel_id=1, source_target_pairs={{0,8},{4,12},{8,0},{12,4},{1,9},{5,13},{9,1},{13,5},{2,10},{6,14},... | collective-permute-start | bytes 294920 | tf_op jit(solution)/shard_map/ppermute | solution.py:418
  9.8 1.3 %collective-permute-start.3 = (bf16[2,8,24,128]{3,2,1,0:T(8,128)(2,1)S(1)}, bf16[2,8,24,128]{3,2,1,0:T(8,128)(2,1)S(1)}, u32[]{:S(2)}, u32[]{:S(2)}) collective-permute-start(bf16[2,8,24,128]{3,2,1,0:T(8,128)(2,1)S(1)} %shard_map.105.held_ref.refs_11_.refs_8_), channel_id=1, source_target_pairs={{0,12},{4,0},{8,4},{12,8},{1,13},{5,1},{9,5},{13,9},{2,14},{6,2},{... | collective-permute-start | bytes 294920 | tf_op jit(solution)/shard_map/ppermute | solution.py:418
  11.1 0.7 %collective-permute-start.2 = (bf16[2,8,24,128]{3,2,1,0:T(8,128)(2,1)S(1)}, bf16[2,8,24,128]{3,2,1,0:T(8,128)(2,1)S(1)}, u32[]{:S(2)}, u32[]{:S(2)}) collective-permute-start(bf16[2,8,24,128]{3,2,1,0:T(8,128)(2,1)S(1)} %shard_map.105.held_ref.refs_11_.refs_8_), channel_id=1, source_target_pairs={{0,4},{4,8},{8,12},{12,0},{1,5},{5,9},{9,13},{13,1},{2,6},{6,10},{... | collective-permute-start | bytes 294920 | tf_op jit(solution)/shard_map/ppermute | solution.py:418
  11.8 0.7 %copy-done.3 = s32[4,4,2]{1,2,0:T(2,128)S(1)} copy-done((s32[4,4,2]{1,2,0:T(2,128)S(1)}, s32[4,4,2]{1,2,0:T(2,128)}, u32[]{:S(2)}) %copy-start.3) | copy-done | bytes 152
  12.5 0.0 copy-done.2
  12.5 0.4 %shard_map.108 = (f32[5,24,128]{2,1,0:T(8,128)S(1)}, s32[2,4,4,2,128]{4,3,2,1,0:T(2,128)S(1)}, f32[4,24,128]{2,1,0:T(8,128)S(1)}, f32[4,24,128]{2,1,0:T(8,128)S(1)}, bf16[9,24,128]{2,1,0:T(8,128)(2,1)S(1)}) custom-call(bf16[2,8,24,128]{3,2,1,0:T(8,128)(2,1)S(1)} %shard_map.105.held_ref.refs_11_.refs_8_, bf16[4,4,2,128,128]{4,3,2,1,0:T(8,128)(2,1)S(1)} %copy-done, ...), custom_call_target="tpu_custom_call" | custom-call | flops 1000000 | bytes 4000000 | tf_op jit(solution)/shard_map/pallas_call | solution.py:423
  12.9 1.9 %collective-permute-start.6 = (bf16[9,24,128]{2,1,0:T(8,128)(2,1)S(1)}, bf16[9,24,128]{2,1,0:T(8,128)(2,1)S(1)}, u32[]{:S(2)}, u32[]{:S(2)}) collective-permute-start(bf16[9,24,128]{2,1,0:T(8,128)(2,1)S(1)} %get-tuple-element.22), channel_id=1, source_target_pairs={{0,2},{2,0},{1,3},{3,1},{4,6},{6,4},{5,7},{7,5},{8,10},{10,8},{9,1... | collective-permute-start | bytes 165896 | tf_op jit(solution)/shard_map/ppermute | solution.py:34
  14.7 0.2 %collective-permute-done.1.held_ref.refs_0_ = bf16[2,8,24,128]{3,2,1,0:T(8,128)(2,1)S(1)} collective-permute-done((bf16[2,8,24,128]{3,2,1,0:T(8,128)(2,1)S(1)}, bf16[2,8,24,128]{3,2,1,0:T(8,128)(2,1)S(1)}, u32[]{:S(2)}, u32[]{:S(2)}) %collective-permute-start.1) | collective-permute-done | bytes 98336 | tf_op jit(solution)/shard_map/ppermute | solution.py:418
  14.9 0.3 %shard_map.109 = (f32[4,24,128]{2,1,0:T(8,128)S(1)}, f32[4,24,128]{2,1,0:T(8,128)S(1)}) custom-call(s32[2,4,4,2,128]{4,3,2,1,0:T(2,128)S(1)} %get-tuple-element.16.table_ref.refs_4_, bf16[2,8,24,128]{3,2,1,0:T(8,128)(2,1)S(1)} %collective-permute-done.1.held_ref.refs_0_, bf16[4,4,2,128,128]{4,3,2,1,0:T(8,128)(2,1)S(1)} %copy-done, ...), custom_call_target="tpu_custom_call" | custom-call | flops 3000000000 | bytes 4000000 | tf_op jit(solution)/shard_map/pallas_call | solution.py:438
  15.2 1.2 %collective-permute-done.4.refs_3_ = bf16[3,2,2,128,128]{4,3,2,1,0:T(8,128)(2,1)S(1)} collective-permute-done((bf16[3,2,2,128,128]{4,3,2,1,0:T(8,128)(2,1)S(1)}, bf16[3,2,2,128,128]{4,3,2,1,0:T(8,128)(2,1)S(1)}, u32[]{:S(2)}, u32[]{:S(2)}) %collective-permute-start.4) | collective-permute-done | bytes 393248 | tf_op jit(solution)/shard_map/ppermute | solution.py:34
  16.4 0.6 %collective-permute-done.6.refs_9_.refs_6_ = bf16[9,24,128]{2,1,0:T(8,128)(2,1)S(1)} collective-permute-done((bf16[9,24,128]{2,1,0:T(8,128)(2,1)S(1)}, bf16[9,24,128]{2,1,0:T(8,128)(2,1)S(1)}, u32[]{:S(2)}, u32[]{:S(2)}) %collective-permute-start.6) | collective-permute-done | bytes 55328 | tf_op jit(solution)/shard_map/ppermute | solution.py:34
  17.1 0.6 %collective-permute-done.2.refs_1_ = bf16[2,8,24,128]{3,2,1,0:T(8,128)(2,1)S(1)} collective-permute-done((bf16[2,8,24,128]{3,2,1,0:T(8,128)(2,1)S(1)}, bf16[2,8,24,128]{3,2,1,0:T(8,128)(2,1)S(1)}, u32[]{:S(2)}, u32[]{:S(2)}) %collective-permute-start.2) | collective-permute-done | bytes 98336 | tf_op jit(solution)/shard_map/ppermute | solution.py:418
  17.6 0.8 %shard_map.110 = (f32[24,512]{1,0:T(8,128)S(1)}, s32[24,128]{1,0:T(8,128)S(1)}) custom-call(bf16[2,8,24,128]{3,2,1,0:T(8,128)(2,1)S(1)} %collective-permute-done.1.held_ref.refs_0_, bf16[2,8,24,128]{3,2,1,0:T(8,128)(2,1)S(1)} %collective-permute-done.2.refs_1_, bf16[2,8,24,128]{3,2,1,0:T(8,128)(2,1)S(1)} %collective-permute-done.3.refs_2_, ...), custom_call_target="tpu_custom_call" | custom-call | flops 6000000000 | bytes 4000000 | tf_op jit(solution)/shard_map/pallas_call | solution.py:444
  18.5 0.0 collective-permute-done.5.refs_3_
  18.5 1.1 %shard_map.111 = (f32[12,2,512]{2,1,0:T(2,128)}, f32[12,2,512]{2,1,0:T(2,128)}) custom-call(bf16[2,8,24,128]{3,2,1,0:T(8,128)(2,1)S(1)} %collective-permute-done.1.held_ref.refs_0_, bf16[2,8,24,128]{3,2,1,0:T(8,128)(2,1)S(1)} %collective-permute-done.2.refs_1_, bf16[2,8,24,128]{3,2,1,0:T(8,128)(2,1)S(1)} %collective-permute-done.3.refs_2_, ...), custom_call_target="tpu_custom_call" | custom-call | flops 8000000000 | bytes 4000000 | tf_op jit(solution)/shard_map/pallas_call | solution.py:452
  (17 shorter events, 0.1 us)
Async XLA Ops:
  0.6 0.8 %copy-start.7 = (bf16[12,2,512]{2,1,0:T(2,128)(2,1)S(1)}, bf16[12,2,512]{2,1,0:T(2,128)(2,1)}, u32[]{:S(2)}) copy-start(bf16[12,2,512]{2,1,0:T(2,128)(2,1)} %param.14) | copy-start | bytes 73732
  1.5 3.0 %copy-start.4 = (s32[2,512]{1,0:T(2,128)S(1)}, s32[2,512]{1,0:T(2,128)}, u32[]{:S(2)}) copy-start(s32[2,512]{1,0:T(2,128)} %ends_ref.1) | copy-start | bytes 12292
  1.5 3.6 %copy-start = (bf16[4,4,2,128,128]{4,3,2,1,0:T(8,128)(2,1)S(1)}, bf16[4,4,2,128,128]{4,3,2,1,0:T(8,128)(2,1)}, u32[]{:S(2)}) copy-start(bf16[4,4,2,128,128]{4,3,2,1,0:T(8,128)(2,1)} %refs_5_.1) | copy-start | bytes 3145732
  1.5 5.1 %collective-permute-start = (bf16[2,4,24,128]{3,2,1,0:T(8,128)(2,1)S(1)}, bf16[2,4,24,128]{3,2,1,0:T(8,128)(2,1)S(1)}, u32[]{:S(2)}, u32[]{:S(2)}) collective-permute-start(bf16[2,4,24,128]{3,2,1,0:T(8,128)(2,1)S(1)} %shard_map.104.own_ref.message_ref), channel_id=1, source_target_pairs={{0,2},{2,0},{1,3},{3,1},{4,6},{6,4},{5,7},{7,5},{8,10},{10,8},{9,1... | collective-permute-start | bytes 147464 | tf_op jit(solution)/shard_map/ppermute | solution.py:34
  5.2 6.6 %copy-start.1 = (bf16[4,4,2,128,128]{4,3,2,1,0:T(8,128)(2,1)S(1)}, bf16[4,4,2,128,128]{4,3,2,1,0:T(8,128)(2,1)}, u32[]{:S(2)}) copy-start(bf16[4,4,2,128,128]{4,3,2,1,0:T(8,128)(2,1)} %refs_6_.1) | copy-start | bytes 3145732
  5.2 11.2 %collective-permute-start.4 = (bf16[3,2,2,128,128]{4,3,2,1,0:T(8,128)(2,1)S(1)}, bf16[3,2,2,128,128]{4,3,2,1,0:T(8,128)(2,1)S(1)}, u32[]{:S(2)}, u32[]{:S(2)}) collective-permute-start(bf16[3,2,2,128,128]{4,3,2,1,0:T(8,128)(2,1)S(1)} %shard_map.107), channel_id=1, source_target_pairs={{0,2},{2,0},{1,3},{3,1},{4,6},{6,4},{5,7},{7,5},{8,10},{10,8},{9,1... | collective-permute-start | bytes 1179656 | tf_op jit(solution)/shard_map/ppermute | solution.py:34
  6.6 5.2 %copy-start.5 = (f32[512]{0:T(512)S(1)}, f32[512]{0:T(512)}, u32[]{:S(2)}) copy-start(f32[512]{0:T(512)} %param.16) | copy-start | bytes 6148
  6.6 8.3 %collective-permute-start.1 = (bf16[2,8,24,128]{3,2,1,0:T(8,128)(2,1)S(1)}, bf16[2,8,24,128]{3,2,1,0:T(8,128)(2,1)S(1)}, u32[]{:S(2)}, u32[]{:S(2)}) collective-permute-start(bf16[2,8,24,128]{3,2,1,0:T(8,128)(2,1)S(1)} %shard_map.105.held_ref.refs_11_.refs_8_), channel_id=1, source_target_pairs={{0,8},{4,12},{8,0},{12,4},{1,9},{5,13},{9,1},{13,5},{2,10},{6,14},... | collective-permute-start | bytes 294920 | tf_op jit(solution)/shard_map/ppermute | solution.py:418
  9.8 7.3 %collective-permute-start.3 = (bf16[2,8,24,128]{3,2,1,0:T(8,128)(2,1)S(1)}, bf16[2,8,24,128]{3,2,1,0:T(8,128)(2,1)S(1)}, u32[]{:S(2)}, u32[]{:S(2)}) collective-permute-start(bf16[2,8,24,128]{3,2,1,0:T(8,128)(2,1)S(1)} %shard_map.105.held_ref.refs_11_.refs_8_), channel_id=1, source_target_pairs={{0,12},{4,0},{8,4},{12,8},{1,13},{5,1},{9,5},{13,9},{2,14},{6,2},{... | collective-permute-start | bytes 294920 | tf_op jit(solution)/shard_map/ppermute | solution.py:418
  11.1 6.5 %collective-permute-start.2 = (bf16[2,8,24,128]{3,2,1,0:T(8,128)(2,1)S(1)}, bf16[2,8,24,128]{3,2,1,0:T(8,128)(2,1)S(1)}, u32[]{:S(2)}, u32[]{:S(2)}) collective-permute-start(bf16[2,8,24,128]{3,2,1,0:T(8,128)(2,1)S(1)} %shard_map.105.held_ref.refs_11_.refs_8_), channel_id=1, source_target_pairs={{0,4},{4,8},{8,12},{12,0},{1,5},{5,9},{9,13},{13,1},{2,6},{6,10},{... | collective-permute-start | bytes 294920 | tf_op jit(solution)/shard_map/ppermute | solution.py:418
  11.8 0.7 %copy-start.3 = (s32[4,4,2]{1,2,0:T(2,128)S(1)}, s32[4,4,2]{1,2,0:T(2,128)}, u32[]{:S(2)}) copy-start(s32[4,4,2]{1,2,0:T(2,128)} %param.12) | copy-start | bytes 388
  11.8 0.7 %copy-start.2 = (s32[4,4,2]{1,2,0:T(2,128)S(1)}, s32[4,4,2]{1,2,0:T(2,128)}, u32[]{:S(2)}) copy-start(s32[4,4,2]{1,2,0:T(2,128)} %param.10) | copy-start | bytes 388
  11.8 0.7 %copy-start.6 = (f32[12]{0:T(128)S(1)}, f32[12]{0:T(128)}, u32[]{:S(2)}) copy-start(f32[12]{0:T(128)} %param.15) | copy-start | bytes 148
  12.9 4.2 %collective-permute-start.6 = (bf16[9,24,128]{2,1,0:T(8,128)(2,1)S(1)}, bf16[9,24,128]{2,1,0:T(8,128)(2,1)S(1)}, u32[]{:S(2)}, u32[]{:S(2)}) collective-permute-start(bf16[9,24,128]{2,1,0:T(8,128)(2,1)S(1)} %get-tuple-element.22), channel_id=1, source_target_pairs={{0,2},{2,0},{1,3},{3,1},{4,6},{6,4},{5,7},{7,5},{8,10},{10,8},{9,1... | collective-permute-start | bytes 165896 | tf_op jit(solution)/shard_map/ppermute | solution.py:34
  16.4 2.1 %collective-permute-start.5 = (bf16[3,2,2,128,128]{4,3,2,1,0:T(8,128)(2,1)S(1)}, bf16[3,2,2,128,128]{4,3,2,1,0:T(8,128)(2,1)S(1)}, u32[]{:S(2)}, u32[]{:S(2)}) collective-permute-start(bf16[3,2,2,128,128]{4,3,2,1,0:T(8,128)(2,1)S(1)} %collective-permute-done.4.refs_3_), channel_id=1, source_target_pairs={{0,1},{1,0},{2,3},{3,2},{4,5},{5,4},{6,7},{7,6},{8,9},{9,8},{10,11... | collective-permute-start | bytes 1179656 | tf_op jit(solution)/shard_map/ppermute | solution.py:34

commit v4 on v3

--- a/solution.py
+++ b/solution.py
@@ -13,7 +13,7 @@
 SMEM = pl.BlockSpec(memory_space=pltpu.SMEM)
 ANY = pl.BlockSpec(memory_space=pl.ANY)
 HBM = pl.BlockSpec(memory_space=pltpu.HBM)
-MAIN = 6_000_000
+MAIN = 3_000_000
 STACK = 5_000_000
 JOIN = 10_000_000
 SEND = 1_000
@@ -176,13 +176,22 @@
     return (cell_rows.reshape(freq_count, 2, share), panel_rows.reshape(freq_count, 2, share))
 
 
-def back(regions, shift):
-    return lax.rem(lax.axis_index("blk") + regions - shift, regions)
+def back(regions, move):
+    own = lax.axis_index("blk")
+    if move == 0:
+        return own
+    targets = region_moves(regions)[move - 1]
+    return sum(jnp.where(own == target, source, 0) for source, target in enumerate(targets))
+
+
+def region_moves(regions):
+    if regions == 4:
+        return [[2, 3, 0, 1], [1, 0, 3, 2], [3, 2, 1, 0]]
+    return [[(place + shift) % regions for place in range(regions)] for shift in range(1, regions)]
 
 
 def shift_order(regions):
-    order = list(range(1, regions))
-    return [2, 1, 3]
+    return list(range(1, regions))
 
 
 def turned_rows(array):
@@ -415,8 +424,7 @@
     theirs = swapped(mine, "col", 1)
 
     pieces = [
-        lax.ppermute(held, "blk", [(i, (i + shift) % regions) for i in range(regions)])
-        for shift in order
+        lax.ppermute(held, "blk", list(enumerate(targets))) for targets in region_moves(regions)
     ]
 
     slots = p_cols.shape[2]

time: 19.8 us -> 19.4 us (0.980)
  starting transfers between devices: 10.7 us -> 10.3 us
    ppermute x4, waiting for transfers between devices: 2.6 us -> 3.43 us  [swapped(): lax.ppermute(array, axis, [(i, i ^ distance) for i in range(lax.axis_size...]
    ppermute x3, waiting for transfers between devices: 0.78 us -> 0.06 us  [paired_step(): lax.ppermute(held, 'blk', list(enumerate(targets)))]
    ppermute x3, starting transfers between devices: 5.21 us -> 4.76 us  [paired_step(): lax.ppermute(held, 'blk', list(enumerate(targets)))]
where the time goes in v4:
time: 19.4 us; the launch traced here: 19.2 us
  starting transfers between devices  10.3 us (53%)
  waiting for transfers between devices  3.49 us (18%)
  Pallas kernels  3.22 us (17%)
  local copies, waits for them, and re-layouts  1.51 us (8%)
  between operations  0.73 us (4%)
    ppermute x4, starting transfers between devices, swapped(): lax.ppermute(array, axis, [(i, i ^ distance) for i in range(lax.axis_size...  5.51 us
    ppermute x3, starting transfers between devices, paired_step(): lax.ppermute(held, 'blk', list(enumerate(targets)))  4.76 us
    ppermute x4, waiting for transfers between devices, swapped(): lax.ppermute(array, axis, [(i, i ^ distance) for i in range(lax.axis_size...  3.43 us
    pallas_call x1, Pallas kernels, paired_step(): kernel_call(functools.partial(last_kernel, regions), (result, result), 'v...  1.07 us
    pallas_call x1, Pallas kernels, paired_step(): kernel_call(functools.partial(main_kernel, regions), (jax.ShapeDtypeStruc...  0.82 us
    reshape x2, local copies, waits for them, and re-layouts, blocked(): return array.reshape(rows, row_blocks, block_size).transpose(1, 0, 2)  0.79 us
    unnamed x16, local copies, waits for them, and re-layouts  0.72 us
    pallas_call x1, Pallas kernels, paired_step(): kernel_call(outflow_kernel, (jax.ShapeDtypeStruct((2 * row_blocks, block_...  0.61 us
  transfers between devices with their start and end apart: 7, of which 5 were waited for; matrix products, arithmetic and copies ran while one was open for 0% of the time, Pallas kernels for 11%

profile of v4, /device:TPU:0, one launch (start us, length us, event | category | flops | bytes accessed | tf_op | source)
XLA Modules:
  0.0 19.2 jit_solution(6707965168829540020)
XLA Ops:
  0.6 0.8 %reshape.10 = bf16[24,4,128]{2,1,0:T(4,128)(2,1)S(1)} reshape(bf16[12,2,512]{2,1,0:T(2,128)(2,1)} %param.13) | data formatting | bytes 49152 | tf_op jit(solution)/shard_map/reshape | solution.py:401
  1.5 0.0 copy-start.4
  1.5 0.0 copy-start
  1.5 3.0 %collective-permute-start = (bf16[2,4,24,128]{3,2,1,0:T(8,128)(2,1)S(1)}, bf16[2,4,24,128]{3,2,1,0:T(8,128)(2,1)S(1)}, u32[]{:S(2)}, u32[]{:S(2)}) collective-permute-start(bf16[2,4,24,128]{3,2,1,0:T(8,128)(2,1)S(1)} %shard_map.104.own_ref.message_ref), channel_id=1, source_target_pairs={{0,2},{2,0},{1,3},{3,1},{4,6},{6,4},{5,7},{7,5},{8,10},{10,8},{9,1... | collective-permute-start | bytes 147464 | tf_op jit(solution)/shard_map/ppermute | solution.py:34
  4.5 0.6 %shard_map.106 = (bf16[8,128,512]{2,1,0:T(8,128)(2,1)S(1)}, f32[4,24,128]{2,1,0:T(8,128)S(1)}, bf16[4,24,128]{2,1,0:T(8,128)(2,1)S(1)}) custom-call(bf16[2,4,24,128]{3,2,1,0:T(8,128)(2,1)S(1)} %shard_map.104.own_ref.message_ref, s32[2,512]{1,0:T(2,128)S(1)} %copy-done.4), custom_call_target="tpu_custom_call" | custom-call | flops 1000000 | bytes 4000000 | tf_op jit(solution)/shard_map/pallas_call | solution.py:411
  5.1 0.0 copy-done
  5.2 0.0 copy-start.1
  5.2 0.6 %collective-permute-start.4 = (bf16[3,2,2,128,128]{4,3,2,1,0:T(8,128)(2,1)S(1)}, bf16[3,2,2,128,128]{4,3,2,1,0:T(8,128)(2,1)S(1)}, u32[]{:S(2)}, u32[]{:S(2)}) collective-permute-start(bf16[3,2,2,128,128]{4,3,2,1,0:T(8,128)(2,1)S(1)} %shard_map.107), channel_id=1, source_target_pairs={{0,2},{2,0},{1,3},{3,1},{4,6},{6,4},{5,7},{7,5},{8,10},{10,8},{9,1... | collective-permute-start | bytes 1179656 | tf_op jit(solution)/shard_map/ppermute | solution.py:34
  5.8 0.7 %collective-permute-done.other_ref = bf16[2,4,24,128]{3,2,1,0:T(8,128)(2,1)S(1)} collective-permute-done((bf16[2,4,24,128]{3,2,1,0:T(8,128)(2,1)S(1)}, bf16[2,4,24,128]{3,2,1,0:T(8,128)(2,1)S(1)}, u32[]{:S(2)}, u32[]{:S(2)}) %collective-permute-start) | collective-permute-done | bytes 49184 | tf_op jit(solution)/shard_map/ppermute | solution.py:34
  6.6 3.2 %collective-permute-start.1 = (bf16[2,8,24,128]{3,2,1,0:T(8,128)(2,1)S(1)}, bf16[2,8,24,128]{3,2,1,0:T(8,128)(2,1)S(1)}, u32[]{:S(2)}, u32[]{:S(2)}) collective-permute-start(bf16[2,8,24,128]{3,2,1,0:T(8,128)(2,1)S(1)} %shard_map.105.held_ref.refs_11_.refs_8_), channel_id=1, source_target_pairs={{0,8},{4,12},{8,0},{12,4},{1,9},{5,13},{9,1},{13,5},{2,10},{6,14},... | collective-permute-start | bytes 294920 | tf_op jit(solution)/shard_map/ppermute | solution.py:427
  9.8 1.3 %collective-permute-start.3 = (bf16[2,8,24,128]{3,2,1,0:T(8,128)(2,1)S(1)}, bf16[2,8,24,128]{3,2,1,0:T(8,128)(2,1)S(1)}, u32[]{:S(2)}, u32[]{:S(2)}) collective-permute-start(bf16[2,8,24,128]{3,2,1,0:T(8,128)(2,1)S(1)} %shard_map.105.held_ref.refs_11_.refs_8_), channel_id=1, source_target_pairs={{0,12},{4,8},{8,4},{12,0},{1,13},{5,9},{9,5},{13,1},{2,14},{6,10},... | collective-permute-start | bytes 294920 | tf_op jit(solution)/shard_map/ppermute | solution.py:427
  11.1 0.2 %collective-permute-start.2 = (bf16[2,8,24,128]{3,2,1,0:T(8,128)(2,1)S(1)}, bf16[2,8,24,128]{3,2,1,0:T(8,128)(2,1)S(1)}, u32[]{:S(2)}, u32[]{:S(2)}) collective-permute-start(bf16[2,8,24,128]{3,2,1,0:T(8,128)(2,1)S(1)} %shard_map.105.held_ref.refs_11_.refs_8_), channel_id=1, source_target_pairs={{0,4},{4,0},{8,12},{12,8},{1,5},{5,1},{9,13},{13,9},{2,6},{6,2},{1... | collective-permute-start | bytes 294920 | tf_op jit(solution)/shard_map/ppermute | solution.py:427
  11.4 0.7 %copy-done.3 = s32[4,4,2]{1,2,0:T(2,128)S(1)} copy-done((s32[4,4,2]{1,2,0:T(2,128)S(1)}, s32[4,4,2]{1,2,0:T(2,128)}, u32[]{:S(2)}) %copy-start.3) | copy-done | bytes 152
  12.0 0.0 copy-done.2
  12.1 0.4 %shard_map.108 = (f32[5,24,128]{2,1,0:T(8,128)S(1)}, s32[2,4,4,2,128]{4,3,2,1,0:T(2,128)S(1)}, f32[4,24,128]{2,1,0:T(8,128)S(1)}, f32[4,24,128]{2,1,0:T(8,128)S(1)}, bf16[9,24,128]{2,1,0:T(8,128)(2,1)S(1)}) custom-call(bf16[2,8,24,128]{3,2,1,0:T(8,128)(2,1)S(1)} %shard_map.105.held_ref.refs_11_.refs_8_, bf16[4,4,2,128,128]{4,3,2,1,0:T(8,128)(2,1)S(1)} %copy-done, ...), custom_call_target="tpu_custom_call" | custom-call | flops 1000000 | bytes 4000000 | tf_op jit(solution)/shard_map/pallas_call | solution.py:431
  12.4 1.9 %collective-permute-start.6 = (bf16[9,24,128]{2,1,0:T(8,128)(2,1)S(1)}, bf16[9,24,128]{2,1,0:T(8,128)(2,1)S(1)}, u32[]{:S(2)}, u32[]{:S(2)}) collective-permute-start(bf16[9,24,128]{2,1,0:T(8,128)(2,1)S(1)} %get-tuple-element.22), channel_id=1, source_target_pairs={{0,2},{2,0},{1,3},{3,1},{4,6},{6,4},{5,7},{7,5},{8,10},{10,8},{9,1... | collective-permute-start | bytes 165896 | tf_op jit(solution)/shard_map/ppermute | solution.py:34
  14.3 2.2 %collective-permute-done.4.refs_3_ = bf16[3,2,2,128,128]{4,3,2,1,0:T(8,128)(2,1)S(1)} collective-permute-done((bf16[3,2,2,128,128]{4,3,2,1,0:T(8,128)(2,1)S(1)}, bf16[3,2,2,128,128]{4,3,2,1,0:T(8,128)(2,1)S(1)}, u32[]{:S(2)}, u32[]{:S(2)}) %collective-permute-start.4) | collective-permute-done | bytes 393248 | tf_op jit(solution)/shard_map/ppermute | solution.py:34
  16.4 0.0 collective-permute-start.5
  16.4 0.3 %shard_map.109 = (f32[4,24,128]{2,1,0:T(8,128)S(1)}, f32[4,24,128]{2,1,0:T(8,128)S(1)}) custom-call(s32[2,4,4,2,128]{4,3,2,1,0:T(2,128)S(1)} %get-tuple-element.16.table_ref.refs_4_, bf16[2,8,24,128]{3,2,1,0:T(8,128)(2,1)S(1)} %collective-permute-done.1.held_ref.refs_0_, bf16[4,4,2,128,128]{4,3,2,1,0:T(8,128)(2,1)S(1)} %copy-done, ...), custom_call_target="tpu_custom_call" | custom-call | flops 3000000000 | bytes 4000000 | tf_op jit(solution)/shard_map/pallas_call | solution.py:446
  16.7 0.3 %collective-permute-done.6.refs_9_.refs_6_ = bf16[9,24,128]{2,1,0:T(8,128)(2,1)S(1)} collective-permute-done((bf16[9,24,128]{2,1,0:T(8,128)(2,1)S(1)}, bf16[9,24,128]{2,1,0:T(8,128)(2,1)S(1)}, u32[]{:S(2)}, u32[]{:S(2)}) %collective-permute-start.6) | collective-permute-done | bytes 55328 | tf_op jit(solution)/shard_map/ppermute | solution.py:34
  17.0 0.1 collective-permute-done.2.refs_1_
  17.1 0.8 %shard_map.110 = (f32[24,512]{1,0:T(8,128)S(1)}, s32[24,128]{1,0:T(8,128)S(1)}) custom-call(bf16[2,8,24,128]{3,2,1,0:T(8,128)(2,1)S(1)} %collective-permute-done.1.held_ref.refs_0_, bf16[2,8,24,128]{3,2,1,0:T(8,128)(2,1)S(1)} %collective-permute-done.2.refs_1_, bf16[2,8,24,128]{3,2,1,0:T(8,128)(2,1)S(1)} %collective-permute-done.3.refs_2_, ...), custom_call_target="tpu_custom_call" | custom-call | flops 3000000000 | bytes 4000000 | tf_op jit(solution)/shard_map/pallas_call | solution.py:452
  17.9 0.2 %collective-permute-done.5.refs_3_ = bf16[3,2,2,128,128]{4,3,2,1,0:T(8,128)(2,1)S(1)} collective-permute-done((bf16[3,2,2,128,128]{4,3,2,1,0:T(8,128)(2,1)S(1)}, bf16[3,2,2,128,128]{4,3,2,1,0:T(8,128)(2,1)S(1)}, u32[]{:S(2)}, u32[]{:S(2)}) %collective-permute-start.5) | collective-permute-done | bytes 393248 | tf_op jit(solution)/shard_map/ppermute | solution.py:34
  18.2 1.1 %shard_map.111 = (f32[12,2,512]{2,1,0:T(2,128)}, f32[12,2,512]{2,1,0:T(2,128)}) custom-call(bf16[2,8,24,128]{3,2,1,0:T(8,128)(2,1)S(1)} %collective-permute-done.1.held_ref.refs_0_, bf16[2,8,24,128]{3,2,1,0:T(8,128)(2,1)S(1)} %collective-permute-done.2.refs_1_, bf16[2,8,24,128]{3,2,1,0:T(8,128)(2,1)S(1)} %collective-permute-done.3.refs_2_, ...), custom_call_target="tpu_custom_call" | custom-call | flops 8000000000 | bytes 4000000 | tf_op jit(solution)/shard_map/pallas_call | solution.py:460
  (17 shorter events, 0.1 us)
Async XLA Ops:
  0.6 0.8 %copy-start.7 = (bf16[12,2,512]{2,1,0:T(2,128)(2,1)S(1)}, bf16[12,2,512]{2,1,0:T(2,128)(2,1)}, u32[]{:S(2)}) copy-start(bf16[12,2,512]{2,1,0:T(2,128)(2,1)} %param.14) | copy-start | bytes 73732
  1.5 3.0 %copy-start.4 = (s32[2,512]{1,0:T(2,128)S(1)}, s32[2,512]{1,0:T(2,128)}, u32[]{:S(2)}) copy-start(s32[2,512]{1,0:T(2,128)} %ends_ref.1) | copy-start | bytes 12292
  1.5 3.6 %copy-start = (bf16[4,4,2,128,128]{4,3,2,1,0:T(8,128)(2,1)S(1)}, bf16[4,4,2,128,128]{4,3,2,1,0:T(8,128)(2,1)}, u32[]{:S(2)}) copy-start(bf16[4,4,2,128,128]{4,3,2,1,0:T(8,128)(2,1)} %refs_5_.1) | copy-start | bytes 3145732
  1.5 5.1 %collective-permute-start = (bf16[2,4,24,128]{3,2,1,0:T(8,128)(2,1)S(1)}, bf16[2,4,24,128]{3,2,1,0:T(8,128)(2,1)S(1)}, u32[]{:S(2)}, u32[]{:S(2)}) collective-permute-start(bf16[2,4,24,128]{3,2,1,0:T(8,128)(2,1)S(1)} %shard_map.104.own_ref.message_ref), channel_id=1, source_target_pairs={{0,2},{2,0},{1,3},{3,1},{4,6},{6,4},{5,7},{7,5},{8,10},{10,8},{9,1... | collective-permute-start | bytes 147464 | tf_op jit(solution)/shard_map/ppermute | solution.py:34
  5.2 6.2 %copy-start.1 = (bf16[4,4,2,128,128]{4,3,2,1,0:T(8,128)(2,1)S(1)}, bf16[4,4,2,128,128]{4,3,2,1,0:T(8,128)(2,1)}, u32[]{:S(2)}) copy-start(bf16[4,4,2,128,128]{4,3,2,1,0:T(8,128)(2,1)} %refs_6_.1) | copy-start | bytes 3145732
  5.2 11.2 %collective-permute-start.4 = (bf16[3,2,2,128,128]{4,3,2,1,0:T(8,128)(2,1)S(1)}, bf16[3,2,2,128,128]{4,3,2,1,0:T(8,128)(2,1)S(1)}, u32[]{:S(2)}, u32[]{:S(2)}) collective-permute-start(bf16[3,2,2,128,128]{4,3,2,1,0:T(8,128)(2,1)S(1)} %shard_map.107), channel_id=1, source_target_pairs={{0,2},{2,0},{1,3},{3,1},{4,6},{6,4},{5,7},{7,5},{8,10},{10,8},{9,1... | collective-permute-start | bytes 1179656 | tf_op jit(solution)/shard_map/ppermute | solution.py:34
  6.6 4.8 %copy-start.5 = (f32[512]{0:T(512)S(1)}, f32[512]{0:T(512)}, u32[]{:S(2)}) copy-start(f32[512]{0:T(512)} %param.16) | copy-start | bytes 6148
  6.6 9.8 %collective-permute-start.1 = (bf16[2,8,24,128]{3,2,1,0:T(8,128)(2,1)S(1)}, bf16[2,8,24,128]{3,2,1,0:T(8,128)(2,1)S(1)}, u32[]{:S(2)}, u32[]{:S(2)}) collective-permute-start(bf16[2,8,24,128]{3,2,1,0:T(8,128)(2,1)S(1)} %shard_map.105.held_ref.refs_11_.refs_8_), channel_id=1, source_target_pairs={{0,8},{4,12},{8,0},{12,4},{1,9},{5,13},{9,1},{13,5},{2,10},{6,14},... | collective-permute-start | bytes 294920 | tf_op jit(solution)/shard_map/ppermute | solution.py:427
  9.8 7.3 %collective-permute-start.3 = (bf16[2,8,24,128]{3,2,1,0:T(8,128)(2,1)S(1)}, bf16[2,8,24,128]{3,2,1,0:T(8,128)(2,1)S(1)}, u32[]{:S(2)}, u32[]{:S(2)}) collective-permute-start(bf16[2,8,24,128]{3,2,1,0:T(8,128)(2,1)S(1)} %shard_map.105.held_ref.refs_11_.refs_8_), channel_id=1, source_target_pairs={{0,12},{4,8},{8,4},{12,0},{1,13},{5,9},{9,5},{13,1},{2,14},{6,10},... | collective-permute-start | bytes 294920 | tf_op jit(solution)/shard_map/ppermute | solution.py:427
  11.1 6.0 %collective-permute-start.2 = (bf16[2,8,24,128]{3,2,1,0:T(8,128)(2,1)S(1)}, bf16[2,8,24,128]{3,2,1,0:T(8,128)(2,1)S(1)}, u32[]{:S(2)}, u32[]{:S(2)}) collective-permute-start(bf16[2,8,24,128]{3,2,1,0:T(8,128)(2,1)S(1)} %shard_map.105.held_ref.refs_11_.refs_8_), channel_id=1, source_target_pairs={{0,4},{4,0},{8,12},{12,8},{1,5},{5,1},{9,13},{13,9},{2,6},{6,2},{1... | collective-permute-start | bytes 294920 | tf_op jit(solution)/shard_map/ppermute | solution.py:427
  11.4 0.7 %copy-start.3 = (s32[4,4,2]{1,2,0:T(2,128)S(1)}, s32[4,4,2]{1,2,0:T(2,128)}, u32[]{:S(2)}) copy-start(s32[4,4,2]{1,2,0:T(2,128)} %param.12) | copy-start | bytes 388
  11.4 0.7 %copy-start.2 = (s32[4,4,2]{1,2,0:T(2,128)S(1)}, s32[4,4,2]{1,2,0:T(2,128)}, u32[]{:S(2)}) copy-start(s32[4,4,2]{1,2,0:T(2,128)} %param.10) | copy-start | bytes 388
  11.4 0.7 %copy-start.6 = (f32[12]{0:T(128)S(1)}, f32[12]{0:T(128)}, u32[]{:S(2)}) copy-start(f32[12]{0:T(128)} %param.15) | copy-start | bytes 148
  12.4 4.6 %collective-permute-start.6 = (bf16[9,24,128]{2,1,0:T(8,128)(2,1)S(1)}, bf16[9,24,128]{2,1,0:T(8,128)(2,1)S(1)}, u32[]{:S(2)}, u32[]{:S(2)}) collective-permute-start(bf16[9,24,128]{2,1,0:T(8,128)(2,1)S(1)} %get-tuple-element.22), channel_id=1, source_target_pairs={{0,2},{2,0},{1,3},{3,1},{4,6},{6,4},{5,7},{7,5},{8,10},{10,8},{9,1... | collective-permute-start | bytes 165896 | tf_op jit(solution)/shard_map/ppermute | solution.py:34
  16.4 1.7 %collective-permute-start.5 = (bf16[3,2,2,128,128]{4,3,2,1,0:T(8,128)(2,1)S(1)}, bf16[3,2,2,128,128]{4,3,2,1,0:T(8,128)(2,1)S(1)}, u32[]{:S(2)}, u32[]{:S(2)}) collective-permute-start(bf16[3,2,2,128,128]{4,3,2,1,0:T(8,128)(2,1)S(1)} %collective-permute-done.4.refs_3_), channel_id=1, source_target_pairs={{0,1},{1,0},{2,3},{3,2},{4,5},{5,4},{6,7},{7,6},{8,9},{9,8},{10,11... | collective-permute-start | bytes 1179656 | tf_op jit(solution)/shard_map/ppermute | solution.py:34

commit v5 on v4

--- a/solution.py
+++ b/solution.py
@@ -12,13 +12,11 @@
 VMEM = pl.BlockSpec(memory_space=pltpu.VMEM)
 SMEM = pl.BlockSpec(memory_space=pltpu.SMEM)
 ANY = pl.BlockSpec(memory_space=pl.ANY)
-HBM = pl.BlockSpec(memory_space=pltpu.HBM)
-MAIN = 3_000_000
 STACK = 5_000_000
 JOIN = 10_000_000
-SEND = 1_000
-FIRST = 1_000
+SMALL = 1_000
 NEXT = 3_000_000
+MAIN = 3_000_000
 LAST = 8_000_000
 
 
@@ -186,12 +184,8 @@
 
 def region_moves(regions):
     if regions == 4:
-        return [[2, 3, 0, 1], [1, 0, 3, 2], [3, 2, 1, 0]]
+        return [[3, 2, 0, 1], [1, 0, 3, 2], [2, 3, 1, 0]]
     return [[(place + shift) % regions for place in range(regions)] for shift in range(1, regions)]
-
-
-def shift_order(regions):
-    return list(range(1, regions))
 
 
 def turned_rows(array):
@@ -216,39 +210,42 @@
     )
 
 
-def region_terms(shift, table_ref, held_ref, p_ref, l_ref, region, row):
+def region_terms(regions, move, table_ref, held_ref, p_ref, l_ref, row):
+    region = back(regions, move)
     slots = range(p_ref.shape[2])
     return tuple(
         pair_dot(
             held_ref.at[kind],
-            [table_ref[kind, shift, row, slot, 0] for slot in slots],
+            [table_ref[kind, move, row, slot, 0] for slot in slots],
             [slab_ref[row, region, slot] for slot in slots],
         )
         for kind, slab_ref in enumerate((p_ref, l_ref))
     )
 
 
-def outflow_kernel(message_ref, ends_ref, matrix_ref, outflow_ref, away_ref):
-    row_blocks, _, block_size = outflow_ref.shape
+def outflow_terms(side, ends_ref, current_ref, matrix_ref, store):
+    row_blocks, block_size = matrix_ref.shape[:2]
     leaves, enters = ends_ref[0:1, :], ends_ref[1:2, :]
-    current = lanes([message_ref[1, block] for block in range(row_blocks)])
-    for block in range(2 * row_blocks):
-        side, at = divmod(block, row_blocks)
-        base = ((lax.axis_index("cell") ^ side) * row_blocks + at) * block_size
+    current = lanes([current_ref[1, block] for block in range(row_blocks)])
+    for block in range(row_blocks):
+        base = ((lax.axis_index("cell") ^ side) * row_blocks + block) * block_size
         panel = lax.broadcasted_iota(jnp.int32, (block_size, ends_ref.shape[1]), 0) + base
         entry = (leaves == panel).astype(jnp.float32) - (enters == panel).astype(jnp.float32)
         entry = entry.astype(jnp.bfloat16)
         matrix_ref[block] = entry
-        sums = lax.dot_general(current, entry, NT, preferred_element_type=jnp.float32)
-        if side == 0:
-            outflow_ref[at] = sums
-        else:
-            away_ref[at] = sums.astype(jnp.bfloat16)
+        store(block, lax.dot_general(current, entry, NT, preferred_element_type=jnp.float32))
+
+
+def outflow_kernel(message_ref, ends_ref, matrix_ref, outflow_ref):
+    def store(block, sums):
+        outflow_ref[block] = sums
+
+    outflow_terms(0, ends_ref, message_ref, matrix_ref, store)
 
 
 def first_kernel(
-    regions, held_ref, p_ref, l_ref, p_cols_ref, l_cols_ref, omega_ref, resist_ref, away_ref,
-    factor_ref, table_ref, potential_ref, flux_ref, early_ref, numbers_ref,
+    regions, held_ref, p_ref, l_ref, p_cols_ref, l_cols_ref, omega_ref, resist_ref, ends_ref,
+    factor_ref, table_ref, potential_ref, flux_ref, early_ref, matrix_ref, numbers_ref,
 ):
     row_blocks, rows, block_size = potential_ref.shape
     slots = p_ref.shape[2]
@@ -259,20 +256,24 @@
     for kind, cols_ref in enumerate((p_cols_ref, l_cols_ref)):
         columns = cols_ref[...].astype(jnp.float32)
         place = lax.broadcasted_iota(jnp.int32, columns.shape, 2)
-        for shift in range(regions):
-            column = jnp.sum(jnp.where(place == back(regions, shift), columns, 0.0), axis=2, keepdims=True)
+        for move in range(regions):
+            column = jnp.sum(jnp.where(place == back(regions, move), columns, 0.0), axis=2, keepdims=True)
             column = jnp.broadcast_to(column, shape)
             other = jnp.where(column < row_blocks, column + row_blocks, column - row_blocks)
-            table_ref[kind, shift] = jnp.where(cell == 0, column, other).astype(jnp.int32)
+            table_ref[kind, move] = jnp.where(cell == 0, column, other).astype(jnp.int32)
             if kind == 0:
-                numbers = jnp.where(lane == shift, jnp.where(cell == 0, other, column), numbers)
+                numbers = jnp.where(lane == move, jnp.where(cell == 0, other, column), numbers)
     numbers_ref[...] = jnp.zeros_like(numbers_ref)
     for row in range(row_blocks):
         numbers_ref[row * slots : (row + 1) * slots, :] = numbers[row]
     early_ref[2 * row_blocks] = numbers_ref[...].astype(jnp.bfloat16)
-    early_ref[row_blocks : 2 * row_blocks] = away_ref[...]
-    for row in range(row_blocks):
-        potential, flux = region_terms(0, table_ref, held_ref, p_ref, l_ref, back(regions, 0), row)
+
+    def store(block, sums):
+        early_ref[row_blocks + block] = sums.astype(jnp.bfloat16)
+
+    outflow_terms(1, ends_ref, held_ref, matrix_ref, store)
+    for row in range(row_blocks):
+        potential, flux = region_terms(regions, 0, table_ref, held_ref, p_ref, l_ref, row)
         potential_ref[row], flux_ref[row] = potential, flux
         early_ref[row] = potential.astype(jnp.bfloat16)
     factor_ref[0] = jnp.broadcast_to(row_scale(omega_ref, rows), (rows, block_size))
@@ -281,11 +282,12 @@
         factor_ref[1 + row] = jnp.broadcast_to(resist_ref[:, columns], (rows, block_size))
 
 
-def next_kernel(regions, shift, table_ref, held_ref, p_ref, l_ref, p_in_ref, f_in_ref, *refs):
-    potential_ref, flux_ref = refs[-2:]
-    region = back(regions, shift)
+def next_kernel(
+    regions, move, table_ref, held_ref, p_ref, l_ref, p_in_ref, f_in_ref, matrix_ref, potential_ref, flux_ref
+):
+    del matrix_ref
     for row in range(potential_ref.shape[0]):
-        potential, flux = region_terms(shift, table_ref, held_ref, p_ref, l_ref, region, row)
+        potential, flux = region_terms(regions, move, table_ref, held_ref, p_ref, l_ref, row)
         potential_ref[row], flux_ref[row] = p_in_ref[row] + potential, f_in_ref[row] + flux
 
 
@@ -297,9 +299,9 @@
 def send_kernel(regions, p_ref, after_ref, out_ref):
     del after_ref
     half = out_ref.shape[1]
-    for at, shift in enumerate(shift_order(regions)):
+    for move in range(1, regions):
         for row in range(half):
-            out_ref[at, row] = p_ref[lax.axis_index("col") * half + row, back(regions, shift)]
+            out_ref[move - 1, row] = p_ref[lax.axis_index("col") * half + row, back(regions, move)]
 
 
 def join_kernel(own_ref, other_ref, out_ref):
@@ -314,15 +316,15 @@
         out_ref[freq, :, columns] = array[2 * freq : 2 * freq + 2]
 
 
-def other_rows(order, part, slab_ref, numbers_ref, early_ref, piece_refs, other_ref):
+def other_rows(part, slab_ref, numbers_ref, early_ref, piece_refs, other_ref):
     half, slots = slab_ref.shape[1:3]
     for position in range(half):
         row = (lax.axis_index("col") ^ part) * half + position
         total = early_ref[row].astype(jnp.float32)
-        for at, shift in enumerate(order):
+        for at, piece_ref in enumerate(piece_refs):
             total += pair_dot(
-                piece_refs[at].at[0],
-                [numbers_ref[row * slots + slot, shift] for slot in range(slots)],
+                piece_ref.at[0],
+                [numbers_ref[row * slots + slot, at + 1] for slot in range(slots)],
                 [slab_ref[at, position, slot] for slot in range(slots)],
             )
         other_ref[row] = total.astype(jnp.bfloat16)
@@ -331,29 +333,25 @@
 def other_drop(part, half, other_ref, matrix_ref):
     start = (lax.axis_index("col") ^ part) * half
     rows = lanes([other_ref[start + position] for position in range(half)])
-    matrix = matrix_ref[pl.ds(2 * half + start, half)].reshape(rows.shape[1], -1)
+    matrix = matrix_ref[pl.ds(start, half)].reshape(rows.shape[1], -1)
     return lax.dot_general(rows, matrix, NN, preferred_element_type=jnp.float32)
 
 
 def main_kernel(regions, *refs):
-    order = shift_order(regions)
     piece_refs = refs[: regions - 1]
-    (mine_ref, table_ref, p_ref, l_ref, p_in_ref, f_in_ref, early_ref, matrix_ref, held_ref, factor_ref,
-     out_ref, numbers_ref, other_ref) = refs[regions - 1 :]
+    (mine_ref, table_ref, p_ref, l_ref, p_in_ref, f_in_ref, early_ref, matrix_ref, other_matrix_ref, held_ref,
+     factor_ref, out_ref, numbers_ref, other_ref) = refs[regions - 1 :]
     row_blocks, _, block_size = p_in_ref.shape
     numbers_ref[...] = early_ref[2 * row_blocks].astype(jnp.float32).astype(jnp.int32)
     potentials, fluxes = [], []
     for row in range(row_blocks):
-        potential, flux = p_in_ref[row], f_in_ref[row]
-        for shift, piece_ref in list(zip(order, piece_refs))[1:]:
-            terms = region_terms(shift, table_ref, piece_ref, p_ref, l_ref, back(regions, shift), row)
-            potential, flux = potential + terms[0], flux + terms[1]
-        potentials.append(potential.astype(jnp.bfloat16))
-        fluxes.append(flux)
-    other_rows(order, 0, mine_ref, numbers_ref, early_ref, piece_refs, other_ref)
-    matrix = matrix_ref[:row_blocks].reshape(row_blocks * block_size, -1)
+        potential, flux = region_terms(regions, regions - 1, table_ref, piece_refs[-1], p_ref, l_ref, row)
+        potentials.append((p_in_ref[row] + potential).astype(jnp.bfloat16))
+        fluxes.append(f_in_ref[row] + flux)
+    other_rows(0, mine_ref, numbers_ref, early_ref, piece_refs, other_ref)
+    matrix = matrix_ref[...].reshape(row_blocks * block_size, -1)
     drop = lax.dot_general(lanes(potentials), matrix, NN, preferred_element_type=jnp.float32)
-    drop += other_drop(0, row_blocks // 2, other_ref, matrix_ref)
+    drop += other_drop(0, row_blocks // 2, other_ref, other_matrix_ref)
     for row in range(row_blocks):
         columns = slice(row * block_size, (row + 1) * block_size)
         current = held_ref[1, row].astype(jnp.float32)
@@ -366,7 +364,7 @@
     (theirs_ref, numbers_ref, begun_ref, early_ref, matrix_ref, held_ref, outflow_ref, factor_ref,
      cell_ref, panel_ref, other_ref) = refs[regions - 1 :]
     row_blocks, _, block_size = outflow_ref.shape
-    other_rows(shift_order(regions), 1, theirs_ref, numbers_ref, early_ref, piece_refs, other_ref)
+    other_rows(1, theirs_ref, numbers_ref, early_ref, piece_refs, other_ref)
     total = begun_ref[...] + other_drop(1, row_blocks // 2, other_ref, matrix_ref)
     for row in range(row_blocks):
         columns = slice(row * block_size, (row + 1) * block_size)
@@ -376,16 +374,16 @@
         store_rows(panel_ref, columns, outflow + charge)
 
 
-def kernel_call(body, out_shape, memories, cost, scratch=(), size=4_000_000):
+def kernel_call(body, out_shape, memories, weight, scratch=()):
     many = isinstance(out_shape, tuple)
     return pl.pallas_call(
         body,
         out_shape=out_shape,
-        in_specs=[{"h": HBM, "v": VMEM, "a": ANY}[m] for m in memories],
+        in_specs=[{"v": VMEM, "a": ANY}[m] for m in memories],
         out_specs=tuple(VMEM for _ in out_shape) if many else VMEM,
         scratch_shapes=scratch,
         compiler_params=pltpu.CompilerParams(vmem_limit_bytes=16 * 1024 * 1024),
-        cost_estimate=pl.CostEstimate(flops=cost * 1000, bytes_accessed=size, transcendentals=0),
+        cost_estimate=pl.CostEstimate(flops=weight * 1000, bytes_accessed=4_000_000, transcendentals=0),
     )
 
 
@@ -395,7 +393,6 @@
     row_blocks = p_blocks.shape[0]
     rows = 2 * freq_count
     regions = lax.axis_size("blk")
-    order = shift_order(regions)
 
     def blocked(array):
         return array.reshape(rows, row_blocks, block_size).transpose(1, 0, 2)
@@ -408,27 +405,17 @@
     )(message, swapped(message, "cell", 1))
 
     totals = jax.ShapeDtypeStruct((row_blocks, rows, block_size), jnp.float32)
-    matrix, outflow, away = kernel_call(
-        outflow_kernel,
-        (
-            jax.ShapeDtypeStruct((2 * row_blocks, block_size, share), jnp.bfloat16),
-            totals,
-            jax.ShapeDtypeStruct((row_blocks, rows, block_size), jnp.bfloat16),
-        ),
-        "vv",
-        SEND,
-    )(message, branch_ends)
+    matrix_shape = jax.ShapeDtypeStruct((row_blocks, block_size, share), jnp.bfloat16)
+    matrix, outflow = kernel_call(outflow_kernel, (matrix_shape, totals), "vv", SMALL)(message, branch_ends)
     half_shape = jax.ShapeDtypeStruct((regions - 1, row_blocks // 2) + p_blocks.shape[2:], jnp.bfloat16)
-    sent = kernel_call(functools.partial(send_kernel, regions), half_shape, "va", SEND)(p_blocks, outflow)
+    sent = kernel_call(functools.partial(send_kernel, regions), half_shape, "va", SMALL)(p_blocks, outflow)
     mine = swapped(sent, "cell", 1)
     theirs = swapped(mine, "col", 1)
 
-    pieces = [
-        lax.ppermute(held, "blk", list(enumerate(targets))) for targets in region_moves(regions)
-    ]
+    pieces = [lax.ppermute(held, "blk", list(enumerate(targets))) for targets in region_moves(regions)]
 
     slots = p_cols.shape[2]
-    factors, table, potential, flux, early = kernel_call(
+    factors, table, potential, flux, early, other_matrix = kernel_call(
         functools.partial(first_kernel, regions),
         (
             jax.ShapeDtypeStruct((1 + row_blocks, rows, block_size), jnp.float32),
@@ -436,15 +423,19 @@
             totals,
             totals,
             jax.ShapeDtypeStruct((2 * row_blocks + 1, rows, block_size), jnp.bfloat16),
+            matrix_shape,
         ),
         "vvvvvvvv",
-        FIRST,
+        SMALL,
         [pltpu.VMEM((rows, block_size), jnp.float32)],
-    )(held, p_blocks, l_blocks, p_cols.transpose(0, 2, 1), l_cols.transpose(0, 2, 1), omegas[None], resist[None], away)
+    )(
+        held, p_blocks, l_blocks, p_cols.transpose(0, 2, 1), l_cols.transpose(0, 2, 1), omegas[None], resist[None],
+        branch_ends,
+    )
     early = swapped(early, "cell", 1)
-    for shift, piece in list(zip(order, pieces))[:1]:
+    for move, piece in enumerate(pieces[:-1], 1):
         potential, flux = kernel_call(
-            functools.partial(next_kernel, regions, shift), (totals, totals), "vvvvvvv", NEXT
+            functools.partial(next_kernel, regions, move), (totals, totals), "vvvvvvv", NEXT
         )(table, piece, p_blocks, l_blocks, potential, flux, matrix)
 
     numbers_shape = jax.ShapeDtypeStruct((rows, block_size), jnp.int32)
@@ -452,14 +443,14 @@
     begun, numbers = kernel_call(
         functools.partial(main_kernel, regions),
         (jax.ShapeDtypeStruct((rows, share), jnp.float32), numbers_shape),
-        "v" * (9 + regions),
+        "v" * (10 + regions),
         MAIN,
         [other_scratch],
-    )(*pieces, mine, table, p_blocks, l_blocks, potential, flux, early, matrix, held, factors)
+    )(*pieces, mine, table, p_blocks, l_blocks, potential, flux, early, matrix, other_matrix, held, factors)
     result = jax.ShapeDtypeStruct(charges.shape, jnp.float32)
     return kernel_call(
         functools.partial(last_kernel, regions), (result, result), "v" * (7 + regions), LAST, [other_scratch]
-    )(*pieces, theirs, numbers, begun, early, matrix, held, outflow, factors)
+    )(*pieces, theirs, numbers, begun, early, other_matrix, held, outflow, factors)
 
 
 def per_device(*args):

time: 19.4 us -> 19.3 us (level)
  waiting for transfers between devices: 3.49 us -> 2.69 us
  starting transfers between devices: 10.3 us -> 10.8 us
    ppermute x4, waiting for transfers between devices: 3.43 us -> 2.51 us  [swapped(): lax.ppermute(array, axis, [(i, i ^ distance) for i in range(lax.axis_size...]
    ppermute x3, starting transfers between devices: 4.76 us -> 5.08 us  [paired_step(): lax.ppermute(held, 'blk', list(enumerate(targets)))]
    ppermute x4, starting transfers between devices: 5.51 us -> 5.76 us  [swapped(): lax.ppermute(array, axis, [(i, i ^ distance) for i in range(lax.axis_size...]
    pallas_call x1, Pallas kernels: 0.36 us -> 0.57 us  [paired_step(): kernel_call(functools.partial(first_kernel, regions), (jax.ShapeDtypeStru...]
    pallas_call x3 -> x4, Pallas kernels: 0.95 us -> 0.99 us  [the longest x2 0.58 us: paired_step(): kernel_call(functools.partial(next_kernel, regions, move), (totals, total...]
  transfers between devices with their start and end apart: 7 -> 7, of which waited for: 5 -> 4; matrix products, arithmetic and copies ran while one was open for 0% -> 0% of each run, Pallas kernels for 11% -> 12%
where the time goes in v5:
time: 19.3 us; the launch traced here: 19.1 us
  starting transfers between devices  10.8 us (56%)
  Pallas kernels  3.3 us (17%)
  waiting for transfers between devices  2.69 us (14%)
  local copies, waits for them, and re-layouts  1.5 us (8%)
  between operations  0.75 us (4%)
    ppermute x4, starting transfers between devices, swapped(): lax.ppermute(array, axis, [(i, i ^ distance) for i in range(lax.axis_size...  5.76 us
    ppermute x3, starting transfers between devices, paired_step(): lax.ppermute(held, 'blk', list(enumerate(targets)))  5.08 us
    ppermute x4, waiting for transfers between devices, swapped(): lax.ppermute(array, axis, [(i, i ^ distance) for i in range(lax.axis_size...  2.51 us
    pallas_call x1, Pallas kernels, paired_step(): kernel_call(functools.partial(last_kernel, regions), (result, result), 'v...  1.08 us
    reshape x2, local copies, waits for them, and re-layouts, blocked(): return array.reshape(rows, row_blocks, block_size).transpose(1, 0, 2)  0.79 us
    unnamed x16, local copies, waits for them, and re-layouts  0.7 us
    pallas_call x1, Pallas kernels, paired_step(): kernel_call(functools.partial(main_kernel, regions), (jax.ShapeDtypeStruc...  0.64 us
    pallas_call x2, Pallas kernels, paired_step(): kernel_call(functools.partial(next_kernel, regions, move), (totals, total...  0.58 us
  transfers between devices with their start and end apart: 7, of which 4 were waited for; matrix products, arithmetic and copies ran while one was open for 0% of the time, Pallas kernels for 12%

profile of v5, /device:TPU:0, one launch (start us, length us, event | category | flops | bytes accessed | tf_op | source)
XLA Modules:
  0.0 19.1 jit_solution(637325021553108555)
XLA Ops:
  0.6 0.8 %reshape.10 = bf16[24,4,128]{2,1,0:T(4,128)(2,1)S(1)} reshape(bf16[12,2,512]{2,1,0:T(2,128)(2,1)} %param.13) | data formatting | bytes 49152 | tf_op jit(solution)/shard_map/reshape | solution.py:398
  1.5 0.0 copy-start.2
  1.5 0.0 copy-start
  1.5 3.0 %collective-permute-start = (bf16[2,4,24,128]{3,2,1,0:T(8,128)(2,1)S(1)}, bf16[2,4,24,128]{3,2,1,0:T(8,128)(2,1)S(1)}, u32[]{:S(2)}, u32[]{:S(2)}) collective-permute-start(bf16[2,4,24,128]{3,2,1,0:T(8,128)(2,1)S(1)} %shard_map.104.own_ref.message_ref), channel_id=1, source_target_pairs={{0,2},{2,0},{1,3},{3,1},{4,6},{6,4},{5,7},{7,5},{8,10},{10,8},{9,1... | collective-permute-start | bytes 147464 | tf_op jit(solution)/shard_map/ppermute | solution.py:32
  4.5 0.4 %shard_map.106 = (bf16[4,128,512]{2,1,0:T(8,128)(2,1)S(1)}, f32[4,24,128]{2,1,0:T(8,128)S(1)}) custom-call(bf16[2,4,24,128]{3,2,1,0:T(8,128)(2,1)S(1)} %shard_map.104.own_ref.message_ref, s32[2,512]{1,0:T(2,128)S(1)} %copy-done.2), custom_call_target="tpu_custom_call" | custom-call | flops 1000000 | bytes 4000000 | tf_op jit(solution)/shard_map/pallas_call | solution.py:409
  4.9 0.0 copy-start.1
  4.9 0.8 %collective-permute-start.4 = (bf16[3,2,2,128,128]{4,3,2,1,0:T(8,128)(2,1)S(1)}, bf16[3,2,2,128,128]{4,3,2,1,0:T(8,128)(2,1)S(1)}, u32[]{:S(2)}, u32[]{:S(2)}) collective-permute-start(bf16[3,2,2,128,128]{4,3,2,1,0:T(8,128)(2,1)S(1)} %shard_map.107), channel_id=1, source_target_pairs={{0,2},{2,0},{1,3},{3,1},{4,6},{6,4},{5,7},{7,5},{8,10},{10,8},{9,1... | collective-permute-start | bytes 1179656 | tf_op jit(solution)/shard_map/ppermute | solution.py:32
  5.8 0.8 %collective-permute-done.other_ref = bf16[2,4,24,128]{3,2,1,0:T(8,128)(2,1)S(1)} collective-permute-done((bf16[2,4,24,128]{3,2,1,0:T(8,128)(2,1)S(1)}, bf16[2,4,24,128]{3,2,1,0:T(8,128)(2,1)S(1)}, u32[]{:S(2)}, u32[]{:S(2)}) %collective-permute-start) | collective-permute-done | bytes 49184 | tf_op jit(solution)/shard_map/ppermute | solution.py:32
  6.6 0.0 copy-start.3
  6.6 4.2 %collective-permute-start.1 = (bf16[2,8,24,128]{3,2,1,0:T(8,128)(2,1)S(1)}, bf16[2,8,24,128]{3,2,1,0:T(8,128)(2,1)S(1)}, u32[]{:S(2)}, u32[]{:S(2)}) collective-permute-start(bf16[2,8,24,128]{3,2,1,0:T(8,128)(2,1)S(1)} %shard_map.105.held_ref.refs_12_.refs_8_), channel_id=1, source_target_pairs={{0,12},{4,8},{8,0},{12,4},{1,13},{5,9},{9,1},{13,5},{2,14},{6,10},... | collective-permute-start | bytes 294920 | tf_op jit(solution)/shard_map/ppermute | solution.py:415
  10.8 0.0 collective-permute-start.2
  10.8 0.9 %collective-permute-start.3 = (bf16[2,8,24,128]{3,2,1,0:T(8,128)(2,1)S(1)}, bf16[2,8,24,128]{3,2,1,0:T(8,128)(2,1)S(1)}, u32[]{:S(2)}, u32[]{:S(2)}) collective-permute-start(bf16[2,8,24,128]{3,2,1,0:T(8,128)(2,1)S(1)} %shard_map.105.held_ref.refs_12_.refs_8_), channel_id=1, source_target_pairs={{0,8},{4,12},{8,4},{12,0},{1,9},{5,13},{9,5},{13,1},{2,10},{6,14},... | collective-permute-start | bytes 294920 | tf_op jit(solution)/shard_map/ppermute | solution.py:415
  11.7 0.7 %copy-done.5 = f32[512]{0:T(512)S(1)} copy-done((f32[512]{0:T(512)S(1)}, f32[512]{0:T(512)}, u32[]{:S(2)}) %copy-start.5) | copy-done | bytes 2072
  12.4 0.6 %shard_map.108 = (f32[5,24,128]{2,1,0:T(8,128)S(1)}, s32[2,4,4,2,128]{4,3,2,1,0:T(2,128)S(1)}, f32[4,24,128]{2,1,0:T(8,128)S(1)}, f32[4,24,128]{2,1,0:T(8,128)S(...) custom-call(bf16[2,8,24,128]{3,2,1,0:T(8,128)(2,1)S(1)} %shard_map.105.held_ref.refs_12_.refs_8_, ...), custom_call_target="tpu_custom_call" | custom-call | flops 1000000 | bytes 4000000 | tf_op jit(solution)/shard_map/pallas_call | solution.py:418
  12.9 1.9 %collective-permute-start.6 = (bf16[9,24,128]{2,1,0:T(8,128)(2,1)S(1)}, bf16[9,24,128]{2,1,0:T(8,128)(2,1)S(1)}, u32[]{:S(2)}, u32[]{:S(2)}) collective-permute-start(bf16[9,24,128]{2,1,0:T(8,128)(2,1)S(1)} %get-tuple-element.25), channel_id=1, source_target_pairs={{0,2},{2,0},{1,3},{3,1},{4,6},{6,4},{5,7},{7,5},{8,10},{10,8},{9,1... | collective-permute-start | bytes 165896 | tf_op jit(solution)/shard_map/ppermute | solution.py:32
  14.9 0.0 collective-permute-done.1.held_ref.refs_0_
  14.9 0.3 %shard_map.109 = (f32[4,24,128]{2,1,0:T(8,128)S(1)}, f32[4,24,128]{2,1,0:T(8,128)S(1)}) custom-call(s32[2,4,4,2,128]{4,3,2,1,0:T(2,128)S(1)} %get-tuple-element.17.table_ref.refs_4_, bf16[2,8,24,128]{3,2,1,0:T(8,128)(2,1)S(1)} %collective-permute-done.1.held_ref.refs_0_, bf16[4,4,2,128,128]{4,3,2,1,0:T(8,128)(2,1)S(1)} %copy-done, ...), custom_call_target="tpu_custom_call" | custom-call | flops 3000000000 | bytes 4000000 | tf_op jit(solution)/shard_map/pallas_call | solution.py:437
  15.2 1.0 %collective-permute-done.4.refs_3_ = bf16[3,2,2,128,128]{4,3,2,1,0:T(8,128)(2,1)S(1)} collective-permute-done((bf16[3,2,2,128,128]{4,3,2,1,0:T(8,128)(2,1)S(1)}, bf16[3,2,2,128,128]{4,3,2,1,0:T(8,128)(2,1)S(1)}, u32[]{:S(2)}, u32[]{:S(2)}) %collective-permute-start.4) | collective-permute-done | bytes 393248 | tf_op jit(solution)/shard_map/ppermute | solution.py:32
  16.2 0.3 %shard_map.110 = (f32[4,24,128]{2,1,0:T(8,128)S(1)}, f32[4,24,128]{2,1,0:T(8,128)S(1)}) custom-call(s32[2,4,4,2,128]{4,3,2,1,0:T(2,128)S(1)} %get-tuple-element.17.table_ref.refs_4_, bf16[2,8,24,128]{3,2,1,0:T(8,128)(2,1)S(1)} %collective-permute-done.2.held_ref.refs_1_, bf16[4,4,2,128,128]{4,3,2,1,0:T(8,128)(2,1)S(1)} %copy-done, ...), custom_call_target="tpu_custom_call" | custom-call | flops 3000000000 | bytes 4000000 | tf_op jit(solution)/shard_map/pallas_call | solution.py:437
  16.5 0.7 %collective-permute-done.6.refs_9_.refs_6_ = bf16[9,24,128]{2,1,0:T(8,128)(2,1)S(1)} collective-permute-done((bf16[9,24,128]{2,1,0:T(8,128)(2,1)S(1)}, bf16[9,24,128]{2,1,0:T(8,128)(2,1)S(1)}, u32[]{:S(2)}, u32[]{:S(2)}) %collective-permute-start.6) | collective-permute-done | bytes 55328 | tf_op jit(solution)/shard_map/ppermute | solution.py:32
  17.1 0.2 collective-permute-done.3.refs_2_
  17.3 0.6 %shard_map.111 = (f32[24,512]{1,0:T(8,128)S(1)}, s32[24,128]{1,0:T(8,128)S(1)}) custom-call(bf16[2,8,24,128]{3,2,1,0:T(8,128)(2,1)S(1)} %collective-permute-done.1.held_ref.refs_0_, bf16[2,8,24,128]{3,2,1,0:T(8,128)(2,1)S(1)} %collective-permute-done.2.held_ref.refs_1_, bf16[2,8,24,128]{3,2,1,0:T(8,128)(2,1)S(1)} %collective-permute-done.3.refs_2_, ...), custom_call_target="tpu_custom_call" | custom-call | flops 3000000000 | bytes 4000000 | tf_op jit(solution)/shard_map/pallas_call | solution.py:443
  18.0 0.0 collective-permute-done.5.refs_3_
  18.0 1.1 %shard_map.112 = (f32[12,2,512]{2,1,0:T(2,128)}, f32[12,2,512]{2,1,0:T(2,128)}) custom-call(bf16[2,8,24,128]{3,2,1,0:T(8,128)(2,1)S(1)} %collective-permute-done.1.held_ref.refs_0_, bf16[2,8,24,128]{3,2,1,0:T(8,128)(2,1)S(1)} %collective-permute-done.2.held_ref.refs_1_, bf16[2,8,24,128]{3,2,1,0:T(8,128)(2,1)S(1)} %collective-permute-done.3.refs_2_, ...), custom_call_target="tpu_custom_call" | custom-call | flops 8000000000 | bytes 4000000 | tf_op jit(solution)/shard_map/pallas_call | solution.py:451
  (18 shorter events, 0.1 us)
Async XLA Ops:
  0.6 0.8 %copy-start.7 = (bf16[12,2,512]{2,1,0:T(2,128)(2,1)S(1)}, bf16[12,2,512]{2,1,0:T(2,128)(2,1)}, u32[]{:S(2)}) copy-start(bf16[12,2,512]{2,1,0:T(2,128)(2,1)} %param.14) | copy-start | bytes 73732
  1.5 3.0 %copy-start.2 = (s32[2,512]{1,0:T(2,128)S(1)}, s32[2,512]{1,0:T(2,128)}, u32[]{:S(2)}) copy-start(s32[2,512]{1,0:T(2,128)} %ends_ref.3) | copy-start | bytes 12292
  1.5 3.4 %copy-start = (bf16[4,4,2,128,128]{4,3,2,1,0:T(8,128)(2,1)S(1)}, bf16[4,4,2,128,128]{4,3,2,1,0:T(8,128)(2,1)}, u32[]{:S(2)}) copy-start(bf16[4,4,2,128,128]{4,3,2,1,0:T(8,128)(2,1)} %refs_5_.1) | copy-start | bytes 3145732
  1.5 5.1 %collective-permute-start = (bf16[2,4,24,128]{3,2,1,0:T(8,128)(2,1)S(1)}, bf16[2,4,24,128]{3,2,1,0:T(8,128)(2,1)S(1)}, u32[]{:S(2)}, u32[]{:S(2)}) collective-permute-start(bf16[2,4,24,128]{3,2,1,0:T(8,128)(2,1)S(1)} %shard_map.104.own_ref.message_ref), channel_id=1, source_target_pairs={{0,2},{2,0},{1,3},{3,1},{4,6},{6,4},{5,7},{7,5},{8,10},{10,8},{9,1... | collective-permute-start | bytes 147464 | tf_op jit(solution)/shard_map/ppermute | solution.py:32
  4.9 6.8 %copy-start.1 = (bf16[4,4,2,128,128]{4,3,2,1,0:T(8,128)(2,1)S(1)}, bf16[4,4,2,128,128]{4,3,2,1,0:T(8,128)(2,1)}, u32[]{:S(2)}) copy-start(bf16[4,4,2,128,128]{4,3,2,1,0:T(8,128)(2,1)} %refs_6_.1) | copy-start | bytes 3145732
  4.9 11.2 %collective-permute-start.4 = (bf16[3,2,2,128,128]{4,3,2,1,0:T(8,128)(2,1)S(1)}, bf16[3,2,2,128,128]{4,3,2,1,0:T(8,128)(2,1)S(1)}, u32[]{:S(2)}, u32[]{:S(2)}) collective-permute-start(bf16[3,2,2,128,128]{4,3,2,1,0:T(8,128)(2,1)S(1)} %shard_map.107), channel_id=1, source_target_pairs={{0,2},{2,0},{1,3},{3,1},{4,6},{6,4},{5,7},{7,5},{8,10},{10,8},{9,1... | collective-permute-start | bytes 1179656 | tf_op jit(solution)/shard_map/ppermute | solution.py:32
  6.6 5.1 %copy-start.4 = (s32[4,4,2]{1,2,0:T(2,128)S(1)}, s32[4,4,2]{1,2,0:T(2,128)}, u32[]{:S(2)}) copy-start(s32[4,4,2]{1,2,0:T(2,128)} %param.12) | copy-start | bytes 388
  6.6 5.1 %copy-start.3 = (s32[4,4,2]{1,2,0:T(2,128)S(1)}, s32[4,4,2]{1,2,0:T(2,128)}, u32[]{:S(2)}) copy-start(s32[4,4,2]{1,2,0:T(2,128)} %param.10) | copy-start | bytes 388
  6.6 8.3 %collective-permute-start.1 = (bf16[2,8,24,128]{3,2,1,0:T(8,128)(2,1)S(1)}, bf16[2,8,24,128]{3,2,1,0:T(8,128)(2,1)S(1)}, u32[]{:S(2)}, u32[]{:S(2)}) collective-permute-start(bf16[2,8,24,128]{3,2,1,0:T(8,128)(2,1)S(1)} %shard_map.105.held_ref.refs_12_.refs_8_), channel_id=1, source_target_pairs={{0,12},{4,8},{8,0},{12,4},{1,13},{5,9},{9,1},{13,5},{2,14},{6,10},... | collective-permute-start | bytes 294920 | tf_op jit(solution)/shard_map/ppermute | solution.py:415
  10.8 5.4 %collective-permute-start.2 = (bf16[2,8,24,128]{3,2,1,0:T(8,128)(2,1)S(1)}, bf16[2,8,24,128]{3,2,1,0:T(8,128)(2,1)S(1)}, u32[]{:S(2)}, u32[]{:S(2)}) collective-permute-start(bf16[2,8,24,128]{3,2,1,0:T(8,128)(2,1)S(1)} %shard_map.105.held_ref.refs_12_.refs_8_), channel_id=1, source_target_pairs={{0,4},{4,0},{8,12},{12,8},{1,5},{5,1},{9,13},{13,9},{2,6},{6,2},{1... | collective-permute-start | bytes 294920 | tf_op jit(solution)/shard_map/ppermute | solution.py:415
  10.8 6.5 %collective-permute-start.3 = (bf16[2,8,24,128]{3,2,1,0:T(8,128)(2,1)S(1)}, bf16[2,8,24,128]{3,2,1,0:T(8,128)(2,1)S(1)}, u32[]{:S(2)}, u32[]{:S(2)}) collective-permute-start(bf16[2,8,24,128]{3,2,1,0:T(8,128)(2,1)S(1)} %shard_map.105.held_ref.refs_12_.refs_8_), channel_id=1, source_target_pairs={{0,8},{4,12},{8,4},{12,0},{1,9},{5,13},{9,5},{13,1},{2,10},{6,14},... | collective-permute-start | bytes 294920 | tf_op jit(solution)/shard_map/ppermute | solution.py:415
  11.7 0.7 %copy-start.5 = (f32[512]{0:T(512)S(1)}, f32[512]{0:T(512)}, u32[]{:S(2)}) copy-start(f32[512]{0:T(512)} %param.16) | copy-start | bytes 6148
  11.7 0.7 %copy-start.6 = (f32[12]{0:T(128)S(1)}, f32[12]{0:T(128)}, u32[]{:S(2)}) copy-start(f32[12]{0:T(128)} %param.15) | copy-start | bytes 148
  12.9 4.2 %collective-permute-start.6 = (bf16[9,24,128]{2,1,0:T(8,128)(2,1)S(1)}, bf16[9,24,128]{2,1,0:T(8,128)(2,1)S(1)}, u32[]{:S(2)}, u32[]{:S(2)}) collective-permute-start(bf16[9,24,128]{2,1,0:T(8,128)(2,1)S(1)} %get-tuple-element.25), channel_id=1, source_target_pairs={{0,2},{2,0},{1,3},{3,1},{4,6},{6,4},{5,7},{7,5},{8,10},{10,8},{9,1... | collective-permute-start | bytes 165896 | tf_op jit(solution)/shard_map/ppermute | solution.py:32
  16.2 1.8 %collective-permute-start.5 = (bf16[3,2,2,128,128]{4,3,2,1,0:T(8,128)(2,1)S(1)}, bf16[3,2,2,128,128]{4,3,2,1,0:T(8,128)(2,1)S(1)}, u32[]{:S(2)}, u32[]{:S(2)}) collective-permute-start(bf16[3,2,2,128,128]{4,3,2,1,0:T(8,128)(2,1)S(1)} %collective-permute-done.4.refs_3_), channel_id=1, source_target_pairs={{0,1},{1,0},{2,3},{3,2},{4,5},{5,4},{6,7},{7,6},{8,9},{9,8},{10,11... | collective-permute-start | bytes 1179656 | tf_op jit(solution)/shard_map/ppermute | solution.py:32

commit v6 on v5

--- a/solution.py
+++ b/solution.py
@@ -16,7 +16,7 @@
 JOIN = 10_000_000
 SMALL = 1_000
 NEXT = 3_000_000
-MAIN = 3_000_000
+MAIN = 1000000
 LAST = 8_000_000
 
 
@@ -184,7 +184,7 @@
 
 def region_moves(regions):
     if regions == 4:
-        return [[3, 2, 0, 1], [1, 0, 3, 2], [2, 3, 1, 0]]
+        return [[2, 3, 0, 1], [3, 2, 1, 0], [1, 0, 3, 2]]
     return [[(place + shift) % regions for place in range(regions)] for shift in range(1, regions)]
 
 

time: 19.3 us -> 19.2 us (level)
  starting transfers between devices: 10.8 us -> 10.5 us
  waiting for transfers between devices: 2.69 us -> 2.9 us
    ppermute x3, starting transfers between devices: 5.08 us -> 4.76 us  [paired_step(): lax.ppermute(held, 'blk', list(enumerate(targets)))]
    ppermute x3, waiting for transfers between devices: 0.18 us -> 0.43 us  [paired_step(): lax.ppermute(held, 'blk', list(enumerate(targets)))]
  transfers between devices with their start and end apart: 7 -> 7, of which waited for: 4 -> 3; matrix products, arithmetic and copies ran while one was open for 0% -> 0% of each run, Pallas kernels for 12% -> 12%
where the time goes in v6:
time: 19.2 us; the launch traced here: 19 us
  starting transfers between devices  10.5 us (55%)
  Pallas kernels  3.3 us (17%)
  waiting for transfers between devices  2.9 us (15%)
  local copies, waits for them, and re-layouts  1.5 us (8%)
  between operations  0.76 us (4%)
    ppermute x4, starting transfers between devices, swapped(): lax.ppermute(array, axis, [(i, i ^ distance) for i in range(lax.axis_size...  5.76 us
    ppermute x3, starting transfers between devices, paired_step(): lax.ppermute(held, 'blk', list(enumerate(targets)))  4.76 us
    ppermute x4, waiting for transfers between devices, swapped(): lax.ppermute(array, axis, [(i, i ^ distance) for i in range(lax.axis_size...  2.47 us
    pallas_call x1, Pallas kernels, paired_step(): kernel_call(functools.partial(last_kernel, regions), (result, result), 'v...  1.08 us
    reshape x2, local copies, waits for them, and re-layouts, blocked(): return array.reshape(rows, row_blocks, block_size).transpose(1, 0, 2)  0.79 us
    unnamed x16, local copies, waits for them, and re-layouts  0.7 us
    pallas_call x1, Pallas kernels, paired_step(): kernel_call(functools.partial(main_kernel, regions), (jax.ShapeDtypeStruc...  0.65 us
    pallas_call x2, Pallas kernels, paired_step(): kernel_call(functools.partial(next_kernel, regions, move), (totals, total...  0.58 us
  transfers between devices with their start and end apart: 7, of which 3 were waited for; matrix products, arithmetic and copies ran while one was open for 0% of the time, Pallas kernels for 12%

profile of v6, /device:TPU:0, one launch (start us, length us, event | category | flops | bytes accessed | tf_op | source)
XLA Modules:
  0.0 19.0 jit_solution(11692074877897252549)
XLA Ops:
  0.6 0.8 %reshape.10 = bf16[24,4,128]{2,1,0:T(4,128)(2,1)S(1)} reshape(bf16[12,2,512]{2,1,0:T(2,128)(2,1)} %param.13) | data formatting | bytes 49152 | tf_op jit(solution)/shard_map/reshape | solution.py:398
  1.5 0.0 copy-start.2
  1.5 0.0 copy-start
  1.5 3.0 %collective-permute-start = (bf16[2,4,24,128]{3,2,1,0:T(8,128)(2,1)S(1)}, bf16[2,4,24,128]{3,2,1,0:T(8,128)(2,1)S(1)}, u32[]{:S(2)}, u32[]{:S(2)}) collective-permute-start(bf16[2,4,24,128]{3,2,1,0:T(8,128)(2,1)S(1)} %shard_map.104.own_ref.message_ref), channel_id=1, source_target_pairs={{0,2},{2,0},{1,3},{3,1},{4,6},{6,4},{5,7},{7,5},{8,10},{10,8},{9,1... | collective-permute-start | bytes 147464 | tf_op jit(solution)/shard_map/ppermute | solution.py:32
  4.5 0.4 %shard_map.106 = (bf16[4,128,512]{2,1,0:T(8,128)(2,1)S(1)}, f32[4,24,128]{2,1,0:T(8,128)S(1)}) custom-call(bf16[2,4,24,128]{3,2,1,0:T(8,128)(2,1)S(1)} %shard_map.104.own_ref.message_ref, s32[2,512]{1,0:T(2,128)S(1)} %copy-done.2), custom_call_target="tpu_custom_call" | custom-call | flops 1000000 | bytes 4000000 | tf_op jit(solution)/shard_map/pallas_call | solution.py:409
  4.9 0.0 copy-start.1
  4.9 0.8 %collective-permute-start.4 = (bf16[3,2,2,128,128]{4,3,2,1,0:T(8,128)(2,1)S(1)}, bf16[3,2,2,128,128]{4,3,2,1,0:T(8,128)(2,1)S(1)}, u32[]{:S(2)}, u32[]{:S(2)}) collective-permute-start(bf16[3,2,2,128,128]{4,3,2,1,0:T(8,128)(2,1)S(1)} %shard_map.107), channel_id=1, source_target_pairs={{0,2},{2,0},{1,3},{3,1},{4,6},{6,4},{5,7},{7,5},{8,10},{10,8},{9,1... | collective-permute-start | bytes 1179656 | tf_op jit(solution)/shard_map/ppermute | solution.py:32
  5.8 0.8 %collective-permute-done.other_ref = bf16[2,4,24,128]{3,2,1,0:T(8,128)(2,1)S(1)} collective-permute-done((bf16[2,4,24,128]{3,2,1,0:T(8,128)(2,1)S(1)}, bf16[2,4,24,128]{3,2,1,0:T(8,128)(2,1)S(1)}, u32[]{:S(2)}, u32[]{:S(2)}) %collective-permute-start) | collective-permute-done | bytes 49184 | tf_op jit(solution)/shard_map/ppermute | solution.py:32
  6.6 0.0 copy-start.3
  6.6 3.2 %collective-permute-start.1 = (bf16[2,8,24,128]{3,2,1,0:T(8,128)(2,1)S(1)}, bf16[2,8,24,128]{3,2,1,0:T(8,128)(2,1)S(1)}, u32[]{:S(2)}, u32[]{:S(2)}) collective-permute-start(bf16[2,8,24,128]{3,2,1,0:T(8,128)(2,1)S(1)} %shard_map.105.held_ref.refs_12_.refs_8_), channel_id=1, source_target_pairs={{0,8},{4,12},{8,0},{12,4},{1,9},{5,13},{9,1},{13,5},{2,10},{6,14},... | collective-permute-start | bytes 294920 | tf_op jit(solution)/shard_map/ppermute | solution.py:415
  9.8 1.3 %collective-permute-start.2 = (bf16[2,8,24,128]{3,2,1,0:T(8,128)(2,1)S(1)}, bf16[2,8,24,128]{3,2,1,0:T(8,128)(2,1)S(1)}, u32[]{:S(2)}, u32[]{:S(2)}) collective-permute-start(bf16[2,8,24,128]{3,2,1,0:T(8,128)(2,1)S(1)} %shard_map.105.held_ref.refs_12_.refs_8_), channel_id=1, source_target_pairs={{0,12},{4,8},{8,4},{12,0},{1,13},{5,9},{9,5},{13,1},{2,14},{6,10},... | collective-permute-start | bytes 294920 | tf_op jit(solution)/shard_map/ppermute | solution.py:415
  11.1 0.2 %collective-permute-start.3 = (bf16[2,8,24,128]{3,2,1,0:T(8,128)(2,1)S(1)}, bf16[2,8,24,128]{3,2,1,0:T(8,128)(2,1)S(1)}, u32[]{:S(2)}, u32[]{:S(2)}) collective-permute-start(bf16[2,8,24,128]{3,2,1,0:T(8,128)(2,1)S(1)} %shard_map.105.held_ref.refs_12_.refs_8_), channel_id=1, source_target_pairs={{0,4},{4,0},{8,12},{12,8},{1,5},{5,1},{9,13},{13,9},{2,6},{6,2},{1... | collective-permute-start | bytes 294920 | tf_op jit(solution)/shard_map/ppermute | solution.py:415
  11.4 0.7 %copy-done.5 = f32[512]{0:T(512)S(1)} copy-done((f32[512]{0:T(512)S(1)}, f32[512]{0:T(512)}, u32[]{:S(2)}) %copy-start.5) | copy-done | bytes 2072
  12.0 0.6 %shard_map.108 = (f32[5,24,128]{2,1,0:T(8,128)S(1)}, s32[2,4,4,2,128]{4,3,2,1,0:T(2,128)S(1)}, f32[4,24,128]{2,1,0:T(8,128)S(1)}, f32[4,24,128]{2,1,0:T(8,128)S(...) custom-call(bf16[2,8,24,128]{3,2,1,0:T(8,128)(2,1)S(1)} %shard_map.105.held_ref.refs_12_.refs_8_, ...), custom_call_target="tpu_custom_call" | custom-call | flops 1000000 | bytes 4000000 | tf_op jit(solution)/shard_map/pallas_call | solution.py:418
  12.6 1.9 %collective-permute-start.6 = (bf16[9,24,128]{2,1,0:T(8,128)(2,1)S(1)}, bf16[9,24,128]{2,1,0:T(8,128)(2,1)S(1)}, u32[]{:S(2)}, u32[]{:S(2)}) collective-permute-start(bf16[9,24,128]{2,1,0:T(8,128)(2,1)S(1)} %get-tuple-element.25), channel_id=1, source_target_pairs={{0,2},{2,0},{1,3},{3,1},{4,6},{6,4},{5,7},{7,5},{8,10},{10,8},{9,1... | collective-permute-start | bytes 165896 | tf_op jit(solution)/shard_map/ppermute | solution.py:32
  14.6 1.6 %collective-permute-done.4.refs_3_ = bf16[3,2,2,128,128]{4,3,2,1,0:T(8,128)(2,1)S(1)} collective-permute-done((bf16[3,2,2,128,128]{4,3,2,1,0:T(8,128)(2,1)S(1)}, bf16[3,2,2,128,128]{4,3,2,1,0:T(8,128)(2,1)S(1)}, u32[]{:S(2)}, u32[]{:S(2)}) %collective-permute-start.4) | collective-permute-done | bytes 393248 | tf_op jit(solution)/shard_map/ppermute | solution.py:32
  16.2 0.0 collective-permute-start.5
  16.2 0.3 %shard_map.109 = (f32[4,24,128]{2,1,0:T(8,128)S(1)}, f32[4,24,128]{2,1,0:T(8,128)S(1)}) custom-call(s32[2,4,4,2,128]{4,3,2,1,0:T(2,128)S(1)} %get-tuple-element.17.table_ref.refs_4_, bf16[2,8,24,128]{3,2,1,0:T(8,128)(2,1)S(1)} %collective-permute-done.1.held_ref.refs_0_, bf16[4,4,2,128,128]{4,3,2,1,0:T(8,128)(2,1)S(1)} %copy-done, ...), custom_call_target="tpu_custom_call" | custom-call | flops 3000000000 | bytes 4000000 | tf_op jit(solution)/shard_map/pallas_call | solution.py:437
  16.5 0.4 %collective-permute-done.2.held_ref.refs_1_ = bf16[2,8,24,128]{3,2,1,0:T(8,128)(2,1)S(1)} collective-permute-done((bf16[2,8,24,128]{3,2,1,0:T(8,128)(2,1)S(1)}, bf16[2,8,24,128]{3,2,1,0:T(8,128)(2,1)S(1)}, u32[]{:S(2)}, u32[]{:S(2)}) %collective-permute-start.2) | collective-permute-done | bytes 98336 | tf_op jit(solution)/shard_map/ppermute | solution.py:415
  16.9 0.3 %shard_map.110 = (f32[4,24,128]{2,1,0:T(8,128)S(1)}, f32[4,24,128]{2,1,0:T(8,128)S(1)}) custom-call(s32[2,4,4,2,128]{4,3,2,1,0:T(2,128)S(1)} %get-tuple-element.17.table_ref.refs_4_, bf16[2,8,24,128]{3,2,1,0:T(8,128)(2,1)S(1)} %collective-permute-done.2.held_ref.refs_1_, bf16[4,4,2,128,128]{4,3,2,1,0:T(8,128)(2,1)S(1)} %copy-done, ...), custom_call_target="tpu_custom_call" | custom-call | flops 3000000000 | bytes 4000000 | tf_op jit(solution)/shard_map/pallas_call | solution.py:437
  17.2 0.0 collective-permute-done.3.refs_2_
  17.2 0.6 %shard_map.111 = (f32[24,512]{1,0:T(8,128)S(1)}, s32[24,128]{1,0:T(8,128)S(1)}) custom-call(bf16[2,8,24,128]{3,2,1,0:T(8,128)(2,1)S(1)} %collective-permute-done.1.held_ref.refs_0_, bf16[2,8,24,128]{3,2,1,0:T(8,128)(2,1)S(1)} %collective-permute-done.2.held_ref.refs_1_, bf16[2,8,24,128]{3,2,1,0:T(8,128)(2,1)S(1)} %collective-permute-done.3.refs_2_, ...), custom_call_target="tpu_custom_call" | custom-call | flops 1000000000 | bytes 4000000 | tf_op jit(solution)/shard_map/pallas_call | solution.py:443
  17.9 0.0 collective-permute-done.5.refs_3_
  17.9 1.1 %shard_map.112 = (f32[12,2,512]{2,1,0:T(2,128)}, f32[12,2,512]{2,1,0:T(2,128)}) custom-call(bf16[2,8,24,128]{3,2,1,0:T(8,128)(2,1)S(1)} %collective-permute-done.1.held_ref.refs_0_, bf16[2,8,24,128]{3,2,1,0:T(8,128)(2,1)S(1)} %collective-permute-done.2.held_ref.refs_1_, bf16[2,8,24,128]{3,2,1,0:T(8,128)(2,1)S(1)} %collective-permute-done.3.refs_2_, ...), custom_call_target="tpu_custom_call" | custom-call | flops 8000000000 | bytes 4000000 | tf_op jit(solution)/shard_map/pallas_call | solution.py:451
  (18 shorter events, 0.1 us)
Async XLA Ops:
  0.6 0.8 %copy-start.7 = (bf16[12,2,512]{2,1,0:T(2,128)(2,1)S(1)}, bf16[12,2,512]{2,1,0:T(2,128)(2,1)}, u32[]{:S(2)}) copy-start(bf16[12,2,512]{2,1,0:T(2,128)(2,1)} %param.14) | copy-start | bytes 73732
  1.5 3.0 %copy-start.2 = (s32[2,512]{1,0:T(2,128)S(1)}, s32[2,512]{1,0:T(2,128)}, u32[]{:S(2)}) copy-start(s32[2,512]{1,0:T(2,128)} %ends_ref.3) | copy-start | bytes 12292
  1.5 3.4 %copy-start = (bf16[4,4,2,128,128]{4,3,2,1,0:T(8,128)(2,1)S(1)}, bf16[4,4,2,128,128]{4,3,2,1,0:T(8,128)(2,1)}, u32[]{:S(2)}) copy-start(bf16[4,4,2,128,128]{4,3,2,1,0:T(8,128)(2,1)} %refs_5_.1) | copy-start | bytes 3145732
  1.5 5.1 %collective-permute-start = (bf16[2,4,24,128]{3,2,1,0:T(8,128)(2,1)S(1)}, bf16[2,4,24,128]{3,2,1,0:T(8,128)(2,1)S(1)}, u32[]{:S(2)}, u32[]{:S(2)}) collective-permute-start(bf16[2,4,24,128]{3,2,1,0:T(8,128)(2,1)S(1)} %shard_map.104.own_ref.message_ref), channel_id=1, source_target_pairs={{0,2},{2,0},{1,3},{3,1},{4,6},{6,4},{5,7},{7,5},{8,10},{10,8},{9,1... | collective-permute-start | bytes 147464 | tf_op jit(solution)/shard_map/ppermute | solution.py:32
  4.9 6.4 %copy-start.1 = (bf16[4,4,2,128,128]{4,3,2,1,0:T(8,128)(2,1)S(1)}, bf16[4,4,2,128,128]{4,3,2,1,0:T(8,128)(2,1)}, u32[]{:S(2)}) copy-start(bf16[4,4,2,128,128]{4,3,2,1,0:T(8,128)(2,1)} %refs_6_.1) | copy-start | bytes 3145732
  4.9 11.2 %collective-permute-start.4 = (bf16[3,2,2,128,128]{4,3,2,1,0:T(8,128)(2,1)S(1)}, bf16[3,2,2,128,128]{4,3,2,1,0:T(8,128)(2,1)S(1)}, u32[]{:S(2)}, u32[]{:S(2)}) collective-permute-start(bf16[3,2,2,128,128]{4,3,2,1,0:T(8,128)(2,1)S(1)} %shard_map.107), channel_id=1, source_target_pairs={{0,2},{2,0},{1,3},{3,1},{4,6},{6,4},{5,7},{7,5},{8,10},{10,8},{9,1... | collective-permute-start | bytes 1179656 | tf_op jit(solution)/shard_map/ppermute | solution.py:32
  6.6 4.8 %copy-start.4 = (s32[4,4,2]{1,2,0:T(2,128)S(1)}, s32[4,4,2]{1,2,0:T(2,128)}, u32[]{:S(2)}) copy-start(s32[4,4,2]{1,2,0:T(2,128)} %param.12) | copy-start | bytes 388
  6.6 4.8 %copy-start.3 = (s32[4,4,2]{1,2,0:T(2,128)S(1)}, s32[4,4,2]{1,2,0:T(2,128)}, u32[]{:S(2)}) copy-start(s32[4,4,2]{1,2,0:T(2,128)} %param.10) | copy-start | bytes 388
  6.6 9.6 %collective-permute-start.1 = (bf16[2,8,24,128]{3,2,1,0:T(8,128)(2,1)S(1)}, bf16[2,8,24,128]{3,2,1,0:T(8,128)(2,1)S(1)}, u32[]{:S(2)}, u32[]{:S(2)}) collective-permute-start(bf16[2,8,24,128]{3,2,1,0:T(8,128)(2,1)S(1)} %shard_map.105.held_ref.refs_12_.refs_8_), channel_id=1, source_target_pairs={{0,8},{4,12},{8,0},{12,4},{1,9},{5,13},{9,1},{13,5},{2,10},{6,14},... | collective-permute-start | bytes 294920 | tf_op jit(solution)/shard_map/ppermute | solution.py:415
  9.8 7.1 %collective-permute-start.2 = (bf16[2,8,24,128]{3,2,1,0:T(8,128)(2,1)S(1)}, bf16[2,8,24,128]{3,2,1,0:T(8,128)(2,1)S(1)}, u32[]{:S(2)}, u32[]{:S(2)}) collective-permute-start(bf16[2,8,24,128]{3,2,1,0:T(8,128)(2,1)S(1)} %shard_map.105.held_ref.refs_12_.refs_8_), channel_id=1, source_target_pairs={{0,12},{4,8},{8,4},{12,0},{1,13},{5,9},{9,5},{13,1},{2,14},{6,10},... | collective-permute-start | bytes 294920 | tf_op jit(solution)/shard_map/ppermute | solution.py:415
  11.1 6.1 %collective-permute-start.3 = (bf16[2,8,24,128]{3,2,1,0:T(8,128)(2,1)S(1)}, bf16[2,8,24,128]{3,2,1,0:T(8,128)(2,1)S(1)}, u32[]{:S(2)}, u32[]{:S(2)}) collective-permute-start(bf16[2,8,24,128]{3,2,1,0:T(8,128)(2,1)S(1)} %shard_map.105.held_ref.refs_12_.refs_8_), channel_id=1, source_target_pairs={{0,4},{4,0},{8,12},{12,8},{1,5},{5,1},{9,13},{13,9},{2,6},{6,2},{1... | collective-permute-start | bytes 294920 | tf_op jit(solution)/shard_map/ppermute | solution.py:415
  11.4 0.7 %copy-start.5 = (f32[512]{0:T(512)S(1)}, f32[512]{0:T(512)}, u32[]{:S(2)}) copy-start(f32[512]{0:T(512)} %param.16) | copy-start | bytes 6148
  11.4 0.7 %copy-start.6 = (f32[12]{0:T(128)S(1)}, f32[12]{0:T(128)}, u32[]{:S(2)}) copy-start(f32[12]{0:T(128)} %param.15) | copy-start | bytes 148
  12.6 4.6 %collective-permute-start.6 = (bf16[9,24,128]{2,1,0:T(8,128)(2,1)S(1)}, bf16[9,24,128]{2,1,0:T(8,128)(2,1)S(1)}, u32[]{:S(2)}, u32[]{:S(2)}) collective-permute-start(bf16[9,24,128]{2,1,0:T(8,128)(2,1)S(1)} %get-tuple-element.25), channel_id=1, source_target_pairs={{0,2},{2,0},{1,3},{3,1},{4,6},{6,4},{5,7},{7,5},{8,10},{10,8},{9,1... | collective-permute-start | bytes 165896 | tf_op jit(solution)/shard_map/ppermute | solution.py:32
  16.2 1.7 %collective-permute-start.5 = (bf16[3,2,2,128,128]{4,3,2,1,0:T(8,128)(2,1)S(1)}, bf16[3,2,2,128,128]{4,3,2,1,0:T(8,128)(2,1)S(1)}, u32[]{:S(2)}, u32[]{:S(2)}) collective-permute-start(bf16[3,2,2,128,128]{4,3,2,1,0:T(8,128)(2,1)S(1)} %collective-permute-done.4.refs_3_), channel_id=1, source_target_pairs={{0,1},{1,0},{2,3},{3,2},{4,5},{5,4},{6,7},{7,6},{8,9},{9,8},{10,11... | collective-permute-start | bytes 1179656 | tf_op jit(solution)/shard_map/ppermute | solution.py:32

commit v7 on v6

--- a/solution.py
+++ b/solution.py
@@ -316,10 +316,12 @@
         out_ref[freq, :, columns] = array[2 * freq : 2 * freq + 2]
 
 
-def other_rows(part, slab_ref, numbers_ref, early_ref, piece_refs, other_ref):
+def other_drop(part, slab_ref, numbers_ref, early_ref, piece_refs, matrix_ref):
     half, slots = slab_ref.shape[1:3]
+    start = (lax.axis_index("col") ^ part) * half
+    rows = []
     for position in range(half):
-        row = (lax.axis_index("col") ^ part) * half + position
+        row = start + position
         total = early_ref[row].astype(jnp.float32)
         for at, piece_ref in enumerate(piece_refs):
             total += pair_dot(
@@ -327,20 +329,15 @@
                 [numbers_ref[row * slots + slot, at + 1] for slot in range(slots)],
                 [slab_ref[at, position, slot] for slot in range(slots)],
             )
-        other_ref[row] = total.astype(jnp.bfloat16)
-
-
-def other_drop(part, half, other_ref, matrix_ref):
-    start = (lax.axis_index("col") ^ part) * half
-    rows = lanes([other_ref[start + position] for position in range(half)])
-    matrix = matrix_ref[pl.ds(start, half)].reshape(rows.shape[1], -1)
-    return lax.dot_general(rows, matrix, NN, preferred_element_type=jnp.float32)
+        rows.append(total.astype(jnp.bfloat16))
+    matrix = matrix_ref[pl.ds(start, half)].reshape(half * matrix_ref.shape[1], -1)
+    return lax.dot_general(lanes(rows), matrix, NN, preferred_element_type=jnp.float32)
 
 
 def main_kernel(regions, *refs):
     piece_refs = refs[: regions - 1]
     (mine_ref, table_ref, p_ref, l_ref, p_in_ref, f_in_ref, early_ref, matrix_ref, other_matrix_ref, held_ref,
-     factor_ref, out_ref, numbers_ref, other_ref) = refs[regions - 1 :]
+     factor_ref, out_ref, numbers_ref) = refs[regions - 1 :]
     row_blocks, _, block_size = p_in_ref.shape
     numbers_ref[...] = early_ref[2 * row_blocks].astype(jnp.float32).astype(jnp.int32)
     potentials, fluxes = [], []
@@ -348,10 +345,9 @@
         potential, flux = region_terms(regions, regions - 1, table_ref, piece_refs[-1], p_ref, l_ref, row)
         potentials.append((p_in_ref[row] + potential).astype(jnp.bfloat16))
         fluxes.append(f_in_ref[row] + flux)
-    other_rows(0, mine_ref, numbers_ref, early_ref, piece_refs, other_ref)
+    drop = other_drop(0, mine_ref, numbers_ref, early_ref, piece_refs, other_matrix_ref)
     matrix = matrix_ref[...].reshape(row_blocks * block_size, -1)
-    drop = lax.dot_general(lanes(potentials), matrix, NN, preferred_element_type=jnp.float32)
-    drop += other_drop(0, row_blocks // 2, other_ref, other_matrix_ref)
+    drop += lax.dot_general(lanes(potentials), matrix, NN, preferred_element_type=jnp.float32)
     for row in range(row_blocks):
         columns = slice(row * block_size, (row + 1) * block_size)
         current = held_ref[1, row].astype(jnp.float32)
@@ -362,10 +358,9 @@
 def last_kernel(regions, *refs):
     piece_refs = refs[: regions - 1]
     (theirs_ref, numbers_ref, begun_ref, early_ref, matrix_ref, held_ref, outflow_ref, factor_ref,
-     cell_ref, panel_ref, other_ref) = refs[regions - 1 :]
+     cell_ref, panel_ref) = refs[regions - 1 :]
     row_blocks, _, block_size = outflow_ref.shape
-    other_rows(1, theirs_ref, numbers_ref, early_ref, piece_refs, other_ref)
-    total = begun_ref[...] + other_drop(1, row_blocks // 2, other_ref, matrix_ref)
+    total = begun_ref[...] + other_drop(1, theirs_ref, numbers_ref, early_ref, piece_refs, matrix_ref)
     for row in range(row_blocks):
         columns = slice(row * block_size, (row + 1) * block_size)
         store_rows(cell_ref, columns, total[:, columns])
@@ -439,17 +434,15 @@
         )(table, piece, p_blocks, l_blocks, potential, flux, matrix)
 
     numbers_shape = jax.ShapeDtypeStruct((rows, block_size), jnp.int32)
-    other_scratch = pltpu.VMEM((row_blocks, rows, block_size), jnp.bfloat16)
     begun, numbers = kernel_call(
         functools.partial(main_kernel, regions),
         (jax.ShapeDtypeStruct((rows, share), jnp.float32), numbers_shape),
         "v" * (10 + regions),
         MAIN,
-        [other_scratch],
     )(*pieces, mine, table, p_blocks, l_blocks, potential, flux, early, matrix, other_matrix, held, factors)
     result = jax.ShapeDtypeStruct(charges.shape, jnp.float32)
     return kernel_call(
-        functools.partial(last_kernel, regions), (result, result), "v" * (7 + regions), LAST, [other_scratch]
+        functools.partial(last_kernel, regions), (result, result), "v" * (7 + regions), LAST
     )(*pieces, theirs, numbers, begun, early, other_matrix, held, outflow, factors)
 
 

time: 19.2 us -> 19.2 us (level)
  transfers between devices with their start and end apart: 7 -> 7, of which waited for: 3 -> 4; matrix products, arithmetic and copies ran while one was open for 0% -> 0% of each run, Pallas kernels for 12% -> 11%
where the time goes in v7:
time: 19.2 us; the launch traced here: 19 us
  starting transfers between devices  10.5 us (55%)
  Pallas kernels  3.21 us (17%)
  waiting for transfers between devices  2.97 us (15%)
  local copies, waits for them, and re-layouts  1.5 us (8%)
  between operations  0.76 us (4%)
    ppermute x4, starting transfers between devices, swapped(): lax.ppermute(array, axis, [(i, i ^ distance) for i in range(lax.axis_size...  5.76 us
    ppermute x3, starting transfers between devices, paired_step(): lax.ppermute(held, 'blk', list(enumerate(targets)))  4.76 us
    ppermute x4, waiting for transfers between devices, swapped(): lax.ppermute(array, axis, [(i, i ^ distance) for i in range(lax.axis_size...  2.55 us
    pallas_call x1, Pallas kernels, paired_step(): kernel_call(functools.partial(last_kernel, regions), (result, result), 'v...  1.06 us
    reshape x2, local copies, waits for them, and re-layouts, blocked(): return array.reshape(rows, row_blocks, block_size).transpose(1, 0, 2)  0.79 us
    unnamed x16, local copies, waits for them, and re-layouts  0.7 us
    pallas_call x2, Pallas kernels, paired_step(): kernel_call(functools.partial(next_kernel, regions, move), (totals, total...  0.58 us
    pallas_call x1, Pallas kernels, paired_step(): kernel_call(functools.partial(main_kernel, regions), (jax.ShapeDtypeStruc...  0.57 us
  transfers between devices with their start and end apart: 7, of which 4 were waited for; matrix products, arithmetic and copies ran while one was open for 0% of the time, Pallas kernels for 11%

profile of v7, /device:TPU:0, one launch (start us, length us, event | category | flops | bytes accessed | tf_op | source)
XLA Modules:
  0.0 19.0 jit_solution(16982323877873725485)
XLA Ops:
  0.6 0.8 %reshape.10 = bf16[24,4,128]{2,1,0:T(4,128)(2,1)S(1)} reshape(bf16[12,2,512]{2,1,0:T(2,128)(2,1)} %param.13) | data formatting | bytes 49152 | tf_op jit(solution)/shard_map/reshape | solution.py:393
  1.5 0.0 copy-start.2
  1.5 0.0 copy-start
  1.5 3.0 %collective-permute-start = (bf16[2,4,24,128]{3,2,1,0:T(8,128)(2,1)S(1)}, bf16[2,4,24,128]{3,2,1,0:T(8,128)(2,1)S(1)}, u32[]{:S(2)}, u32[]{:S(2)}) collective-permute-start(bf16[2,4,24,128]{3,2,1,0:T(8,128)(2,1)S(1)} %shard_map.104.own_ref.message_ref), channel_id=1, source_target_pairs={{0,2},{2,0},{1,3},{3,1},{4,6},{6,4},{5,7},{7,5},{8,10},{10,8},{9,1... | collective-permute-start | bytes 147464 | tf_op jit(solution)/shard_map/ppermute | solution.py:32
  4.5 0.4 %shard_map.106 = (bf16[4,128,512]{2,1,0:T(8,128)(2,1)S(1)}, f32[4,24,128]{2,1,0:T(8,128)S(1)}) custom-call(bf16[2,4,24,128]{3,2,1,0:T(8,128)(2,1)S(1)} %shard_map.104.own_ref.message_ref, s32[2,512]{1,0:T(2,128)S(1)} %copy-done.2), custom_call_target="tpu_custom_call" | custom-call | flops 1000000 | bytes 4000000 | tf_op jit(solution)/shard_map/pallas_call | solution.py:404
  4.9 0.0 copy-start.1
  4.9 0.8 %collective-permute-start.4 = (bf16[3,2,2,128,128]{4,3,2,1,0:T(8,128)(2,1)S(1)}, bf16[3,2,2,128,128]{4,3,2,1,0:T(8,128)(2,1)S(1)}, u32[]{:S(2)}, u32[]{:S(2)}) collective-permute-start(bf16[3,2,2,128,128]{4,3,2,1,0:T(8,128)(2,1)S(1)} %shard_map.107), channel_id=1, source_target_pairs={{0,2},{2,0},{1,3},{3,1},{4,6},{6,4},{5,7},{7,5},{8,10},{10,8},{9,1... | collective-permute-start | bytes 1179656 | tf_op jit(solution)/shard_map/ppermute | solution.py:32
  5.8 0.8 %collective-permute-done.other_ref = bf16[2,4,24,128]{3,2,1,0:T(8,128)(2,1)S(1)} collective-permute-done((bf16[2,4,24,128]{3,2,1,0:T(8,128)(2,1)S(1)}, bf16[2,4,24,128]{3,2,1,0:T(8,128)(2,1)S(1)}, u32[]{:S(2)}, u32[]{:S(2)}) %collective-permute-start) | collective-permute-done | bytes 49184 | tf_op jit(solution)/shard_map/ppermute | solution.py:32
  6.6 0.0 copy-start.3
  6.6 3.2 %collective-permute-start.1 = (bf16[2,8,24,128]{3,2,1,0:T(8,128)(2,1)S(1)}, bf16[2,8,24,128]{3,2,1,0:T(8,128)(2,1)S(1)}, u32[]{:S(2)}, u32[]{:S(2)}) collective-permute-start(bf16[2,8,24,128]{3,2,1,0:T(8,128)(2,1)S(1)} %shard_map.105.held_ref.refs_12_.refs_8_), channel_id=1, source_target_pairs={{0,8},{4,12},{8,0},{12,4},{1,9},{5,13},{9,1},{13,5},{2,10},{6,14},... | collective-permute-start | bytes 294920 | tf_op jit(solution)/shard_map/ppermute | solution.py:410
  9.8 1.3 %collective-permute-start.2 = (bf16[2,8,24,128]{3,2,1,0:T(8,128)(2,1)S(1)}, bf16[2,8,24,128]{3,2,1,0:T(8,128)(2,1)S(1)}, u32[]{:S(2)}, u32[]{:S(2)}) collective-permute-start(bf16[2,8,24,128]{3,2,1,0:T(8,128)(2,1)S(1)} %shard_map.105.held_ref.refs_12_.refs_8_), channel_id=1, source_target_pairs={{0,12},{4,8},{8,4},{12,0},{1,13},{5,9},{9,5},{13,1},{2,14},{6,10},... | collective-permute-start | bytes 294920 | tf_op jit(solution)/shard_map/ppermute | solution.py:410
  11.1 0.2 %collective-permute-start.3 = (bf16[2,8,24,128]{3,2,1,0:T(8,128)(2,1)S(1)}, bf16[2,8,24,128]{3,2,1,0:T(8,128)(2,1)S(1)}, u32[]{:S(2)}, u32[]{:S(2)}) collective-permute-start(bf16[2,8,24,128]{3,2,1,0:T(8,128)(2,1)S(1)} %shard_map.105.held_ref.refs_12_.refs_8_), channel_id=1, source_target_pairs={{0,4},{4,0},{8,12},{12,8},{1,5},{5,1},{9,13},{13,9},{2,6},{6,2},{1... | collective-permute-start | bytes 294920 | tf_op jit(solution)/shard_map/ppermute | solution.py:410
  11.4 0.7 %copy-done.5 = f32[512]{0:T(512)S(1)} copy-done((f32[512]{0:T(512)S(1)}, f32[512]{0:T(512)}, u32[]{:S(2)}) %copy-start.5) | copy-done | bytes 2072
  12.0 0.6 %shard_map.108 = (f32[5,24,128]{2,1,0:T(8,128)S(1)}, s32[2,4,4,2,128]{4,3,2,1,0:T(2,128)S(1)}, f32[4,24,128]{2,1,0:T(8,128)S(1)}, f32[4,24,128]{2,1,0:T(8,128)S(...) custom-call(bf16[2,8,24,128]{3,2,1,0:T(8,128)(2,1)S(1)} %shard_map.105.held_ref.refs_12_.refs_8_, ...), custom_call_target="tpu_custom_call" | custom-call | flops 1000000 | bytes 4000000 | tf_op jit(solution)/shard_map/pallas_call | solution.py:413
  12.6 1.9 %collective-permute-start.6 = (bf16[9,24,128]{2,1,0:T(8,128)(2,1)S(1)}, bf16[9,24,128]{2,1,0:T(8,128)(2,1)S(1)}, u32[]{:S(2)}, u32[]{:S(2)}) collective-permute-start(bf16[9,24,128]{2,1,0:T(8,128)(2,1)S(1)} %get-tuple-element.25), channel_id=1, source_target_pairs={{0,2},{2,0},{1,3},{3,1},{4,6},{6,4},{5,7},{7,5},{8,10},{10,8},{9,1... | collective-permute-start | bytes 165896 | tf_op jit(solution)/shard_map/ppermute | solution.py:32
  14.6 1.6 %collective-permute-done.4.refs_3_ = bf16[3,2,2,128,128]{4,3,2,1,0:T(8,128)(2,1)S(1)} collective-permute-done((bf16[3,2,2,128,128]{4,3,2,1,0:T(8,128)(2,1)S(1)}, bf16[3,2,2,128,128]{4,3,2,1,0:T(8,128)(2,1)S(1)}, u32[]{:S(2)}, u32[]{:S(2)}) %collective-permute-start.4) | collective-permute-done | bytes 393248 | tf_op jit(solution)/shard_map/ppermute | solution.py:32
  16.2 0.0 collective-permute-start.5
  16.2 0.3 %shard_map.109 = (f32[4,24,128]{2,1,0:T(8,128)S(1)}, f32[4,24,128]{2,1,0:T(8,128)S(1)}) custom-call(s32[2,4,4,2,128]{4,3,2,1,0:T(2,128)S(1)} %get-tuple-element.17.table_ref.refs_4_, bf16[2,8,24,128]{3,2,1,0:T(8,128)(2,1)S(1)} %collective-permute-done.1.held_ref.refs_0_, bf16[4,4,2,128,128]{4,3,2,1,0:T(8,128)(2,1)S(1)} %copy-done, ...), custom_call_target="tpu_custom_call" | custom-call | flops 3000000000 | bytes 4000000 | tf_op jit(solution)/shard_map/pallas_call | solution.py:432
  16.5 0.4 %collective-permute-done.2.held_ref.refs_1_ = bf16[2,8,24,128]{3,2,1,0:T(8,128)(2,1)S(1)} collective-permute-done((bf16[2,8,24,128]{3,2,1,0:T(8,128)(2,1)S(1)}, bf16[2,8,24,128]{3,2,1,0:T(8,128)(2,1)S(1)}, u32[]{:S(2)}, u32[]{:S(2)}) %collective-permute-start.2) | collective-permute-done | bytes 98336 | tf_op jit(solution)/shard_map/ppermute | solution.py:410
  16.9 0.3 %shard_map.110 = (f32[4,24,128]{2,1,0:T(8,128)S(1)}, f32[4,24,128]{2,1,0:T(8,128)S(1)}) custom-call(s32[2,4,4,2,128]{4,3,2,1,0:T(2,128)S(1)} %get-tuple-element.17.table_ref.refs_4_, bf16[2,8,24,128]{3,2,1,0:T(8,128)(2,1)S(1)} %collective-permute-done.2.held_ref.refs_1_, bf16[4,4,2,128,128]{4,3,2,1,0:T(8,128)(2,1)S(1)} %copy-done, ...), custom_call_target="tpu_custom_call" | custom-call | flops 3000000000 | bytes 4000000 | tf_op jit(solution)/shard_map/pallas_call | solution.py:432
  17.2 0.0 collective-permute-done.3.refs_2_
  17.2 0.6 %shard_map.111 = (f32[24,512]{1,0:T(8,128)S(1)}, s32[24,128]{1,0:T(8,128)S(1)}) custom-call(bf16[2,8,24,128]{3,2,1,0:T(8,128)(2,1)S(1)} %collective-permute-done.1.held_ref.refs_0_, bf16[2,8,24,128]{3,2,1,0:T(8,128)(2,1)S(1)} %collective-permute-done.2.held_ref.refs_1_, bf16[2,8,24,128]{3,2,1,0:T(8,128)(2,1)S(1)} %collective-permute-done.3.refs_2_, ...), custom_call_target="tpu_custom_call" | custom-call | flops 1000000000 | bytes 4000000 | tf_op jit(solution)/shard_map/pallas_call | solution.py:437
  17.8 0.1 collective-permute-done.5.refs_3_
  17.9 1.1 %shard_map.112 = (f32[12,2,512]{2,1,0:T(2,128)}, f32[12,2,512]{2,1,0:T(2,128)}) custom-call(bf16[2,8,24,128]{3,2,1,0:T(8,128)(2,1)S(1)} %collective-permute-done.1.held_ref.refs_0_, bf16[2,8,24,128]{3,2,1,0:T(8,128)(2,1)S(1)} %collective-permute-done.2.held_ref.refs_1_, bf16[2,8,24,128]{3,2,1,0:T(8,128)(2,1)S(1)} %collective-permute-done.3.refs_2_, ...), custom_call_target="tpu_custom_call" | custom-call | flops 8000000000 | bytes 4000000 | tf_op jit(solution)/shard_map/pallas_call | solution.py:444
  (18 shorter events, 0.1 us)
Async XLA Ops:
  0.6 0.8 %copy-start.7 = (bf16[12,2,512]{2,1,0:T(2,128)(2,1)S(1)}, bf16[12,2,512]{2,1,0:T(2,128)(2,1)}, u32[]{:S(2)}) copy-start(bf16[12,2,512]{2,1,0:T(2,128)(2,1)} %param.14) | copy-start | bytes 73732
  1.5 3.0 %copy-start.2 = (s32[2,512]{1,0:T(2,128)S(1)}, s32[2,512]{1,0:T(2,128)}, u32[]{:S(2)}) copy-start(s32[2,512]{1,0:T(2,128)} %ends_ref.3) | copy-start | bytes 12292
  1.5 3.4 %copy-start = (bf16[4,4,2,128,128]{4,3,2,1,0:T(8,128)(2,1)S(1)}, bf16[4,4,2,128,128]{4,3,2,1,0:T(8,128)(2,1)}, u32[]{:S(2)}) copy-start(bf16[4,4,2,128,128]{4,3,2,1,0:T(8,128)(2,1)} %refs_5_.1) | copy-start | bytes 3145732
  1.5 5.1 %collective-permute-start = (bf16[2,4,24,128]{3,2,1,0:T(8,128)(2,1)S(1)}, bf16[2,4,24,128]{3,2,1,0:T(8,128)(2,1)S(1)}, u32[]{:S(2)}, u32[]{:S(2)}) collective-permute-start(bf16[2,4,24,128]{3,2,1,0:T(8,128)(2,1)S(1)} %shard_map.104.own_ref.message_ref), channel_id=1, source_target_pairs={{0,2},{2,0},{1,3},{3,1},{4,6},{6,4},{5,7},{7,5},{8,10},{10,8},{9,1... | collective-permute-start | bytes 147464 | tf_op jit(solution)/shard_map/ppermute | solution.py:32
  4.9 6.4 %copy-start.1 = (bf16[4,4,2,128,128]{4,3,2,1,0:T(8,128)(2,1)S(1)}, bf16[4,4,2,128,128]{4,3,2,1,0:T(8,128)(2,1)}, u32[]{:S(2)}) copy-start(bf16[4,4,2,128,128]{4,3,2,1,0:T(8,128)(2,1)} %refs_6_.1) | copy-start | bytes 3145732
  4.9 11.2 %collective-permute-start.4 = (bf16[3,2,2,128,128]{4,3,2,1,0:T(8,128)(2,1)S(1)}, bf16[3,2,2,128,128]{4,3,2,1,0:T(8,128)(2,1)S(1)}, u32[]{:S(2)}, u32[]{:S(2)}) collective-permute-start(bf16[3,2,2,128,128]{4,3,2,1,0:T(8,128)(2,1)S(1)} %shard_map.107), channel_id=1, source_target_pairs={{0,2},{2,0},{1,3},{3,1},{4,6},{6,4},{5,7},{7,5},{8,10},{10,8},{9,1... | collective-permute-start | bytes 1179656 | tf_op jit(solution)/shard_map/ppermute | solution.py:32
  6.6 4.8 %copy-start.4 = (s32[4,4,2]{1,2,0:T(2,128)S(1)}, s32[4,4,2]{1,2,0:T(2,128)}, u32[]{:S(2)}) copy-start(s32[4,4,2]{1,2,0:T(2,128)} %param.12) | copy-start | bytes 388
  6.6 4.8 %copy-start.3 = (s32[4,4,2]{1,2,0:T(2,128)S(1)}, s32[4,4,2]{1,2,0:T(2,128)}, u32[]{:S(2)}) copy-start(s32[4,4,2]{1,2,0:T(2,128)} %param.10) | copy-start | bytes 388
  6.6 9.6 %collective-permute-start.1 = (bf16[2,8,24,128]{3,2,1,0:T(8,128)(2,1)S(1)}, bf16[2,8,24,128]{3,2,1,0:T(8,128)(2,1)S(1)}, u32[]{:S(2)}, u32[]{:S(2)}) collective-permute-start(bf16[2,8,24,128]{3,2,1,0:T(8,128)(2,1)S(1)} %shard_map.105.held_ref.refs_12_.refs_8_), channel_id=1, source_target_pairs={{0,8},{4,12},{8,0},{12,4},{1,9},{5,13},{9,1},{13,5},{2,10},{6,14},... | collective-permute-start | bytes 294920 | tf_op jit(solution)/shard_map/ppermute | solution.py:410
  9.8 7.1 %collective-permute-start.2 = (bf16[2,8,24,128]{3,2,1,0:T(8,128)(2,1)S(1)}, bf16[2,8,24,128]{3,2,1,0:T(8,128)(2,1)S(1)}, u32[]{:S(2)}, u32[]{:S(2)}) collective-permute-start(bf16[2,8,24,128]{3,2,1,0:T(8,128)(2,1)S(1)} %shard_map.105.held_ref.refs_12_.refs_8_), channel_id=1, source_target_pairs={{0,12},{4,8},{8,4},{12,0},{1,13},{5,9},{9,5},{13,1},{2,14},{6,10},... | collective-permute-start | bytes 294920 | tf_op jit(solution)/shard_map/ppermute | solution.py:410
  11.1 6.1 %collective-permute-start.3 = (bf16[2,8,24,128]{3,2,1,0:T(8,128)(2,1)S(1)}, bf16[2,8,24,128]{3,2,1,0:T(8,128)(2,1)S(1)}, u32[]{:S(2)}, u32[]{:S(2)}) collective-permute-start(bf16[2,8,24,128]{3,2,1,0:T(8,128)(2,1)S(1)} %shard_map.105.held_ref.refs_12_.refs_8_), channel_id=1, source_target_pairs={{0,4},{4,0},{8,12},{12,8},{1,5},{5,1},{9,13},{13,9},{2,6},{6,2},{1... | collective-permute-start | bytes 294920 | tf_op jit(solution)/shard_map/ppermute | solution.py:410
  11.4 0.7 %copy-start.5 = (f32[512]{0:T(512)S(1)}, f32[512]{0:T(512)}, u32[]{:S(2)}) copy-start(f32[512]{0:T(512)} %param.16) | copy-start | bytes 6148
  11.4 0.7 %copy-start.6 = (f32[12]{0:T(128)S(1)}, f32[12]{0:T(128)}, u32[]{:S(2)}) copy-start(f32[12]{0:T(128)} %param.15) | copy-start | bytes 148
  12.6 4.6 %collective-permute-start.6 = (bf16[9,24,128]{2,1,0:T(8,128)(2,1)S(1)}, bf16[9,24,128]{2,1,0:T(8,128)(2,1)S(1)}, u32[]{:S(2)}, u32[]{:S(2)}) collective-permute-start(bf16[9,24,128]{2,1,0:T(8,128)(2,1)S(1)} %get-tuple-element.25), channel_id=1, source_target_pairs={{0,2},{2,0},{1,3},{3,1},{4,6},{6,4},{5,7},{7,5},{8,10},{10,8},{9,1... | collective-permute-start | bytes 165896 | tf_op jit(solution)/shard_map/ppermute | solution.py:32
  16.2 1.7 %collective-permute-start.5 = (bf16[3,2,2,128,128]{4,3,2,1,0:T(8,128)(2,1)S(1)}, bf16[3,2,2,128,128]{4,3,2,1,0:T(8,128)(2,1)S(1)}, u32[]{:S(2)}, u32[]{:S(2)}) collective-permute-start(bf16[3,2,2,128,128]{4,3,2,1,0:T(8,128)(2,1)S(1)} %collective-permute-done.4.refs_3_), channel_id=1, source_target_pairs={{0,1},{1,0},{2,3},{3,2},{4,5},{5,4},{6,7},{7,6},{8,9},{9,8},{10,11... | collective-permute-start | bytes 1179656 | tf_op jit(solution)/shard_map/ppermute | solution.py:32

commit v8 on v7

--- a/solution.py
+++ b/solution.py
@@ -223,11 +223,12 @@
     )
 
 
-def outflow_terms(side, ends_ref, current_ref, matrix_ref, store):
-    row_blocks, block_size = matrix_ref.shape[:2]
+def outflow_terms(side, chosen, ends_ref, current_ref, matrix_ref, store):
+    block_size = matrix_ref.shape[1]
+    row_blocks = ends_ref.shape[1] // block_size
     leaves, enters = ends_ref[0:1, :], ends_ref[1:2, :]
     current = lanes([current_ref[1, block] for block in range(row_blocks)])
-    for block in range(row_blocks):
+    for block in chosen:
         base = ((lax.axis_index("cell") ^ side) * row_blocks + block) * block_size
         panel = lax.broadcasted_iota(jnp.int32, (block_size, ends_ref.shape[1]), 0) + base
         entry = (leaves == panel).astype(jnp.float32) - (enters == panel).astype(jnp.float32)
@@ -240,12 +241,12 @@
     def store(block, sums):
         outflow_ref[block] = sums
 
-    outflow_terms(0, ends_ref, message_ref, matrix_ref, store)
+    outflow_terms(0, range(matrix_ref.shape[0]), ends_ref, message_ref, matrix_ref, store)
 
 
 def first_kernel(
-    regions, held_ref, p_ref, l_ref, p_cols_ref, l_cols_ref, omega_ref, resist_ref, ends_ref,
-    factor_ref, table_ref, potential_ref, flux_ref, early_ref, matrix_ref, numbers_ref,
+    regions, held_ref, p_ref, l_ref, p_cols_ref, l_cols_ref, omega_ref, resist_ref, ends_ref, part_ref, sums_ref,
+    factor_ref, table_ref, potential_ref, flux_ref, early_ref, matrix_ref, own_matrix_ref, outflow_ref, numbers_ref,
 ):
     row_blocks, rows, block_size = potential_ref.shape
     slots = p_ref.shape[2]
@@ -271,7 +272,14 @@
     def store(block, sums):
         early_ref[row_blocks + block] = sums.astype(jnp.bfloat16)
 
-    outflow_terms(1, ends_ref, held_ref, matrix_ref, store)
+    def store_own(block, sums):
+        outflow_ref[block] = sums
+
+    done = part_ref.shape[0]
+    own_matrix_ref[:done] = part_ref[...]
+    outflow_ref[:done] = sums_ref[...]
+    outflow_terms(0, range(done, row_blocks), ends_ref, held_ref, own_matrix_ref, store_own)
+    outflow_terms(1, range(row_blocks), ends_ref, held_ref, matrix_ref, store)
     for row in range(row_blocks):
         potential, flux = region_terms(regions, 0, table_ref, held_ref, p_ref, l_ref, row)
         potential_ref[row], flux_ref[row] = potential, flux
@@ -401,16 +409,25 @@
 
     totals = jax.ShapeDtypeStruct((row_blocks, rows, block_size), jnp.float32)
     matrix_shape = jax.ShapeDtypeStruct((row_blocks, block_size, share), jnp.bfloat16)
-    matrix, outflow = kernel_call(outflow_kernel, (matrix_shape, totals), "vv", SMALL)(message, branch_ends)
+    done = row_blocks - 1
+    part, sums = kernel_call(
+        outflow_kernel,
+        (
+            jax.ShapeDtypeStruct((done, block_size, share), jnp.bfloat16),
+            jax.ShapeDtypeStruct((done, rows, block_size), jnp.float32),
+        ),
+        "vv",
+        SMALL,
+    )(message, branch_ends)
     half_shape = jax.ShapeDtypeStruct((regions - 1, row_blocks // 2) + p_blocks.shape[2:], jnp.bfloat16)
-    sent = kernel_call(functools.partial(send_kernel, regions), half_shape, "va", SMALL)(p_blocks, outflow)
+    sent = kernel_call(functools.partial(send_kernel, regions), half_shape, "va", SMALL)(p_blocks, sums)
     mine = swapped(sent, "cell", 1)
     theirs = swapped(mine, "col", 1)
 
     pieces = [lax.ppermute(held, "blk", list(enumerate(targets))) for targets in region_moves(regions)]
 
     slots = p_cols.shape[2]
-    factors, table, potential, flux, early, other_matrix = kernel_call(
+    factors, table, potential, flux, early, other_matrix, matrix, outflow = kernel_call(
         functools.partial(first_kernel, regions),
         (
             jax.ShapeDtypeStruct((1 + row_blocks, rows, block_size), jnp.float32),
@@ -419,13 +436,15 @@
             totals,
             jax.ShapeDtypeStruct((2 * row_blocks + 1, rows, block_size), jnp.bfloat16),
             matrix_shape,
-        ),
-        "vvvvvvvv",
+            matrix_shape,
+            totals,
+        ),
+        "vvvvvvvvvv",
         SMALL,
         [pltpu.VMEM((rows, block_size), jnp.float32)],
     )(
         held, p_blocks, l_blocks, p_cols.transpose(0, 2, 1), l_cols.transpose(0, 2, 1), omegas[None], resist[None],
-        branch_ends,
+        branch_ends, part, sums,
     )
     early = swapped(early, "cell", 1)
     for move, piece in enumerate(pieces[:-1], 1):

time: 19.2 us -> 19.1 us (level)
    ppermute x4, waiting for transfers between devices: 2.55 us -> 2.34 us  [swapped(): lax.ppermute(array, axis, [(i, i ^ distance) for i in range(lax.axis_size...]
where the time goes in v8:
time: 19.1 us; the launch traced here: 18.9 us
  starting transfers between devices  10.6 us (55%)
  Pallas kernels  3.24 us (17%)
  waiting for transfers between devices  2.82 us (15%)
  local copies, waits for them, and re-layouts  1.51 us (8%)
  between operations  0.75 us (4%)
    ppermute x4, starting transfers between devices, swapped(): lax.ppermute(array, axis, [(i, i ^ distance) for i in range(lax.axis_size...  5.74 us
    ppermute x3, starting transfers between devices, paired_step(): lax.ppermute(held, 'blk', list(enumerate(targets)))  4.84 us
    ppermute x4, waiting for transfers between devices, swapped(): lax.ppermute(array, axis, [(i, i ^ distance) for i in range(lax.axis_size...  2.34 us
    pallas_call x1, Pallas kernels, paired_step(): kernel_call(functools.partial(last_kernel, regions), (result, result), 'v...  1.06 us
    reshape x2, local copies, waits for them, and re-layouts, blocked(): return array.reshape(rows, row_blocks, block_size).transpose(1, 0, 2)  0.79 us
    unnamed x16, local copies, waits for them, and re-layouts  0.71 us
    pallas_call x1, Pallas kernels, paired_step(): kernel_call(functools.partial(first_kernel, regions), (jax.ShapeDtypeStru...  0.66 us
    pallas_call x2, Pallas kernels, paired_step(): kernel_call(functools.partial(next_kernel, regions, move), (totals, total...  0.58 us
  transfers between devices with their start and end apart: 7, of which 4 were waited for; matrix products, arithmetic and copies ran while one was open for 0% of the time, Pallas kernels for 11%

profile of v8, /device:TPU:0, one launch (start us, length us, event | category | flops | bytes accessed | tf_op | source)
XLA Modules:
  0.0 18.9 jit_solution(14010232757989367726)
XLA Ops:
  0.6 0.8 %reshape.10 = bf16[24,4,128]{2,1,0:T(4,128)(2,1)S(1)} reshape(bf16[12,2,512]{2,1,0:T(2,128)(2,1)} %param.13) | data formatting | bytes 49152 | tf_op jit(solution)/shard_map/reshape | solution.py:401
  1.5 0.0 copy-start.2
  1.5 0.0 copy-start
  1.5 3.0 %collective-permute-start = (bf16[2,4,24,128]{3,2,1,0:T(8,128)(2,1)S(1)}, bf16[2,4,24,128]{3,2,1,0:T(8,128)(2,1)S(1)}, u32[]{:S(2)}, u32[]{:S(2)}) collective-permute-start(bf16[2,4,24,128]{3,2,1,0:T(8,128)(2,1)S(1)} %shard_map.104.own_ref.message_ref), channel_id=1, source_target_pairs={{0,2},{2,0},{1,3},{3,1},{4,6},{6,4},{5,7},{7,5},{8,10},{10,8},{9,1... | collective-permute-start | bytes 147464 | tf_op jit(solution)/shard_map/ppermute | solution.py:32
  4.5 0.3 %shard_map.106 = (bf16[3,128,512]{2,1,0:T(8,128)(2,1)S(1)}, f32[3,24,128]{2,1,0:T(8,128)S(1)}) custom-call(bf16[2,4,24,128]{3,2,1,0:T(8,128)(2,1)S(1)} %shard_map.104.own_ref.message_ref, s32[2,512]{1,0:T(2,128)S(1)} %copy-done.2), custom_call_target="tpu_custom_call" | custom-call | flops 1000000 | bytes 4000000 | tf_op jit(solution)/shard_map/pallas_call | solution.py:413
  4.9 0.0 copy-start.1
  4.9 0.9 %collective-permute-start.4 = (bf16[3,2,2,128,128]{4,3,2,1,0:T(8,128)(2,1)S(1)}, bf16[3,2,2,128,128]{4,3,2,1,0:T(8,128)(2,1)S(1)}, u32[]{:S(2)}, u32[]{:S(2)}) collective-permute-start(bf16[3,2,2,128,128]{4,3,2,1,0:T(8,128)(2,1)S(1)} %shard_map.107), channel_id=1, source_target_pairs={{0,2},{2,0},{1,3},{3,1},{4,6},{6,4},{5,7},{7,5},{8,10},{10,8},{9,1... | collective-permute-start | bytes 1179656 | tf_op jit(solution)/shard_map/ppermute | solution.py:32
  5.8 0.8 %collective-permute-done.other_ref = bf16[2,4,24,128]{3,2,1,0:T(8,128)(2,1)S(1)} collective-permute-done((bf16[2,4,24,128]{3,2,1,0:T(8,128)(2,1)S(1)}, bf16[2,4,24,128]{3,2,1,0:T(8,128)(2,1)S(1)}, u32[]{:S(2)}, u32[]{:S(2)}) %collective-permute-start) | collective-permute-done | bytes 49184 | tf_op jit(solution)/shard_map/ppermute | solution.py:32
  6.6 3.3 %collective-permute-start.1 = (bf16[2,8,24,128]{3,2,1,0:T(8,128)(2,1)S(1)}, bf16[2,8,24,128]{3,2,1,0:T(8,128)(2,1)S(1)}, u32[]{:S(2)}, u32[]{:S(2)}) collective-permute-start(bf16[2,8,24,128]{3,2,1,0:T(8,128)(2,1)S(1)} %shard_map.105.held_ref.refs_12_.refs_8_), channel_id=1, source_target_pairs={{0,8},{4,12},{8,0},{12,4},{1,9},{5,13},{9,1},{13,5},{2,10},{6,14},... | collective-permute-start | bytes 294920 | tf_op jit(solution)/shard_map/ppermute | solution.py:427
  9.8 1.3 %collective-permute-start.2 = (bf16[2,8,24,128]{3,2,1,0:T(8,128)(2,1)S(1)}, bf16[2,8,24,128]{3,2,1,0:T(8,128)(2,1)S(1)}, u32[]{:S(2)}, u32[]{:S(2)}) collective-permute-start(bf16[2,8,24,128]{3,2,1,0:T(8,128)(2,1)S(1)} %shard_map.105.held_ref.refs_12_.refs_8_), channel_id=1, source_target_pairs={{0,12},{4,8},{8,4},{12,0},{1,13},{5,9},{9,5},{13,1},{2,14},{6,10},... | collective-permute-start | bytes 294920 | tf_op jit(solution)/shard_map/ppermute | solution.py:427
  11.2 0.2 %collective-permute-start.3 = (bf16[2,8,24,128]{3,2,1,0:T(8,128)(2,1)S(1)}, bf16[2,8,24,128]{3,2,1,0:T(8,128)(2,1)S(1)}, u32[]{:S(2)}, u32[]{:S(2)}) collective-permute-start(bf16[2,8,24,128]{3,2,1,0:T(8,128)(2,1)S(1)} %shard_map.105.held_ref.refs_12_.refs_8_), channel_id=1, source_target_pairs={{0,4},{4,0},{8,12},{12,8},{1,5},{5,1},{9,13},{13,9},{2,6},{6,2},{1... | collective-permute-start | bytes 294920 | tf_op jit(solution)/shard_map/ppermute | solution.py:427
  11.4 0.7 %copy-done.4 = s32[4,4,2]{1,2,0:T(2,128)S(1)} copy-done((s32[4,4,2]{1,2,0:T(2,128)S(1)}, s32[4,4,2]{1,2,0:T(2,128)}, u32[]{:S(2)}) %copy-start.4) | copy-done | bytes 152
  12.1 0.0 copy-done.3
  12.1 0.7 %shard_map.108 = (f32[5,24,128]{2,1,0:T(8,128)S(1)}, s32[2,4,4,2,128]{4,3,2,1,0:T(2,128)S(1)}, f32[4,24,128]{2,1,0:T(8,128)S(1)}, f32[4,24,128]{2,1,0:T(8,128)S(...) custom-call(bf16[2,8,24,128]{3,2,1,0:T(8,128)(2,1)S(1)} %shard_map.1, ...), custom_call_target="tpu_custom_call" | custom-call | flops 1000000 | bytes 4000000 | tf_op jit(solution)/shard_map/pallas_call | solution.py:430
  12.8 1.9 %collective-permute-start.6 = (bf16[9,24,128]{2,1,0:T(8,128)(2,1)S(1)}, bf16[9,24,128]{2,1,0:T(8,128)(2,1)S(1)}, u32[]{:S(2)}, u32[]{:S(2)}) collective-permute-start(bf16[9,24,128]{2,1,0:T(8,128)(2,1)S(1)} %get-tuple-element.28), channel_id=1, source_target_pairs={{0,2},{2,0},{1,3},{3,1},{4,6},{6,4},{5,7},{7,5},{8,10},{10,8},{9,1... | collective-permute-start | bytes 165896 | tf_op jit(solution)/shard_map/ppermute | solution.py:32
  14.7 1.5 %collective-permute-done.4.refs_3_ = bf16[3,2,2,128,128]{4,3,2,1,0:T(8,128)(2,1)S(1)} collective-permute-done((bf16[3,2,2,128,128]{4,3,2,1,0:T(8,128)(2,1)S(1)}, bf16[3,2,2,128,128]{4,3,2,1,0:T(8,128)(2,1)S(1)}, u32[]{:S(2)}, u32[]{:S(2)}) %collective-permute-start.4) | collective-permute-done | bytes 393248 | tf_op jit(solution)/shard_map/ppermute | solution.py:32
  16.1 0.0 collective-permute-start.5
  16.1 0.3 %shard_map.109 = (f32[4,24,128]{2,1,0:T(8,128)S(1)}, f32[4,24,128]{2,1,0:T(8,128)S(1)}) custom-call(s32[2,4,4,2,128]{4,3,2,1,0:T(2,128)S(1)} %get-tuple-element.20.table_ref.refs_4_, bf16[2,8,24,128]{3,2,1,0:T(8,128)(2,1)S(1)} %collective-permute-done.1.held_ref.refs_0_, bf16[4,4,2,128,128]{4,3,2,1,0:T(8,128)(2,1)S(1)} %copy-done, ...), custom_call_target="tpu_custom_call" | custom-call | flops 3000000000 | bytes 4000000 | tf_op jit(solution)/shard_map/pallas_call | solution.py:451
  16.4 0.5 %collective-permute-done.2.held_ref.refs_1_ = bf16[2,8,24,128]{3,2,1,0:T(8,128)(2,1)S(1)} collective-permute-done((bf16[2,8,24,128]{3,2,1,0:T(8,128)(2,1)S(1)}, bf16[2,8,24,128]{3,2,1,0:T(8,128)(2,1)S(1)}, u32[]{:S(2)}, u32[]{:S(2)}) %collective-permute-start.2) | collective-permute-done | bytes 98336 | tf_op jit(solution)/shard_map/ppermute | solution.py:427
  16.9 0.3 %shard_map.110 = (f32[4,24,128]{2,1,0:T(8,128)S(1)}, f32[4,24,128]{2,1,0:T(8,128)S(1)}) custom-call(s32[2,4,4,2,128]{4,3,2,1,0:T(2,128)S(1)} %get-tuple-element.20.table_ref.refs_4_, bf16[2,8,24,128]{3,2,1,0:T(8,128)(2,1)S(1)} %collective-permute-done.2.held_ref.refs_1_, bf16[4,4,2,128,128]{4,3,2,1,0:T(8,128)(2,1)S(1)} %copy-done, ...), custom_call_target="tpu_custom_call" | custom-call | flops 3000000000 | bytes 4000000 | tf_op jit(solution)/shard_map/pallas_call | solution.py:451
  17.2 0.0 collective-permute-done.3.refs_2_
  17.2 0.6 %shard_map.111 = (f32[24,512]{1,0:T(8,128)S(1)}, s32[24,128]{1,0:T(8,128)S(1)}) custom-call(bf16[2,8,24,128]{3,2,1,0:T(8,128)(2,1)S(1)} %collective-permute-done.1.held_ref.refs_0_, bf16[2,8,24,128]{3,2,1,0:T(8,128)(2,1)S(1)} %collective-permute-done.2.held_ref.refs_1_, bf16[2,8,24,128]{3,2,1,0:T(8,128)(2,1)S(1)} %collective-permute-done.3.refs_2_, ...), custom_call_target="tpu_custom_call" | custom-call | flops 1000000000 | bytes 4000000 | tf_op jit(solution)/shard_map/pallas_call | solution.py:456
  17.8 0.1 collective-permute-done.5.refs_3_
  17.8 1.1 %shard_map.112 = (f32[12,2,512]{2,1,0:T(2,128)}, f32[12,2,512]{2,1,0:T(2,128)}) custom-call(bf16[2,8,24,128]{3,2,1,0:T(8,128)(2,1)S(1)} %collective-permute-done.1.held_ref.refs_0_, bf16[2,8,24,128]{3,2,1,0:T(8,128)(2,1)S(1)} %collective-permute-done.2.held_ref.refs_1_, bf16[2,8,24,128]{3,2,1,0:T(8,128)(2,1)S(1)} %collective-permute-done.3.refs_2_, ...), custom_call_target="tpu_custom_call" | custom-call | flops 8000000000 | bytes 4000000 | tf_op jit(solution)/shard_map/pallas_call | solution.py:463
  (18 shorter events, 0.1 us)
Async XLA Ops:
  0.6 0.8 %copy-start.7 = (bf16[12,2,512]{2,1,0:T(2,128)(2,1)S(1)}, bf16[12,2,512]{2,1,0:T(2,128)(2,1)}, u32[]{:S(2)}) copy-start(bf16[12,2,512]{2,1,0:T(2,128)(2,1)} %param.14) | copy-start | bytes 73732
  1.5 3.0 %copy-start.2 = (s32[2,512]{1,0:T(2,128)S(1)}, s32[2,512]{1,0:T(2,128)}, u32[]{:S(2)}) copy-start(s32[2,512]{1,0:T(2,128)} %ends_ref.3) | copy-start | bytes 12292
  1.5 3.3 %copy-start = (bf16[4,4,2,128,128]{4,3,2,1,0:T(8,128)(2,1)S(1)}, bf16[4,4,2,128,128]{4,3,2,1,0:T(8,128)(2,1)}, u32[]{:S(2)}) copy-start(bf16[4,4,2,128,128]{4,3,2,1,0:T(8,128)(2,1)} %refs_5_.1) | copy-start | bytes 3145732
  1.5 5.1 %collective-permute-start = (bf16[2,4,24,128]{3,2,1,0:T(8,128)(2,1)S(1)}, bf16[2,4,24,128]{3,2,1,0:T(8,128)(2,1)S(1)}, u32[]{:S(2)}, u32[]{:S(2)}) collective-permute-start(bf16[2,4,24,128]{3,2,1,0:T(8,128)(2,1)S(1)} %shard_map.104.own_ref.message_ref), channel_id=1, source_target_pairs={{0,2},{2,0},{1,3},{3,1},{4,6},{6,4},{5,7},{7,5},{8,10},{10,8},{9,1... | collective-permute-start | bytes 147464 | tf_op jit(solution)/shard_map/ppermute | solution.py:32
  4.9 6.6 %copy-start.1 = (bf16[4,4,2,128,128]{4,3,2,1,0:T(8,128)(2,1)S(1)}, bf16[4,4,2,128,128]{4,3,2,1,0:T(8,128)(2,1)}, u32[]{:S(2)}) copy-start(bf16[4,4,2,128,128]{4,3,2,1,0:T(8,128)(2,1)} %refs_6_.1) | copy-start | bytes 3145732
  4.9 11.2 %collective-permute-start.4 = (bf16[3,2,2,128,128]{4,3,2,1,0:T(8,128)(2,1)S(1)}, bf16[3,2,2,128,128]{4,3,2,1,0:T(8,128)(2,1)S(1)}, u32[]{:S(2)}, u32[]{:S(2)}) collective-permute-start(bf16[3,2,2,128,128]{4,3,2,1,0:T(8,128)(2,1)S(1)} %shard_map.107), channel_id=1, source_target_pairs={{0,2},{2,0},{1,3},{3,1},{4,6},{6,4},{5,7},{7,5},{8,10},{10,8},{9,1... | collective-permute-start | bytes 1179656 | tf_op jit(solution)/shard_map/ppermute | solution.py:32
  6.6 4.9 %copy-start.5 = (f32[512]{0:T(512)S(1)}, f32[512]{0:T(512)}, u32[]{:S(2)}) copy-start(f32[512]{0:T(512)} %param.16) | copy-start | bytes 6148
  6.6 9.5 %collective-permute-start.1 = (bf16[2,8,24,128]{3,2,1,0:T(8,128)(2,1)S(1)}, bf16[2,8,24,128]{3,2,1,0:T(8,128)(2,1)S(1)}, u32[]{:S(2)}, u32[]{:S(2)}) collective-permute-start(bf16[2,8,24,128]{3,2,1,0:T(8,128)(2,1)S(1)} %shard_map.105.held_ref.refs_12_.refs_8_), channel_id=1, source_target_pairs={{0,8},{4,12},{8,0},{12,4},{1,9},{5,13},{9,1},{13,5},{2,10},{6,14},... | collective-permute-start | bytes 294920 | tf_op jit(solution)/shard_map/ppermute | solution.py:427
  9.8 7.0 %collective-permute-start.2 = (bf16[2,8,24,128]{3,2,1,0:T(8,128)(2,1)S(1)}, bf16[2,8,24,128]{3,2,1,0:T(8,128)(2,1)S(1)}, u32[]{:S(2)}, u32[]{:S(2)}) collective-permute-start(bf16[2,8,24,128]{3,2,1,0:T(8,128)(2,1)S(1)} %shard_map.105.held_ref.refs_12_.refs_8_), channel_id=1, source_target_pairs={{0,12},{4,8},{8,4},{12,0},{1,13},{5,9},{9,5},{13,1},{2,14},{6,10},... | collective-permute-start | bytes 294920 | tf_op jit(solution)/shard_map/ppermute | solution.py:427
  11.2 6.0 %collective-permute-start.3 = (bf16[2,8,24,128]{3,2,1,0:T(8,128)(2,1)S(1)}, bf16[2,8,24,128]{3,2,1,0:T(8,128)(2,1)S(1)}, u32[]{:S(2)}, u32[]{:S(2)}) collective-permute-start(bf16[2,8,24,128]{3,2,1,0:T(8,128)(2,1)S(1)} %shard_map.105.held_ref.refs_12_.refs_8_), channel_id=1, source_target_pairs={{0,4},{4,0},{8,12},{12,8},{1,5},{5,1},{9,13},{13,9},{2,6},{6,2},{1... | collective-permute-start | bytes 294920 | tf_op jit(solution)/shard_map/ppermute | solution.py:427
  11.4 0.7 %copy-start.4 = (s32[4,4,2]{1,2,0:T(2,128)S(1)}, s32[4,4,2]{1,2,0:T(2,128)}, u32[]{:S(2)}) copy-start(s32[4,4,2]{1,2,0:T(2,128)} %param.12) | copy-start | bytes 388
  11.4 0.7 %copy-start.3 = (s32[4,4,2]{1,2,0:T(2,128)S(1)}, s32[4,4,2]{1,2,0:T(2,128)}, u32[]{:S(2)}) copy-start(s32[4,4,2]{1,2,0:T(2,128)} %param.10) | copy-start | bytes 388
  11.4 0.7 %copy-start.6 = (f32[12]{0:T(128)S(1)}, f32[12]{0:T(128)}, u32[]{:S(2)}) copy-start(f32[12]{0:T(128)} %param.15) | copy-start | bytes 148
  12.8 4.4 %collective-permute-start.6 = (bf16[9,24,128]{2,1,0:T(8,128)(2,1)S(1)}, bf16[9,24,128]{2,1,0:T(8,128)(2,1)S(1)}, u32[]{:S(2)}, u32[]{:S(2)}) collective-permute-start(bf16[9,24,128]{2,1,0:T(8,128)(2,1)S(1)} %get-tuple-element.28), channel_id=1, source_target_pairs={{0,2},{2,0},{1,3},{3,1},{4,6},{6,4},{5,7},{7,5},{8,10},{10,8},{9,1... | collective-permute-start | bytes 165896 | tf_op jit(solution)/shard_map/ppermute | solution.py:32
  16.1 1.7 %collective-permute-start.5 = (bf16[3,2,2,128,128]{4,3,2,1,0:T(8,128)(2,1)S(1)}, bf16[3,2,2,128,128]{4,3,2,1,0:T(8,128)(2,1)S(1)}, u32[]{:S(2)}, u32[]{:S(2)}) collective-permute-start(bf16[3,2,2,128,128]{4,3,2,1,0:T(8,128)(2,1)S(1)} %collective-permute-done.4.refs_3_), channel_id=1, source_target_pairs={{0,1},{1,0},{2,3},{3,2},{4,5},{5,4},{6,7},{7,6},{8,9},{9,8},{10,11... | collective-permute-start | bytes 1179656 | tf_op jit(solution)/shard_map/ppermute | solution.py:32

commit v9 on v8

--- a/solution.py
+++ b/solution.py
@@ -409,7 +409,7 @@
 
     totals = jax.ShapeDtypeStruct((row_blocks, rows, block_size), jnp.float32)
     matrix_shape = jax.ShapeDtypeStruct((row_blocks, block_size, share), jnp.bfloat16)
-    done = row_blocks - 1
+    done = row_blocks // 2
     part, sums = kernel_call(
         outflow_kernel,
         (

time: 19.1 us -> 19.1 us (level)
  transfers between devices with their start and end apart: 7 -> 7, of which waited for: 4 -> 3; matrix products, arithmetic and copies ran while one was open for 0% -> 0% of each run, Pallas kernels for 11% -> 12%
where the time goes in v9:
time: 19.1 us; the launch traced here: 18.9 us
  starting transfers between devices  10.6 us (55%)
  Pallas kernels  3.25 us (17%)
  waiting for transfers between devices  2.72 us (14%)
  local copies, waits for them, and re-layouts  1.52 us (8%)
  between operations  0.76 us (4%)
    ppermute x4, starting transfers between devices, swapped(): lax.ppermute(array, axis, [(i, i ^ distance) for i in range(lax.axis_size...  5.73 us
    ppermute x3, starting transfers between devices, paired_step(): lax.ppermute(held, 'blk', list(enumerate(targets)))  4.91 us
    ppermute x4, waiting for transfers between devices, swapped(): lax.ppermute(array, axis, [(i, i ^ distance) for i in range(lax.axis_size...  2.16 us
    pallas_call x1, Pallas kernels, paired_step(): kernel_call(functools.partial(last_kernel, regions), (result, result), 'v...  1.07 us
    reshape x2, local copies, waits for them, and re-layouts, blocked(): return array.reshape(rows, row_blocks, block_size).transpose(1, 0, 2)  0.79 us
    pallas_call x1, Pallas kernels, paired_step(): kernel_call(functools.partial(first_kernel, regions), (jax.ShapeDtypeStru...  0.73 us
    unnamed x16, local copies, waits for them, and re-layouts  0.72 us
    pallas_call x2, Pallas kernels, paired_step(): kernel_call(functools.partial(next_kernel, regions, move), (totals, total...  0.58 us
  transfers between devices with their start and end apart: 7, of which 3 were waited for; matrix products, arithmetic and copies ran while one was open for 0% of the time, Pallas kernels for 12%

profile of v9, /device:TPU:0, one launch (start us, length us, event | category | flops | bytes accessed | tf_op | source)
XLA Modules:
  0.0 18.9 jit_solution(12204122894879628670)
XLA Ops:
  0.6 0.8 %reshape.10 = bf16[24,4,128]{2,1,0:T(4,128)(2,1)S(1)} reshape(bf16[12,2,512]{2,1,0:T(2,128)(2,1)} %param.13) | data formatting | bytes 49152 | tf_op jit(solution)/shard_map/reshape | solution.py:401
  1.5 0.0 copy-start.2
  1.5 0.0 copy-start
  1.5 3.0 %collective-permute-start = (bf16[2,4,24,128]{3,2,1,0:T(8,128)(2,1)S(1)}, bf16[2,4,24,128]{3,2,1,0:T(8,128)(2,1)S(1)}, u32[]{:S(2)}, u32[]{:S(2)}) collective-permute-start(bf16[2,4,24,128]{3,2,1,0:T(8,128)(2,1)S(1)} %shard_map.104.own_ref.message_ref), channel_id=1, source_target_pairs={{0,2},{2,0},{1,3},{3,1},{4,6},{6,4},{5,7},{7,5},{8,10},{10,8},{9,1... | collective-permute-start | bytes 147464 | tf_op jit(solution)/shard_map/ppermute | solution.py:32
  4.5 0.2 %shard_map.106 = (bf16[2,128,512]{2,1,0:T(8,128)(2,1)S(1)}, f32[2,24,128]{2,1,0:T(8,128)S(1)}) custom-call(bf16[2,4,24,128]{3,2,1,0:T(8,128)(2,1)S(1)} %shard_map.104.own_ref.message_ref, s32[2,512]{1,0:T(2,128)S(1)} %copy-done.2), custom_call_target="tpu_custom_call" | custom-call | flops 1000000 | bytes 4000000 | tf_op jit(solution)/shard_map/pallas_call | solution.py:413
  4.7 0.0 copy-done
  4.8 0.0 copy-start.1
  4.8 0.9 %collective-permute-start.4 = (bf16[3,2,2,128,128]{4,3,2,1,0:T(8,128)(2,1)S(1)}, bf16[3,2,2,128,128]{4,3,2,1,0:T(8,128)(2,1)S(1)}, u32[]{:S(2)}, u32[]{:S(2)}) collective-permute-start(bf16[3,2,2,128,128]{4,3,2,1,0:T(8,128)(2,1)S(1)} %shard_map.107), channel_id=1, source_target_pairs={{0,2},{2,0},{1,3},{3,1},{4,6},{6,4},{5,7},{7,5},{8,10},{10,8},{9,1... | collective-permute-start | bytes 1179656 | tf_op jit(solution)/shard_map/ppermute | solution.py:32
  5.8 0.8 %collective-permute-done.other_ref = bf16[2,4,24,128]{3,2,1,0:T(8,128)(2,1)S(1)} collective-permute-done((bf16[2,4,24,128]{3,2,1,0:T(8,128)(2,1)S(1)}, bf16[2,4,24,128]{3,2,1,0:T(8,128)(2,1)S(1)}, u32[]{:S(2)}, u32[]{:S(2)}) %collective-permute-start) | collective-permute-done | bytes 49184 | tf_op jit(solution)/shard_map/ppermute | solution.py:32
  6.6 3.3 %collective-permute-start.1 = (bf16[2,8,24,128]{3,2,1,0:T(8,128)(2,1)S(1)}, bf16[2,8,24,128]{3,2,1,0:T(8,128)(2,1)S(1)}, u32[]{:S(2)}, u32[]{:S(2)}) collective-permute-start(bf16[2,8,24,128]{3,2,1,0:T(8,128)(2,1)S(1)} %shard_map.105.held_ref.refs_12_.refs_8_), channel_id=1, source_target_pairs={{0,8},{4,12},{8,0},{12,4},{1,9},{5,13},{9,1},{13,5},{2,10},{6,14},... | collective-permute-start | bytes 294920 | tf_op jit(solution)/shard_map/ppermute | solution.py:427
  9.9 1.3 %collective-permute-start.2 = (bf16[2,8,24,128]{3,2,1,0:T(8,128)(2,1)S(1)}, bf16[2,8,24,128]{3,2,1,0:T(8,128)(2,1)S(1)}, u32[]{:S(2)}, u32[]{:S(2)}) collective-permute-start(bf16[2,8,24,128]{3,2,1,0:T(8,128)(2,1)S(1)} %shard_map.105.held_ref.refs_12_.refs_8_), channel_id=1, source_target_pairs={{0,12},{4,8},{8,4},{12,0},{1,13},{5,9},{9,5},{13,1},{2,14},{6,10},... | collective-permute-start | bytes 294920 | tf_op jit(solution)/shard_map/ppermute | solution.py:427
  11.3 0.2 %collective-permute-start.3 = (bf16[2,8,24,128]{3,2,1,0:T(8,128)(2,1)S(1)}, bf16[2,8,24,128]{3,2,1,0:T(8,128)(2,1)S(1)}, u32[]{:S(2)}, u32[]{:S(2)}) collective-permute-start(bf16[2,8,24,128]{3,2,1,0:T(8,128)(2,1)S(1)} %shard_map.105.held_ref.refs_12_.refs_8_), channel_id=1, source_target_pairs={{0,4},{4,0},{8,12},{12,8},{1,5},{5,1},{9,13},{13,9},{2,6},{6,2},{1... | collective-permute-start | bytes 294920 | tf_op jit(solution)/shard_map/ppermute | solution.py:427
  11.5 0.7 %copy-done.4 = s32[4,4,2]{1,2,0:T(2,128)S(1)} copy-done((s32[4,4,2]{1,2,0:T(2,128)S(1)}, s32[4,4,2]{1,2,0:T(2,128)}, u32[]{:S(2)}) %copy-start.4) | copy-done | bytes 152
  12.2 0.0 copy-done.3
  12.2 0.7 %shard_map.108 = (f32[5,24,128]{2,1,0:T(8,128)S(1)}, s32[2,4,4,2,128]{4,3,2,1,0:T(2,128)S(1)}, f32[4,24,128]{2,1,0:T(8,128)S(1)}, f32[4,24,128]{2,1,0:T(8,128)S(...) custom-call(bf16[2,8,24,128]{3,2,1,0:T(8,128)(2,1)S(1)} %shard_map.1, ...), custom_call_target="tpu_custom_call" | custom-call | flops 1000000 | bytes 4000000 | tf_op jit(solution)/shard_map/pallas_call | solution.py:430
  12.9 1.8 %collective-permute-start.6 = (bf16[9,24,128]{2,1,0:T(8,128)(2,1)S(1)}, bf16[9,24,128]{2,1,0:T(8,128)(2,1)S(1)}, u32[]{:S(2)}, u32[]{:S(2)}) collective-permute-start(bf16[9,24,128]{2,1,0:T(8,128)(2,1)S(1)} %get-tuple-element.28), channel_id=1, source_target_pairs={{0,2},{2,0},{1,3},{3,1},{4,6},{6,4},{5,7},{7,5},{8,10},{10,8},{9,1... | collective-permute-start | bytes 165896 | tf_op jit(solution)/shard_map/ppermute | solution.py:32
  14.7 1.3 %collective-permute-done.4.refs_3_ = bf16[3,2,2,128,128]{4,3,2,1,0:T(8,128)(2,1)S(1)} collective-permute-done((bf16[3,2,2,128,128]{4,3,2,1,0:T(8,128)(2,1)S(1)}, bf16[3,2,2,128,128]{4,3,2,1,0:T(8,128)(2,1)S(1)}, u32[]{:S(2)}, u32[]{:S(2)}) %collective-permute-start.4) | collective-permute-done | bytes 393248 | tf_op jit(solution)/shard_map/ppermute | solution.py:32
  16.1 0.3 %shard_map.109 = (f32[4,24,128]{2,1,0:T(8,128)S(1)}, f32[4,24,128]{2,1,0:T(8,128)S(1)}) custom-call(s32[2,4,4,2,128]{4,3,2,1,0:T(2,128)S(1)} %get-tuple-element.20.table_ref.refs_4_, bf16[2,8,24,128]{3,2,1,0:T(8,128)(2,1)S(1)} %collective-permute-done.1.held_ref.refs_0_, bf16[4,4,2,128,128]{4,3,2,1,0:T(8,128)(2,1)S(1)} %copy-done, ...), custom_call_target="tpu_custom_call" | custom-call | flops 3000000000 | bytes 4000000 | tf_op jit(solution)/shard_map/pallas_call | solution.py:451
  16.3 0.5 %collective-permute-done.2.held_ref.refs_1_ = bf16[2,8,24,128]{3,2,1,0:T(8,128)(2,1)S(1)} collective-permute-done((bf16[2,8,24,128]{3,2,1,0:T(8,128)(2,1)S(1)}, bf16[2,8,24,128]{3,2,1,0:T(8,128)(2,1)S(1)}, u32[]{:S(2)}, u32[]{:S(2)}) %collective-permute-start.2) | collective-permute-done | bytes 98336 | tf_op jit(solution)/shard_map/ppermute | solution.py:427
  16.9 0.3 %shard_map.110 = (f32[4,24,128]{2,1,0:T(8,128)S(1)}, f32[4,24,128]{2,1,0:T(8,128)S(1)}) custom-call(s32[2,4,4,2,128]{4,3,2,1,0:T(2,128)S(1)} %get-tuple-element.20.table_ref.refs_4_, bf16[2,8,24,128]{3,2,1,0:T(8,128)(2,1)S(1)} %collective-permute-done.2.held_ref.refs_1_, bf16[4,4,2,128,128]{4,3,2,1,0:T(8,128)(2,1)S(1)} %copy-done, ...), custom_call_target="tpu_custom_call" | custom-call | flops 3000000000 | bytes 4000000 | tf_op jit(solution)/shard_map/pallas_call | solution.py:451
  17.2 0.0 collective-permute-done.3.refs_2_
  17.2 0.6 %shard_map.111 = (f32[24,512]{1,0:T(8,128)S(1)}, s32[24,128]{1,0:T(8,128)S(1)}) custom-call(bf16[2,8,24,128]{3,2,1,0:T(8,128)(2,1)S(1)} %collective-permute-done.1.held_ref.refs_0_, bf16[2,8,24,128]{3,2,1,0:T(8,128)(2,1)S(1)} %collective-permute-done.2.held_ref.refs_1_, bf16[2,8,24,128]{3,2,1,0:T(8,128)(2,1)S(1)} %collective-permute-done.3.refs_2_, ...), custom_call_target="tpu_custom_call" | custom-call | flops 1000000000 | bytes 4000000 | tf_op jit(solution)/shard_map/pallas_call | solution.py:456
  17.8 0.0 collective-permute-done.5.refs_3_
  17.8 1.1 %shard_map.112 = (f32[12,2,512]{2,1,0:T(2,128)}, f32[12,2,512]{2,1,0:T(2,128)}) custom-call(bf16[2,8,24,128]{3,2,1,0:T(8,128)(2,1)S(1)} %collective-permute-done.1.held_ref.refs_0_, bf16[2,8,24,128]{3,2,1,0:T(8,128)(2,1)S(1)} %collective-permute-done.2.held_ref.refs_1_, bf16[2,8,24,128]{3,2,1,0:T(8,128)(2,1)S(1)} %collective-permute-done.3.refs_2_, ...), custom_call_target="tpu_custom_call" | custom-call | flops 8000000000 | bytes 4000000 | tf_op jit(solution)/shard_map/pallas_call | solution.py:463
  (18 shorter events, 0.1 us)
Async XLA Ops:
  0.6 0.8 %copy-start.7 = (bf16[12,2,512]{2,1,0:T(2,128)(2,1)S(1)}, bf16[12,2,512]{2,1,0:T(2,128)(2,1)}, u32[]{:S(2)}) copy-start(bf16[12,2,512]{2,1,0:T(2,128)(2,1)} %param.14) | copy-start | bytes 73732
  1.5 3.0 %copy-start.2 = (s32[2,512]{1,0:T(2,128)S(1)}, s32[2,512]{1,0:T(2,128)}, u32[]{:S(2)}) copy-start(s32[2,512]{1,0:T(2,128)} %ends_ref.3) | copy-start | bytes 12292
  1.5 3.3 %copy-start = (bf16[4,4,2,128,128]{4,3,2,1,0:T(8,128)(2,1)S(1)}, bf16[4,4,2,128,128]{4,3,2,1,0:T(8,128)(2,1)}, u32[]{:S(2)}) copy-start(bf16[4,4,2,128,128]{4,3,2,1,0:T(8,128)(2,1)} %refs_5_.1) | copy-start | bytes 3145732
  1.5 5.1 %collective-permute-start = (bf16[2,4,24,128]{3,2,1,0:T(8,128)(2,1)S(1)}, bf16[2,4,24,128]{3,2,1,0:T(8,128)(2,1)S(1)}, u32[]{:S(2)}, u32[]{:S(2)}) collective-permute-start(bf16[2,4,24,128]{3,2,1,0:T(8,128)(2,1)S(1)} %shard_map.104.own_ref.message_ref), channel_id=1, source_target_pairs={{0,2},{2,0},{1,3},{3,1},{4,6},{6,4},{5,7},{7,5},{8,10},{10,8},{9,1... | collective-permute-start | bytes 147464 | tf_op jit(solution)/shard_map/ppermute | solution.py:32
  4.8 6.7 %copy-start.1 = (bf16[4,4,2,128,128]{4,3,2,1,0:T(8,128)(2,1)S(1)}, bf16[4,4,2,128,128]{4,3,2,1,0:T(8,128)(2,1)}, u32[]{:S(2)}) copy-start(bf16[4,4,2,128,128]{4,3,2,1,0:T(8,128)(2,1)} %refs_6_.1) | copy-start | bytes 3145732
  4.8 11.2 %collective-permute-start.4 = (bf16[3,2,2,128,128]{4,3,2,1,0:T(8,128)(2,1)S(1)}, bf16[3,2,2,128,128]{4,3,2,1,0:T(8,128)(2,1)S(1)}, u32[]{:S(2)}, u32[]{:S(2)}) collective-permute-start(bf16[3,2,2,128,128]{4,3,2,1,0:T(8,128)(2,1)S(1)} %shard_map.107), channel_id=1, source_target_pairs={{0,2},{2,0},{1,3},{3,1},{4,6},{6,4},{5,7},{7,5},{8,10},{10,8},{9,1... | collective-permute-start | bytes 1179656 | tf_op jit(solution)/shard_map/ppermute | solution.py:32
  6.6 4.9 %copy-start.5 = (f32[512]{0:T(512)S(1)}, f32[512]{0:T(512)}, u32[]{:S(2)}) copy-start(f32[512]{0:T(512)} %param.16) | copy-start | bytes 6148
  6.6 9.5 %collective-permute-start.1 = (bf16[2,8,24,128]{3,2,1,0:T(8,128)(2,1)S(1)}, bf16[2,8,24,128]{3,2,1,0:T(8,128)(2,1)S(1)}, u32[]{:S(2)}, u32[]{:S(2)}) collective-permute-start(bf16[2,8,24,128]{3,2,1,0:T(8,128)(2,1)S(1)} %shard_map.105.held_ref.refs_12_.refs_8_), channel_id=1, source_target_pairs={{0,8},{4,12},{8,0},{12,4},{1,9},{5,13},{9,1},{13,5},{2,10},{6,14},... | collective-permute-start | bytes 294920 | tf_op jit(solution)/shard_map/ppermute | solution.py:427
  9.9 7.0 %collective-permute-start.2 = (bf16[2,8,24,128]{3,2,1,0:T(8,128)(2,1)S(1)}, bf16[2,8,24,128]{3,2,1,0:T(8,128)(2,1)S(1)}, u32[]{:S(2)}, u32[]{:S(2)}) collective-permute-start(bf16[2,8,24,128]{3,2,1,0:T(8,128)(2,1)S(1)} %shard_map.105.held_ref.refs_12_.refs_8_), channel_id=1, source_target_pairs={{0,12},{4,8},{8,4},{12,0},{1,13},{5,9},{9,5},{13,1},{2,14},{6,10},... | collective-permute-start | bytes 294920 | tf_op jit(solution)/shard_map/ppermute | solution.py:427
  11.3 5.9 %collective-permute-start.3 = (bf16[2,8,24,128]{3,2,1,0:T(8,128)(2,1)S(1)}, bf16[2,8,24,128]{3,2,1,0:T(8,128)(2,1)S(1)}, u32[]{:S(2)}, u32[]{:S(2)}) collective-permute-start(bf16[2,8,24,128]{3,2,1,0:T(8,128)(2,1)S(1)} %shard_map.105.held_ref.refs_12_.refs_8_), channel_id=1, source_target_pairs={{0,4},{4,0},{8,12},{12,8},{1,5},{5,1},{9,13},{13,9},{2,6},{6,2},{1... | collective-permute-start | bytes 294920 | tf_op jit(solution)/shard_map/ppermute | solution.py:427
  11.5 0.7 %copy-start.4 = (s32[4,4,2]{1,2,0:T(2,128)S(1)}, s32[4,4,2]{1,2,0:T(2,128)}, u32[]{:S(2)}) copy-start(s32[4,4,2]{1,2,0:T(2,128)} %param.12) | copy-start | bytes 388
  11.5 0.7 %copy-start.3 = (s32[4,4,2]{1,2,0:T(2,128)S(1)}, s32[4,4,2]{1,2,0:T(2,128)}, u32[]{:S(2)}) copy-start(s32[4,4,2]{1,2,0:T(2,128)} %param.10) | copy-start | bytes 388
  11.5 0.7 %copy-start.6 = (f32[12]{0:T(128)S(1)}, f32[12]{0:T(128)}, u32[]{:S(2)}) copy-start(f32[12]{0:T(128)} %param.15) | copy-start | bytes 148
  12.9 4.3 %collective-permute-start.6 = (bf16[9,24,128]{2,1,0:T(8,128)(2,1)S(1)}, bf16[9,24,128]{2,1,0:T(8,128)(2,1)S(1)}, u32[]{:S(2)}, u32[]{:S(2)}) collective-permute-start(bf16[9,24,128]{2,1,0:T(8,128)(2,1)S(1)} %get-tuple-element.28), channel_id=1, source_target_pairs={{0,2},{2,0},{1,3},{3,1},{4,6},{6,4},{5,7},{7,5},{8,10},{10,8},{9,1... | collective-permute-start | bytes 165896 | tf_op jit(solution)/shard_map/ppermute | solution.py:32
  16.0 1.8 %collective-permute-start.5 = (bf16[3,2,2,128,128]{4,3,2,1,0:T(8,128)(2,1)S(1)}, bf16[3,2,2,128,128]{4,3,2,1,0:T(8,128)(2,1)S(1)}, u32[]{:S(2)}, u32[]{:S(2)}) collective-permute-start(bf16[3,2,2,128,128]{4,3,2,1,0:T(8,128)(2,1)S(1)} %collective-permute-done.4.refs_3_), channel_id=1, source_target_pairs={{0,1},{1,0},{2,3},{3,2},{4,5},{5,4},{6,7},{7,6},{8,9},{9,8},{10,11... | collective-permute-start | bytes 1179656 | tf_op jit(solution)/shard_map/ppermute | solution.py:32

commit v10 on v8

--- a/solution.py
+++ b/solution.py
@@ -330,14 +330,13 @@
     rows = []
     for position in range(half):
         row = start + position
-        total = early_ref[row].astype(jnp.float32)
+        blocks, slabs = [], []
         for at, piece_ref in enumerate(piece_refs):
-            total += pair_dot(
-                piece_ref.at[0],
-                [numbers_ref[row * slots + slot, at + 1] for slot in range(slots)],
-                [slab_ref[at, position, slot] for slot in range(slots)],
-            )
-        rows.append(total.astype(jnp.bfloat16))
+            for slot in range(slots):
+                blocks.append(piece_ref[0, numbers_ref[row * slots + slot, at + 1]])
+                slabs.append(slab_ref[at, position, slot])
+        total = lax.dot_general(lanes(blocks), lanes(slabs), NT, preferred_element_type=jnp.float32)
+        rows.append((early_ref[row].astype(jnp.float32) + total).astype(jnp.bfloat16))
     matrix = matrix_ref[pl.ds(start, half)].reshape(half * matrix_ref.shape[1], -1)
     return lax.dot_general(lanes(rows), matrix, NN, preferred_element_type=jnp.float32)
 

time: 19.1 us -> 19.1 us (level)
  no operation moved by 1% of the time
where the time goes in v10:
time: 19.1 us; the launch traced here: 18.9 us
  starting transfers between devices  10.6 us (55%)
  Pallas kernels  3.24 us (17%)
  waiting for transfers between devices  2.82 us (15%)
  local copies, waits for them, and re-layouts  1.51 us (8%)
  between operations  0.75 us (4%)
    ppermute x4, starting transfers between devices, swapped(): lax.ppermute(array, axis, [(i, i ^ distance) for i in range(lax.axis_size...  5.74 us
    ppermute x3, starting transfers between devices, paired_step(): lax.ppermute(held, 'blk', list(enumerate(targets)))  4.84 us
    ppermute x4, waiting for transfers between devices, swapped(): lax.ppermute(array, axis, [(i, i ^ distance) for i in range(lax.axis_size...  2.34 us
    pallas_call x1, Pallas kernels, paired_step(): kernel_call(functools.partial(last_kernel, regions), (result, result), 'v...  1.07 us
    reshape x2, local copies, waits for them, and re-layouts, blocked(): return array.reshape(rows, row_blocks, block_size).transpose(1, 0, 2)  0.79 us
    unnamed x16, local copies, waits for them, and re-layouts  0.71 us
    pallas_call x1, Pallas kernels, paired_step(): kernel_call(functools.partial(first_kernel, regions), (jax.ShapeDtypeStru...  0.66 us
    pallas_call x2, Pallas kernels, paired_step(): kernel_call(functools.partial(next_kernel, regions, move), (totals, total...  0.58 us
  transfers between devices with their start and end apart: 7, of which 4 were waited for; matrix products, arithmetic and copies ran while one was open for 0% of the time, Pallas kernels for 11%

profile of v10, /device:TPU:0, one launch (start us, length us, event | category | flops | bytes accessed | tf_op | source)
XLA Modules:
  0.0 18.9 jit_solution(1808605151538454690)
XLA Ops:
  0.6 0.8 %reshape.10 = bf16[24,4,128]{2,1,0:T(4,128)(2,1)S(1)} reshape(bf16[12,2,512]{2,1,0:T(2,128)(2,1)} %param.13) | data formatting | bytes 49152 | tf_op jit(solution)/shard_map/reshape | solution.py:400
  1.5 0.0 copy-start.2
  1.5 0.0 copy-start
  1.5 3.0 %collective-permute-start = (bf16[2,4,24,128]{3,2,1,0:T(8,128)(2,1)S(1)}, bf16[2,4,24,128]{3,2,1,0:T(8,128)(2,1)S(1)}, u32[]{:S(2)}, u32[]{:S(2)}) collective-permute-start(bf16[2,4,24,128]{3,2,1,0:T(8,128)(2,1)S(1)} %shard_map.104.own_ref.message_ref), channel_id=1, source_target_pairs={{0,2},{2,0},{1,3},{3,1},{4,6},{6,4},{5,7},{7,5},{8,10},{10,8},{9,1... | collective-permute-start | bytes 147464 | tf_op jit(solution)/shard_map/ppermute | solution.py:32
  4.5 0.3 %shard_map.106 = (bf16[3,128,512]{2,1,0:T(8,128)(2,1)S(1)}, f32[3,24,128]{2,1,0:T(8,128)S(1)}) custom-call(bf16[2,4,24,128]{3,2,1,0:T(8,128)(2,1)S(1)} %shard_map.104.own_ref.message_ref, s32[2,512]{1,0:T(2,128)S(1)} %copy-done.2), custom_call_target="tpu_custom_call" | custom-call | flops 1000000 | bytes 4000000 | tf_op jit(solution)/shard_map/pallas_call | solution.py:412
  4.8 0.0 copy-done
  4.9 0.0 copy-start.1
  4.9 0.9 %collective-permute-start.4 = (bf16[3,2,2,128,128]{4,3,2,1,0:T(8,128)(2,1)S(1)}, bf16[3,2,2,128,128]{4,3,2,1,0:T(8,128)(2,1)S(1)}, u32[]{:S(2)}, u32[]{:S(2)}) collective-permute-start(bf16[3,2,2,128,128]{4,3,2,1,0:T(8,128)(2,1)S(1)} %shard_map.107), channel_id=1, source_target_pairs={{0,2},{2,0},{1,3},{3,1},{4,6},{6,4},{5,7},{7,5},{8,10},{10,8},{9,1... | collective-permute-start | bytes 1179656 | tf_op jit(solution)/shard_map/ppermute | solution.py:32
  5.8 0.8 %collective-permute-done.other_ref = bf16[2,4,24,128]{3,2,1,0:T(8,128)(2,1)S(1)} collective-permute-done((bf16[2,4,24,128]{3,2,1,0:T(8,128)(2,1)S(1)}, bf16[2,4,24,128]{3,2,1,0:T(8,128)(2,1)S(1)}, u32[]{:S(2)}, u32[]{:S(2)}) %collective-permute-start) | collective-permute-done | bytes 49184 | tf_op jit(solution)/shard_map/ppermute | solution.py:32
  6.6 3.3 %collective-permute-start.1 = (bf16[2,8,24,128]{3,2,1,0:T(8,128)(2,1)S(1)}, bf16[2,8,24,128]{3,2,1,0:T(8,128)(2,1)S(1)}, u32[]{:S(2)}, u32[]{:S(2)}) collective-permute-start(bf16[2,8,24,128]{3,2,1,0:T(8,128)(2,1)S(1)} %shard_map.105.held_ref.refs_12_.refs_8_), channel_id=1, source_target_pairs={{0,8},{4,12},{8,0},{12,4},{1,9},{5,13},{9,1},{13,5},{2,10},{6,14},... | collective-permute-start | bytes 294920 | tf_op jit(solution)/shard_map/ppermute | solution.py:426
  9.8 1.3 %collective-permute-start.2 = (bf16[2,8,24,128]{3,2,1,0:T(8,128)(2,1)S(1)}, bf16[2,8,24,128]{3,2,1,0:T(8,128)(2,1)S(1)}, u32[]{:S(2)}, u32[]{:S(2)}) collective-permute-start(bf16[2,8,24,128]{3,2,1,0:T(8,128)(2,1)S(1)} %shard_map.105.held_ref.refs_12_.refs_8_), channel_id=1, source_target_pairs={{0,12},{4,8},{8,4},{12,0},{1,13},{5,9},{9,5},{13,1},{2,14},{6,10},... | collective-permute-start | bytes 294920 | tf_op jit(solution)/shard_map/ppermute | solution.py:426
  11.2 0.2 %collective-permute-start.3 = (bf16[2,8,24,128]{3,2,1,0:T(8,128)(2,1)S(1)}, bf16[2,8,24,128]{3,2,1,0:T(8,128)(2,1)S(1)}, u32[]{:S(2)}, u32[]{:S(2)}) collective-permute-start(bf16[2,8,24,128]{3,2,1,0:T(8,128)(2,1)S(1)} %shard_map.105.held_ref.refs_12_.refs_8_), channel_id=1, source_target_pairs={{0,4},{4,0},{8,12},{12,8},{1,5},{5,1},{9,13},{13,9},{2,6},{6,2},{1... | collective-permute-start | bytes 294920 | tf_op jit(solution)/shard_map/ppermute | solution.py:426
  11.4 0.7 %copy-done.4 = s32[4,4,2]{1,2,0:T(2,128)S(1)} copy-done((s32[4,4,2]{1,2,0:T(2,128)S(1)}, s32[4,4,2]{1,2,0:T(2,128)}, u32[]{:S(2)}) %copy-start.4) | copy-done | bytes 152
  12.1 0.0 copy-done.3
  12.1 0.7 %shard_map.108 = (f32[5,24,128]{2,1,0:T(8,128)S(1)}, s32[2,4,4,2,128]{4,3,2,1,0:T(2,128)S(1)}, f32[4,24,128]{2,1,0:T(8,128)S(1)}, f32[4,24,128]{2,1,0:T(8,128)S(...) custom-call(bf16[2,8,24,128]{3,2,1,0:T(8,128)(2,1)S(1)} %shard_map.1, ...), custom_call_target="tpu_custom_call" | custom-call | flops 1000000 | bytes 4000000 | tf_op jit(solution)/shard_map/pallas_call | solution.py:429
  12.8 1.9 %collective-permute-start.6 = (bf16[9,24,128]{2,1,0:T(8,128)(2,1)S(1)}, bf16[9,24,128]{2,1,0:T(8,128)(2,1)S(1)}, u32[]{:S(2)}, u32[]{:S(2)}) collective-permute-start(bf16[9,24,128]{2,1,0:T(8,128)(2,1)S(1)} %get-tuple-element.28), channel_id=1, source_target_pairs={{0,2},{2,0},{1,3},{3,1},{4,6},{6,4},{5,7},{7,5},{8,10},{10,8},{9,1... | collective-permute-start | bytes 165896 | tf_op jit(solution)/shard_map/ppermute | solution.py:32
  14.7 1.5 %collective-permute-done.4.refs_3_ = bf16[3,2,2,128,128]{4,3,2,1,0:T(8,128)(2,1)S(1)} collective-permute-done((bf16[3,2,2,128,128]{4,3,2,1,0:T(8,128)(2,1)S(1)}, bf16[3,2,2,128,128]{4,3,2,1,0:T(8,128)(2,1)S(1)}, u32[]{:S(2)}, u32[]{:S(2)}) %collective-permute-start.4) | collective-permute-done | bytes 393248 | tf_op jit(solution)/shard_map/ppermute | solution.py:32
  16.1 0.3 %shard_map.109 = (f32[4,24,128]{2,1,0:T(8,128)S(1)}, f32[4,24,128]{2,1,0:T(8,128)S(1)}) custom-call(s32[2,4,4,2,128]{4,3,2,1,0:T(2,128)S(1)} %get-tuple-element.20.table_ref.refs_4_, bf16[2,8,24,128]{3,2,1,0:T(8,128)(2,1)S(1)} %collective-permute-done.1.held_ref.refs_0_, bf16[4,4,2,128,128]{4,3,2,1,0:T(8,128)(2,1)S(1)} %copy-done, ...), custom_call_target="tpu_custom_call" | custom-call | flops 3000000000 | bytes 4000000 | tf_op jit(solution)/shard_map/pallas_call | solution.py:450
  16.4 0.5 %collective-permute-done.2.held_ref.refs_1_ = bf16[2,8,24,128]{3,2,1,0:T(8,128)(2,1)S(1)} collective-permute-done((bf16[2,8,24,128]{3,2,1,0:T(8,128)(2,1)S(1)}, bf16[2,8,24,128]{3,2,1,0:T(8,128)(2,1)S(1)}, u32[]{:S(2)}, u32[]{:S(2)}) %collective-permute-start.2) | collective-permute-done | bytes 98336 | tf_op jit(solution)/shard_map/ppermute | solution.py:426
  16.9 0.3 %shard_map.110 = (f32[4,24,128]{2,1,0:T(8,128)S(1)}, f32[4,24,128]{2,1,0:T(8,128)S(1)}) custom-call(s32[2,4,4,2,128]{4,3,2,1,0:T(2,128)S(1)} %get-tuple-element.20.table_ref.refs_4_, bf16[2,8,24,128]{3,2,1,0:T(8,128)(2,1)S(1)} %collective-permute-done.2.held_ref.refs_1_, bf16[4,4,2,128,128]{4,3,2,1,0:T(8,128)(2,1)S(1)} %copy-done, ...), custom_call_target="tpu_custom_call" | custom-call | flops 3000000000 | bytes 4000000 | tf_op jit(solution)/shard_map/pallas_call | solution.py:450
  17.2 0.0 collective-permute-done.3.refs_2_
  17.2 0.6 %shard_map.111 = (f32[24,512]{1,0:T(8,128)S(1)}, s32[24,128]{1,0:T(8,128)S(1)}) custom-call(bf16[2,8,24,128]{3,2,1,0:T(8,128)(2,1)S(1)} %collective-permute-done.1.held_ref.refs_0_, bf16[2,8,24,128]{3,2,1,0:T(8,128)(2,1)S(1)} %collective-permute-done.2.held_ref.refs_1_, bf16[2,8,24,128]{3,2,1,0:T(8,128)(2,1)S(1)} %collective-permute-done.3.refs_2_, ...), custom_call_target="tpu_custom_call" | custom-call | flops 1000000000 | bytes 4000000 | tf_op jit(solution)/shard_map/pallas_call | solution.py:455
  17.8 0.1 collective-permute-done.5.refs_3_
  17.8 1.1 %shard_map.112 = (f32[12,2,512]{2,1,0:T(2,128)}, f32[12,2,512]{2,1,0:T(2,128)}) custom-call(bf16[2,8,24,128]{3,2,1,0:T(8,128)(2,1)S(1)} %collective-permute-done.1.held_ref.refs_0_, bf16[2,8,24,128]{3,2,1,0:T(8,128)(2,1)S(1)} %collective-permute-done.2.held_ref.refs_1_, bf16[2,8,24,128]{3,2,1,0:T(8,128)(2,1)S(1)} %collective-permute-done.3.refs_2_, ...), custom_call_target="tpu_custom_call" | custom-call | flops 8000000000 | bytes 4000000 | tf_op jit(solution)/shard_map/pallas_call | solution.py:462
  (18 shorter events, 0.1 us)
Async XLA Ops:
  0.6 0.8 %copy-start.7 = (bf16[12,2,512]{2,1,0:T(2,128)(2,1)S(1)}, bf16[12,2,512]{2,1,0:T(2,128)(2,1)}, u32[]{:S(2)}) copy-start(bf16[12,2,512]{2,1,0:T(2,128)(2,1)} %param.14) | copy-start | bytes 73732
  1.5 3.0 %copy-start.2 = (s32[2,512]{1,0:T(2,128)S(1)}, s32[2,512]{1,0:T(2,128)}, u32[]{:S(2)}) copy-start(s32[2,512]{1,0:T(2,128)} %ends_ref.3) | copy-start | bytes 12292
  1.5 3.3 %copy-start = (bf16[4,4,2,128,128]{4,3,2,1,0:T(8,128)(2,1)S(1)}, bf16[4,4,2,128,128]{4,3,2,1,0:T(8,128)(2,1)}, u32[]{:S(2)}) copy-start(bf16[4,4,2,128,128]{4,3,2,1,0:T(8,128)(2,1)} %refs_5_.1) | copy-start | bytes 3145732
  1.5 5.1 %collective-permute-start = (bf16[2,4,24,128]{3,2,1,0:T(8,128)(2,1)S(1)}, bf16[2,4,24,128]{3,2,1,0:T(8,128)(2,1)S(1)}, u32[]{:S(2)}, u32[]{:S(2)}) collective-permute-start(bf16[2,4,24,128]{3,2,1,0:T(8,128)(2,1)S(1)} %shard_map.104.own_ref.message_ref), channel_id=1, source_target_pairs={{0,2},{2,0},{1,3},{3,1},{4,6},{6,4},{5,7},{7,5},{8,10},{10,8},{9,1... | collective-permute-start | bytes 147464 | tf_op jit(solution)/shard_map/ppermute | solution.py:32
  4.9 6.6 %copy-start.1 = (bf16[4,4,2,128,128]{4,3,2,1,0:T(8,128)(2,1)S(1)}, bf16[4,4,2,128,128]{4,3,2,1,0:T(8,128)(2,1)}, u32[]{:S(2)}) copy-start(bf16[4,4,2,128,128]{4,3,2,1,0:T(8,128)(2,1)} %refs_6_.1) | copy-start | bytes 3145732
  4.9 11.2 %collective-permute-start.4 = (bf16[3,2,2,128,128]{4,3,2,1,0:T(8,128)(2,1)S(1)}, bf16[3,2,2,128,128]{4,3,2,1,0:T(8,128)(2,1)S(1)}, u32[]{:S(2)}, u32[]{:S(2)}) collective-permute-start(bf16[3,2,2,128,128]{4,3,2,1,0:T(8,128)(2,1)S(1)} %shard_map.107), channel_id=1, source_target_pairs={{0,2},{2,0},{1,3},{3,1},{4,6},{6,4},{5,7},{7,5},{8,10},{10,8},{9,1... | collective-permute-start | bytes 1179656 | tf_op jit(solution)/shard_map/ppermute | solution.py:32
  6.6 4.9 %copy-start.5 = (f32[512]{0:T(512)S(1)}, f32[512]{0:T(512)}, u32[]{:S(2)}) copy-start(f32[512]{0:T(512)} %param.16) | copy-start | bytes 6148
  6.6 9.5 %collective-permute-start.1 = (bf16[2,8,24,128]{3,2,1,0:T(8,128)(2,1)S(1)}, bf16[2,8,24,128]{3,2,1,0:T(8,128)(2,1)S(1)}, u32[]{:S(2)}, u32[]{:S(2)}) collective-permute-start(bf16[2,8,24,128]{3,2,1,0:T(8,128)(2,1)S(1)} %shard_map.105.held_ref.refs_12_.refs_8_), channel_id=1, source_target_pairs={{0,8},{4,12},{8,0},{12,4},{1,9},{5,13},{9,1},{13,5},{2,10},{6,14},... | collective-permute-start | bytes 294920 | tf_op jit(solution)/shard_map/ppermute | solution.py:426
  9.8 7.0 %collective-permute-start.2 = (bf16[2,8,24,128]{3,2,1,0:T(8,128)(2,1)S(1)}, bf16[2,8,24,128]{3,2,1,0:T(8,128)(2,1)S(1)}, u32[]{:S(2)}, u32[]{:S(2)}) collective-permute-start(bf16[2,8,24,128]{3,2,1,0:T(8,128)(2,1)S(1)} %shard_map.105.held_ref.refs_12_.refs_8_), channel_id=1, source_target_pairs={{0,12},{4,8},{8,4},{12,0},{1,13},{5,9},{9,5},{13,1},{2,14},{6,10},... | collective-permute-start | bytes 294920 | tf_op jit(solution)/shard_map/ppermute | solution.py:426
  11.2 6.0 %collective-permute-start.3 = (bf16[2,8,24,128]{3,2,1,0:T(8,128)(2,1)S(1)}, bf16[2,8,24,128]{3,2,1,0:T(8,128)(2,1)S(1)}, u32[]{:S(2)}, u32[]{:S(2)}) collective-permute-start(bf16[2,8,24,128]{3,2,1,0:T(8,128)(2,1)S(1)} %shard_map.105.held_ref.refs_12_.refs_8_), channel_id=1, source_target_pairs={{0,4},{4,0},{8,12},{12,8},{1,5},{5,1},{9,13},{13,9},{2,6},{6,2},{1... | collective-permute-start | bytes 294920 | tf_op jit(solution)/shard_map/ppermute | solution.py:426
  11.4 0.7 %copy-start.4 = (s32[4,4,2]{1,2,0:T(2,128)S(1)}, s32[4,4,2]{1,2,0:T(2,128)}, u32[]{:S(2)}) copy-start(s32[4,4,2]{1,2,0:T(2,128)} %param.12) | copy-start | bytes 388
  11.4 0.7 %copy-start.3 = (s32[4,4,2]{1,2,0:T(2,128)S(1)}, s32[4,4,2]{1,2,0:T(2,128)}, u32[]{:S(2)}) copy-start(s32[4,4,2]{1,2,0:T(2,128)} %param.10) | copy-start | bytes 388
  11.4 0.7 %copy-start.6 = (f32[12]{0:T(128)S(1)}, f32[12]{0:T(128)}, u32[]{:S(2)}) copy-start(f32[12]{0:T(128)} %param.15) | copy-start | bytes 148
  12.8 4.4 %collective-permute-start.6 = (bf16[9,24,128]{2,1,0:T(8,128)(2,1)S(1)}, bf16[9,24,128]{2,1,0:T(8,128)(2,1)S(1)}, u32[]{:S(2)}, u32[]{:S(2)}) collective-permute-start(bf16[9,24,128]{2,1,0:T(8,128)(2,1)S(1)} %get-tuple-element.28), channel_id=1, source_target_pairs={{0,2},{2,0},{1,3},{3,1},{4,6},{6,4},{5,7},{7,5},{8,10},{10,8},{9,1... | collective-permute-start | bytes 165896 | tf_op jit(solution)/shard_map/ppermute | solution.py:32
  16.1 1.7 %collective-permute-start.5 = (bf16[3,2,2,128,128]{4,3,2,1,0:T(8,128)(2,1)S(1)}, bf16[3,2,2,128,128]{4,3,2,1,0:T(8,128)(2,1)S(1)}, u32[]{:S(2)}, u32[]{:S(2)}) collective-permute-start(bf16[3,2,2,128,128]{4,3,2,1,0:T(8,128)(2,1)S(1)} %collective-permute-done.4.refs_3_), channel_id=1, source_target_pairs={{0,1},{1,0},{2,3},{3,2},{4,5},{5,4},{6,7},{7,6},{8,9},{9,8},{10,11... | collective-permute-start | bytes 1179656 | tf_op jit(solution)/shard_map/ppermute | solution.py:32
